TPU v7x, 32 devices: a whole 2x2x4 slice. The times are simulated.
32 devices in a mesh: groups: 2 (over x), shard: 16 (over z, y, core).
Axes of the slice: x: 2, y: 2, z: 4, core: 2. Of those that a mesh axis runs over, the one named last changes fastest.
Arguments:
- embeddings: bfloat16 [1280, 1024], P(('groups', 'shard')), parts along dimension 0, may hold values from -250 to 250
- probes: int32 [1280, 8], P(('groups', 'shard')), parts along dimension 0, may hold values from 0 to 15, all different within a row; in each aligned block of 40 rows (0 to 39, 40 to 79, ...) at most 40 rows name the same one
- assigned: int32 [1280], P(('groups', 'shard')), parts along dimension 0, may hold values from 0 to 1023
- prior_counts: int32 [32768], P(('groups', 'shard')), parts along dimension 0, may hold values from 1 to 16
- centroids: bfloat16 [32768, 1024], P(('groups', 'shard')), parts along dimension 0, may hold values from -30 to 30
- candidates: int32 [32768, 1], P(('groups', 'shard')), parts along dimension 0, may hold values from 0 to 47; in each aligned block of 1024 rows (0 to 1023, 1024 to 2047, ...) at most 32 rows name the same one
- centroids2: bfloat16 [12288, 1024], P(('groups', 'shard')), parts along dimension 0, may hold values from -30 to 30
Outputs:
- density: float32 [1280], P(('groups', 'shard')), parts along dimension 0
- new_centroids: bfloat16 [32768, 1024], P(('groups', 'shard')), parts along dimension 0
- new_counts: int32 [32768], P(('groups', 'shard')), parts along dimension 0
- level_two: float32 [32768], P(('groups', 'shard')), parts along dimension 0
There are 2 independent parts, one for each index of `groups`. A program takes and returns all parts, laid end to end along the dimension named above; each array names one. Nothing has to cross between parts.
Inputs may be any that keep to these rules, and one draw needn't show every extreme that they name: `probes`: each row names 8 different blocks. Among the 40 embeddings of one device no block is named more than 40 times, and in every draw some block is named exactly 40 times by one device's embeddings. `candidates`: among the 1024 level-1 centroids of one device no level-2 block is named more than 32 times, and in every draw some is named exactly 32 times.
All inputs are finite; a program needn't handle non-finite values.
Results may differ from a plain program's by a relative error of at most 0.0015.
Values may be sent and summed in bfloat16 or wider, within the bound.
No kernel may reach another device: no remote copies, remote signals or barrier semaphores. Data moves between devices by JAX's collectives and lax.ppermute only.
A program may use at most 64 MiB of HBM per device.

v0:
```python
import functools
import math

import jax
import jax.numpy as jnp
from jax import lax
from jax.experimental import pallas as pl
from jax.experimental.pallas import tpu as pltpu
from jax.sharding import PartitionSpec as P

BLOCK = 1024
BLOCKS_DEV = 1
BLOCK2 = 128
BLOCKS2_DEV = 3


def unit_rows(values):
    wide = values.astype(jnp.float32)
    power = jnp.mean(wide * wide, axis=-1, keepdims=True) + 1e-06
    return (wide * lax.rsqrt(power)).astype(jnp.bfloat16)


def kernel_sums(rows, unit):
    scores = lax.dot_general(
        rows, unit, (((1,), (1,)), ((), ())), preferred_element_type=jnp.float32
    )
    return jnp.sum(jnp.exp((scores / rows.shape[1] - 1.0) / 0.1), axis=1)


def block_update(rows, slots, width):
    matches = slots[:, None] == jnp.arange(width, dtype=jnp.int32)[None, :]
    sums = lax.dot_general(
        matches.astype(jnp.bfloat16),
        rows,
        (((0,), (0,)), ((), ())),
        preferred_element_type=jnp.float32,
    )
    counts = jnp.sum(matches.astype(jnp.int32), axis=0)
    return (sums, counts)


def slot_ranks(targets, buckets):
    matches = (targets[:, None] == jnp.arange(buckets, dtype=jnp.int32)[None, :]).astype(jnp.int32)
    return jnp.sum(jnp.cumsum(matches, axis=0) * matches, axis=1) - 1


def general_body(embeddings, probes, assigned, prior_counts, centroids, candidates, centroids2):
    devices = lax.axis_size("shard")
    emb_rows, width = embeddings.shape
    probe_count = probes.shape[1]
    capacity = max(2, 2 * emb_rows * probe_count // (BLOCKS_DEV * devices))
    scaled = unit_rows(embeddings)
    units_old = unit_rows(centroids).reshape(BLOCKS_DEV, BLOCK, width)
    total = emb_rows * probe_count
    buckets = BLOCKS_DEV * devices
    flat = probes.reshape(-1)
    place = flat * capacity + slot_ranks(flat, buckets)
    leading = jnp.arange(total, dtype=jnp.int32) % probe_count == 0
    repeated = jnp.repeat(scaled, probe_count, axis=0)
    slot_values = jnp.where(leading, jnp.repeat(assigned, probe_count), -1)
    send_rows = jnp.zeros((buckets * capacity, width), jnp.bfloat16).at[place].set(repeated)
    send_slots = jnp.full((buckets * capacity,), -1, jnp.int32).at[place].set(slot_values)
    got_rows, got_slots = (
        lax.all_to_all(
            send_rows.reshape(devices, BLOCKS_DEV * capacity, width),
            "shard",
            split_axis=0,
            concat_axis=0,
            tiled=True,
        ),
        lax.all_to_all(
            send_slots.reshape(devices, BLOCKS_DEV * capacity),
            "shard",
            split_axis=0,
            concat_axis=0,
            tiled=True,
        ),
    )
    got_rows = got_rows.reshape(devices, BLOCKS_DEV, capacity, width)
    got_slots = got_slots.reshape(devices, BLOCKS_DEV, capacity)
    local = 0
    picked = got_rows[:, local].reshape(devices * capacity, width)
    slots = got_slots[:, local].reshape(-1)
    weights = [kernel_sums(picked, units_old[local]).reshape(devices, capacity)]
    more_sums, more_counts = block_update(picked, slots, BLOCK)
    sum_list = [more_sums]
    count_list = [more_counts]
    sums = jnp.stack(sum_list)
    counts = jnp.stack(count_list)
    returned = lax.all_to_all(
        jnp.stack(weights, axis=1).reshape(devices, BLOCKS_DEV * capacity),
        "shard",
        split_axis=0,
        concat_axis=0,
        tiled=True,
    )
    totals = jnp.sum(returned.reshape(-1)[place].reshape(emb_rows, probe_count), axis=1)
    density = jnp.log(totals / (probe_count * BLOCK))
    prior = prior_counts.reshape(BLOCKS_DEV, BLOCK)
    fresh = prior + counts
    updated = (
        prior.astype(jnp.float32)[:, :, None]
        * centroids.reshape(BLOCKS_DEV, BLOCK, width).astype(jnp.float32)
        + sums
    ) / fresh.astype(jnp.float32)[:, :, None]
    new_centroids = updated.astype(jnp.bfloat16).reshape(BLOCKS_DEV * BLOCK, width)
    units_new = unit_rows(updated).reshape(BLOCKS_DEV * BLOCK, width)
    rows_two = units_new.shape[0]
    second_capacity = max(2, 3 * rows_two // (2 * BLOCKS2_DEV * devices))
    buckets_two = BLOCKS2_DEV * devices
    chosen = candidates[:, 0]
    place_two = chosen * second_capacity + slot_ranks(chosen, buckets_two)
    send_two = (
        jnp.zeros((buckets_two * second_capacity, width), jnp.bfloat16).at[place_two].set(units_new)
    )
    send_two = send_two.reshape(devices, BLOCKS2_DEV, second_capacity, width)
    units_two = unit_rows(centroids2).reshape(BLOCKS2_DEV, BLOCK2, width)
    arrived = lax.all_to_all(send_two, "shard", split_axis=0, concat_axis=0, tiled=True)
    items = arrived.shape[2]
    weights_two = [
        kernel_sums(arrived[:, local].reshape(-1, width), units_two[local]).reshape(
            arrived.shape[0], items
        )
        for local in range(BLOCKS2_DEV)
    ]
    returned_two = lax.all_to_all(
        jnp.stack(weights_two, axis=1), "shard", split_axis=0, concat_axis=0, tiled=True
    )
    level_two = jnp.log(returned_two.reshape(-1)[place_two] / BLOCK2)
    return (density, new_centroids, fresh.reshape(-1), level_two)


NT = (((1,), (1,)), ((), ()))
PARAMS = pltpu.CompilerParams(vmem_limit_bytes=48 * 1024 * 1024)
META = 16
SHARE = 1
LATE = 5
STEP = 12
HBM = pl.BlockSpec(memory_space=pltpu.HBM)
ANY = pl.BlockSpec(memory_space=pl.ANY)
VMEM = pl.BlockSpec(memory_space=pltpu.VMEM)


def position():
    me = lax.axis_index("shard")
    return me, me // 4, (me // 2) % 2, me % 2


def unit_wide(wide):
    power = jnp.mean(wide * wide, axis=-1, keepdims=True) + 1e-06
    return (wide * lax.rsqrt(power)).astype(jnp.bfloat16)


def weights(scores, width):
    return jnp.exp(scores * (10.0 / width) - 10.0)


def one_hot(hits):
    return jnp.where(hits, 1.0, 0.0).astype(jnp.bfloat16)


def column(row):
    return jnp.transpose(jnp.broadcast_to(row, (8, row.shape[1])))[:, 0:1]


def fetch(pairs, sems):
    copies = [pltpu.make_async_copy(src, dst, sems.at[i]) for i, (src, dst) in enumerate(pairs)]
    for copy in copies:
        copy.start()
    return copies


def pick_rows(slot, first, count):
    return one_hot(slot == lax.broadcasted_iota(jnp.int32, (count, slot.shape[1]), 0) + first)


def pack(slot, prior, cent, first, out):
    count = out.shape[0] - META
    rows = slot.shape[1]
    ident = lax.broadcasted_iota(jnp.int32, (1, rows), 1) + 1
    line = lax.broadcasted_iota(jnp.int32, (META, rows), 0)
    facts = jnp.where(line == 0, ident >> 5, jnp.where(line == 1, ident & 31, jnp.where(line == 2, prior, 0)))
    facts = facts.astype(jnp.float32).astype(jnp.bfloat16)
    pick = pick_rows(slot, first, count)
    out[0:count, :] = jnp.dot(pick, cent, preferred_element_type=jnp.float32).astype(jnp.bfloat16)
    out[count:, :] = jnp.zeros((META, out.shape[1]), jnp.bfloat16)
    out[count:, 0:count] = lax.dot_general(facts, pick, NT, preferred_element_type=jnp.float32).astype(jnp.bfloat16)


def pack_kernel(
    cap, per, cand_any, emb_any, probes_any, assigned_any, prior_any, cent_any, mine, rows2, rows3, info,
    cand_ref, emb_ref, probes_ref, assigned_ref, prior_ref, cent_ref, sems,
):
    copies = fetch(
        (
            (cand_any, cand_ref),
            (emb_any, emb_ref),
            (probes_any, probes_ref),
            (assigned_any, assigned_ref),
            (prior_any, prior_ref),
            (cent_any, cent_ref),
        ),
        sems,
    )
    me, z, y, core = position()
    rows = cand_ref.shape[1]
    buckets = 16 * per
    before = lax.broadcasted_iota(jnp.int32, (rows, rows), 0) <= lax.broadcasted_iota(jnp.int32, (rows, rows), 1)
    before = one_hot(before)
    copies[0].wait()
    cand = cand_ref[...]
    dev = sum((cand >= per * step).astype(jnp.int32) for step in range(1, 16))
    near = dev >> 2
    plane = jnp.where(z >= 2, 3 - near, near)
    rel = (((dev >> 1) & 1) ^ y) * 2 + ((dev & 1) ^ core)
    named = cand == lax.broadcasted_iota(jnp.int32, (buckets, rows), 0)
    counted = jnp.dot(one_hot(named), before, preferred_element_type=jnp.float32)
    rank = jnp.sum(jnp.where(named, counted, 0.0), axis=0, keepdims=True).astype(jnp.int32) - 1
    kind = plane * per + cand - dev * per
    slot = (rel * 4 * per + kind) * cap + rank
    info[0:1, :] = slot
    info[1:2, :] = rel * 4 + (kind >> 2)
    info[2:3, :] = (kind & 3) * cap + rank
    for copy in copies[1:5]:
        copy.wait()
    count, width = emb_ref.shape
    probe_count = probes_ref.shape[0]
    slots = assigned_ref[...]
    facts = jnp.concatenate([probes_ref[...], slots >> 5, slots & 31], axis=0).astype(jnp.float32)
    facts = jnp.concatenate([facts, jnp.zeros((128 - probe_count - 2, count), jnp.float32)], axis=0)
    same = lax.broadcasted_iota(jnp.int32, (count, count), 0) == lax.broadcasted_iota(jnp.int32, (count, count), 1)
    mine[:, 0:width] = emb_ref[...]
    mine[:, width:] = lax.dot_general(
        one_hot(same), facts.astype(jnp.bfloat16), NT, preferred_element_type=jnp.float32
    ).astype(jnp.bfloat16)
    copies[5].wait()
    pack(slot, prior_ref[...], cent_ref[...], 2 * 4 * per * cap, rows2)
    pack(slot, prior_ref[...], cent_ref[...], 3 * 4 * per * cap, rows3)


def pack_more_kernel(part, info, prior_ref, cent_ref, rows0, rows1, late2, late3):
    for first, out in ((0, rows0), (4 * part, rows1), (11 * part, late2), (15 * part, late3)):
        pack(info[0:1, :], prior_ref[...], cent_ref[...], first, out)


def order_kernel(*refs):
    pass


def prepare_kernel(cent_ref, own_any, near_any, unit_old, units, own, near, sems):
    copies = fetch(((own_any, own), (near_any, near)), sems)
    step = 256
    for start in range(0, cent_ref.shape[0], step):
        unit_old[start : start + step, :] = unit_wide(cent_ref[start : start + step, :].astype(jnp.float32))
    me, z, y, core = position()
    first = jnp.where((z == 0) | (z == 3), 0, 1)
    copies[0].wait()
    units[first] = unit_wide(own[...].astype(jnp.float32))
    copies[1].wait()
    units[1 - first] = unit_wide(near[...].astype(jnp.float32))


def share_kernel(mine_any, other_any, unit_old, scaled, facts, share_low, share_high, mine_ref, other_ref, sems):
    copies = fetch(((mine_any, mine_ref), (other_any, other_ref)), sems)
    me, z, y, core = position()
    half = mine_ref.shape[0]
    count = 2 * half
    rows, width = unit_old.shape
    copies[0].wait()
    scaled[0:half, :] = unit_wide(mine_ref[:, 0:width].astype(jnp.float32))
    copies[1].wait()
    scaled[half:count, :] = unit_wide(other_ref[:, 0:width].astype(jnp.float32))
    aux = jnp.concatenate([mine_ref[:, width:], other_ref[:, width:]], axis=0).astype(jnp.float32)
    aux = jnp.transpose(aux)[0:16, :].astype(jnp.int32)
    facts[...] = aux
    member = jnp.sum((aux[0:8, :] == me).astype(jnp.float32), axis=0, keepdims=True)
    step = 256
    total = jnp.zeros((1, count), jnp.float32)
    for start in range(0, rows, step):
        scores = lax.dot_general(
            unit_old[start : start + step, :], scaled[...], NT, preferred_element_type=jnp.float32
        )
        total = total + jnp.sum(weights(scores, width), axis=0, keepdims=True)
    piece = count // 16
    lane = lax.broadcasted_iota(jnp.int32, (16, count), 1)
    line = lax.broadcasted_iota(jnp.int32, (16, count), 0)
    apart = jnp.where((member > 0.0) & (lane >= line * piece) & (lane < (line + 1) * piece), total, 0.0)
    spot = lax.broadcasted_iota(jnp.int32, (count, 128), 0)
    block = sum((spot >= piece * step).astype(jnp.int32) for step in range(1, 16))
    together = jnp.where(spot - block * piece == lax.broadcasted_iota(jnp.int32, (count, 128), 1), 1.0, 0.0)
    share = jnp.dot(apart, together, precision=lax.Precision.HIGHEST, preferred_element_type=jnp.float32)
    share_low[...] = share[0:8, :]
    share_high[...] = share[8:16, :]


def update_kernel(after, scaled, facts, cent_ref, prior_ref, fresh_rows, fresh_counts):
    me, z, y, core = position()
    rows, width = cent_ref.shape
    count = scaled.shape[0]
    prior = column(prior_ref[...].astype(jnp.float32))
    target = jnp.where(facts[0:1, :] == me, facts[8:9, :] * 32 + facts[9:10, :], -1)
    step = 256
    for start in range(0, rows, step):
        old = cent_ref[start : start + step, :].astype(jnp.float32)
        hits = one_hot(target == lax.broadcasted_iota(jnp.int32, (step, count), 0) + start)
        sums = jnp.dot(hits, scaled[...], preferred_element_type=jnp.float32)
        gained = jnp.sum(hits.astype(jnp.float32), axis=1, keepdims=True)
        ahead = prior[start : start + step, :]
        updated = (ahead * old + sums) * (1.0 / (ahead + gained))
        fresh_rows[start : start + step, :] = updated.astype(jnp.bfloat16)
        gained_row = lax.dot_general(
            jnp.ones((8, count), jnp.bfloat16), hits, NT, preferred_element_type=jnp.float32
        )
        fresh_counts[0:1, start : start + step] = prior_ref[0:1, start : start + step] + gained_row[0:1, :].astype(jnp.int32)


def level_sums(two, packed, floors, w, per):
    block, width = two.shape[0] // per, two.shape[1]
    lines = []
    for j in range(per):
        rows = packed[w, j]
        floor = floors[w, j]
        scores = lax.dot_general(two[j * block : (j + 1) * block, :], rows, NT, preferred_element_type=jnp.float32)
        power = lax.dot_general(
            jnp.ones((8, width), jnp.bfloat16), rows * rows, NT, preferred_element_type=jnp.float32
        ) + lax.dot_general(
            jnp.ones((8, floor.shape[1]), jnp.bfloat16), floor * floor, NT, preferred_element_type=jnp.float32
        )
        power = jnp.where(power > 0.0, power, 1.0) * (1.0 / width)
        lines.append(jnp.sum(weights(scores * lax.rsqrt(power[0:1, :]), width), axis=0, keepdims=True))
    return jnp.concatenate(lines, axis=0)


def redo(cap, per, scaled, facts_in, me, refs, firsts, packed, floors):
    part = per * cap
    planes = packed.shape[0]
    count = planes * part
    width = scaled.shape[1]
    probe0 = facts_in[0:1, :]
    slots = facts_in[8:9, :] * 32 + facts_in[9:10, :]
    lane = lax.broadcasted_iota(jnp.int32, (count, 128), 1)
    for r, (ref, first) in enumerate(zip(refs, firsts)):
        facts = jnp.transpose(ref[ref.shape[0] - META :, first : first + count].astype(jnp.float32))
        hits = (facts[:, 0:1] * 32.0 + facts[:, 1:2]).astype(jnp.int32) == jnp.where(probe0 == (me ^ r), slots + 1, -1)
        gained = jnp.sum(jnp.where(hits, 1.0, 0.0), axis=1, keepdims=True)
        ahead = facts[:, 2:3]
        floor = (ahead + gained) * math.sqrt(1e-06 * width)
        floor = jnp.where(lane == 0, floor, 0.0).astype(jnp.bfloat16)
        added = jnp.dot(one_hot(hits), scaled[...], preferred_element_type=jnp.float32)
        whole = (ahead * ref[0:count, :].astype(jnp.float32) + added).astype(jnp.bfloat16)
        for w in range(planes):
            for j in range(per):
                start = w * part + j * cap
                packed[w, j, r * cap : (r + 1) * cap, :] = whole[start : start + cap, :]
                floors[w, j, r * cap : (r + 1) * cap, :] = floor[start : start + cap, :]


def early_kernel(
    cap, per, scaled, facts_in, units_any, cross_any, passed_any, any0, any1, any2, any3,
    sums, rows0, rows1, rows2, rows3, units, two_last, packed, floors, sems,
):
    me, z, y, core = position()
    end = (z == 0) | (z == 3)
    refs = (rows0, rows1, rows2, rows3)
    at_end = pltpu.make_async_copy(passed_any, two_last, sems.at[5])
    at_mid = pltpu.make_async_copy(cross_any, two_last, sems.at[5])
    copies = fetch(list(zip((any0, any1, any2, any3, units_any), (*refs, units))), sems)
    pl.when(end)(at_end.start)
    pl.when(jnp.logical_not(end))(at_mid.start)
    for copy in copies:
        copy.wait()
    pl.when(end)(at_end.wait)
    pl.when(jnp.logical_not(end))(at_mid.wait)
    redo(cap, per, scaled, facts_in, me, refs, (0, 0, 0, 0), packed, floors)
    third = unit_wide(two_last[...].astype(jnp.float32))
    for w, two in enumerate((units[0], units[1], third)):
        sums[8 * w : 8 * w + per, :] = level_sums(two, packed, floors, w, per)


def late_kernel(
    cap, per, scaled, facts_in, any0, any1, any2, any3, after, updated, packed, floors, rows0, rows1, rows2, rows3, sems
):
    me, z, y, core = position()
    part = per * cap
    tail = pl.ds(3 * part, part + META)
    refs = (rows0, rows1, rows2, rows3)
    copies = fetch(list(zip((any0.at[tail], any1.at[tail], any2, any3), refs)), sems)
    for copy in copies:
        copy.wait()
    redo(cap, per, scaled, facts_in, me, refs, (3 * part, 3 * part, 0, 0), packed, floors)


def third_kernel(cap, per, early, floors, kept_any, last_any, far_any, inside, across, kept, two, sems):
    me, z, y, core = position()
    end = (z == 0) | (z == 3)
    at_end = pltpu.make_async_copy(far_any, two, sems.at[1])
    at_mid = pltpu.make_async_copy(last_any, two, sems.at[1])
    pl.when(end)(at_end.start)
    pl.when(jnp.logical_not(end))(at_mid.start)
    copies = fetch([(kept_any, kept)], sems)
    pl.when(end)(at_end.wait)
    pl.when(jnp.logical_not(end))(at_mid.wait)
    two_unit = unit_wide(two[...].astype(jnp.float32))
    copies[0].wait()
    final = level_sums(two_unit, kept, floors, 0, per)
    lines = [early[8 * w : 8 * w + per, :] for w in range(3)] + [final]
    together = jnp.concatenate(lines + [jnp.zeros((16 - 4 * per, 4 * cap), jnp.float32)], axis=0)
    lane = lax.broadcasted_iota(jnp.int32, together.shape, 1)
    line = lax.broadcasted_iota(jnp.int32, together.shape, 0)
    for r in range(4):
        out, start = (inside, across)[r // 2], 4 * (r % 2)
        spread = jnp.zeros_like(together)
        for s in range(4):
            turned = together if s == r else pltpu.roll(together, ((s - r) % 4) * cap, 1)
            spread = jnp.where((line % 4 == s) & (lane >= s * cap) & (lane < (s + 1) * cap), turned, spread)
        for t in range(4):
            out[start + t : start + t + 1, :] = jnp.sum(spread[4 * t : 4 * t + 4], axis=0, keepdims=True)


def last_kernel(cap, scale_one, scale_two, info, inside, across, beside, share0, share1, share2, share3, density, level_two):
    total = share0[...] + share1[...] + share2[...] + share3[...]
    density[...] = jnp.log(total[:, 0 : density.shape[1]] / scale_one)
    values = jnp.concatenate([inside[0:4, :], beside[0:4, :], across[0:4, :], beside[4:8, :]], axis=0)
    rows = info.shape[1]
    chosen = jnp.where(info[2:3, :] == lax.broadcasted_iota(jnp.int32, (4 * cap, rows), 0), 1.0, 0.0)
    spread = jnp.dot(values, chosen, precision=lax.Precision.HIGHEST, preferred_element_type=jnp.float32)
    found = jnp.where(info[1:2, :] == lax.broadcasted_iota(jnp.int32, (16, rows), 0), spread, 0.0)
    level_two[...] = jnp.log(jnp.sum(found, axis=0, keepdims=True) / scale_two)


def call(kernel, outs, scratch=(), in_specs=None, **kw):
    def run(*args):
        specs = in_specs or [VMEM] * len(args)
        args = [pltpu.with_memory_space_constraint(a, pltpu.HBM) if spec is HBM else a for a, spec in zip(args, specs)]
        return pl.pallas_call(
            kernel, out_shape=outs, in_specs=specs, scratch_shapes=list(scratch), compiler_params=PARAMS, **kw
        )(*args)

    return run


def lasting(micros):
    return pl.CostEstimate(flops=0, transcendentals=0, bytes_accessed=int(micros * 3_690_000))


def in_order(*values, **kw):
    count = len(values)
    return call(
        order_kernel,
        tuple(jax.ShapeDtypeStruct(value.shape, value.dtype) for value in values),
        in_specs=[ANY] * count,
        out_specs=(ANY,) * count,
        input_output_aliases={i: i for i in range(count)},
        **kw,
    )(*values)


def line_body(embeddings, probes, assigned, prior_counts, centroids, candidates, centroids2):
    emb_rows, width = embeddings.shape
    probe_count = probes.shape[1]
    rows = centroids.shape[0]
    per = BLOCKS2_DEV
    cap = max(2, 3 * rows // (2 * per * 16))
    part = per * cap
    bf16, f32, i32 = jnp.bfloat16, jnp.float32, jnp.int32
    shape = jax.ShapeDtypeStruct

    def exchange(value, apart, sources=range(16)):
        return lax.ppermute(value, "shard", [(i, i ^ apart) for i in sources])

    def rows_of(planes):
        return shape((planes * part + META, width), bf16)

    def room(like):
        return pltpu.VMEM(like.shape, like.dtype)

    mids = range(4, 12)
    near_set = exchange(centroids2, 4)
    cross_set = exchange(centroids2, 12, mids)
    prior_row = prior_counts.reshape(1, rows)
    line = pltpu.VMEM((1, rows), i32)
    mine, early2, early3, info = call(
        functools.partial(pack_kernel, cap, per),
        (shape((emb_rows, width + 128), bf16), rows_of(3), rows_of(3), shape((8, rows), i32)),
        [
            line,
            pltpu.VMEM((emb_rows, width), bf16),
            pltpu.VMEM((probe_count, emb_rows), i32),
            pltpu.VMEM((1, emb_rows), i32),
            line,
            pltpu.VMEM((rows, width), bf16),
            pltpu.SemaphoreType.DMA((6,)),
        ],
        in_specs=[HBM] * 6,
    )(candidates.reshape(1, rows), embeddings, probes.T, assigned.reshape(1, emb_rows), prior_row, centroids)
    early2, early3 = exchange(early2, 2), exchange(early3, 3)
    rows0, rows1, late2, late3 = call(
        functools.partial(pack_more_kernel, part), (rows_of(4), rows_of(4), rows_of(1), rows_of(1))
    )(info, prior_row, centroids)
    mine = jnp.concatenate([mine, exchange(mine, 4)], axis=0)
    near_set, cross_set, mine, rows0 = in_order(near_set, cross_set, mine, rows0)
    across = exchange(mine, 12)
    passed = exchange(cross_set, 4, mids)
    last_set = exchange(near_set, 12, mids)
    mine = jnp.concatenate([mine, across], axis=0)
    mine, early2, early3, late2, late3, rows1 = in_order(mine, early2, early3, late2, late3, rows1)
    mine = jnp.concatenate([mine, exchange(mine, 2)], axis=0)
    late2, late3 = exchange(late2, 2), exchange(late3, 3)
    rows1 = exchange(rows1, 1)
    set_rows = per * BLOCK2
    block_set = pltpu.VMEM((set_rows, width), bf16)
    unit_old, units = call(
        prepare_kernel,
        (shape((rows, width), bf16), shape((2, set_rows, width), bf16)),
        [block_set, block_set, pltpu.SemaphoreType.DMA((2,))],
        in_specs=[VMEM, HBM, ANY],
    )(centroids, centroids2, near_set)
    passed, last_set, unit_old, units = in_order(passed, last_set, unit_old, units)
    far_set = exchange(last_set, 4, mids)
    other = exchange(mine, 1)
    gathered = pltpu.VMEM((8 * emb_rows, width + 128), bf16)
    scaled, facts, share, share_high = call(
        share_kernel,
        (
            shape((16 * emb_rows, width), bf16),
            shape((16, 16 * emb_rows), i32),
            shape((8, 4 * cap), f32),
            shape((8, 4 * cap), f32),
        ),
        [gathered, gathered, pltpu.SemaphoreType.DMA((2,))],
        in_specs=[ANY, ANY, VMEM],
    )(mine, other, unit_old)
    share = share + exchange(share_high, 1)
    share = share[0:4] + exchange(share[4:8], 2)
    early = call(
        functools.partial(early_kernel, cap, per),
        shape((24, 4 * cap), f32),
        [room(rows_of(4))] * 2
        + [room(rows_of(3))] * 2
        + [
            pltpu.VMEM((2, set_rows, width), bf16),
            block_set,
            pltpu.VMEM((3, per, 4 * cap, width), bf16),
            pltpu.VMEM((3, per, 4 * cap, 128), bf16),
            pltpu.SemaphoreType.DMA((6,)),
        ],
        in_specs=[VMEM, VMEM] + [ANY] * 7,
    )(scaled, facts, units, cross_set, passed, rows0, rows1, early2, early3)
    new_centroids, counts = call(
        update_kernel, (shape((rows, width), bf16), shape((1, rows), i32)), in_specs=[ANY] + [VMEM] * 4
    )(early, scaled, facts, centroids, prior_row)
    kept = shape((1, per, 4 * cap, width), bf16)
    kept_rows, floors = call(
        functools.partial(late_kernel, cap, per),
        (kept, shape((1, per, 4 * cap, 128), bf16)),
        [room(rows_of(1))] * 4 + [pltpu.SemaphoreType.DMA((4,))],
        in_specs=[VMEM] * 2 + [ANY] * 6,
    )(scaled, facts, rows0, rows1, late2, late3, early, counts)
    tile = shape((8, 4 * cap), f32)
    inside, across = call(
        functools.partial(third_kernel, cap, per),
        (tile,) * 2,
        [room(kept), block_set, pltpu.SemaphoreType.DMA((2,))],
        in_specs=[VMEM, VMEM] + [ANY] * 3,
    )(early, floors, kept_rows, last_set, far_set)
    across = exchange(across, 2)
    beside = exchange(jnp.concatenate([inside[4:8], across[4:8]], axis=0), 1)
    share = [share[0:1]] + [exchange(share[i : i + 1], apart) for i, apart in ((1, 4), (2, 12), (3, 8))]
    density, level_two = call(
        functools.partial(last_kernel, cap, probe_count * BLOCK, BLOCK2), (shape((1, emb_rows), f32), shape((1, rows), f32))
    )(info, inside, across, beside, *share)
    return (density.reshape(-1), new_centroids, counts.reshape(-1), level_two.reshape(-1))


def solution(mesh):
    placed = (
        P(("groups", "shard"), None),
        P(("groups", "shard"), None),
        P(("groups", "shard")),
        P(("groups", "shard")),
        P(("groups", "shard"), None),
        P(("groups", "shard"), None),
        P(("groups", "shard"), None),
    )
    body = line_body if mesh.shape["shard"] == 16 else general_body
    return jax.shard_map(
        body,
        mesh=mesh,
        in_specs=placed,
        out_specs=(
            P(("groups", "shard")),
            P(("groups", "shard"), None),
            P(("groups", "shard")),
            P(("groups", "shard")),
        ),
        check_vma=False,
    )
```

profile of v0, /device:TPU:0, one launch (start us, length us, event | category | flops | bytes accessed | tf_op | source)
XLA Modules:
  0.0 88.5 jit_solution(6860074052075403344)
XLA Ops:
  0.6 0.0 copy-start
  0.6 0.0 copy-start.3
  0.7 3.1 %collective-permute-start = (bf16[384,1024]{1,0:T(8,128)(2,1)}, bf16[384,1024]{1,0:T(8,128)(2,1)S(1)}, u32[]{:S(2)}, u32[]{:S(2)}) collective-permute-start(bf16[384,1024]{1,0:T(8,128)(2,1)} %own_any.1), channel_id=1, source_target_pairs={{0,4},{1,5},{2,6},{3,7},{4,0},{5,1},{6,2},{7,3},{8,12},{9,13},{10,... | collective-permute-start | bytes 2359304 | tf_op jit(solution)/shard_map/ppermute | solution.py:469
  3.7 0.7 collective-permute-start.1
  4.5 3.4 %shard_map.102 = (bf16[40,1152]{1,0:T(8,128)(2,1)S(1)}, bf16[304,1024]{1,0:T(8,128)(2,1)S(1)}, bf16[304,1024]{1,0:T(8,128)(2,1)S(1)}, s32[8,1024]{1,0:T(8,128)S(1)}) custom-call(s32[1,1024]{1,0:T(1,128)} %bitcast.11, bf16[40,1024]{1,0:T(8,128)(2,1)} %emb_any.1, s32[8,40]{1,0:T(8,128)} %bitcast.12, s32[1,40]{1,0:T(1,128)} %bitcast.13, s32[1,1024]{1,0:T(1,128)} %bitcast.7, ...), custom_call_target="tpu_custom_call" | custom-call | tf_op jit(solution)/shard_map/pallas_call | solution.py:435
  7.8 4.4 %collective-permute-start.2 = (bf16[40,1152]{1,0:T(8,128)(2,1)S(1)}, bf16[40,1152]{1,0:T(8,128)(2,1)S(1)}, u32[]{:S(2)}, u32[]{:S(2)}) collective-permute-start(bf16[40,1152]{1,0:T(8,128)(2,1)S(1)} %get-tuple-element.41), channel_id=1, source_target_pairs={{0,4},{1,5},{2,6},{3,7},{4,0},{5,1},{6,2},{7,3},{8,12},{9,13},{10,... | collective-permute-start | bytes 276488 | tf_op jit(solution)/shard_map/ppermute | solution.py:469
  12.3 1.5 %collective-permute-start.4 = (bf16[304,1024]{1,0:T(8,128)(2,1)S(1)}, bf16[304,1024]{1,0:T(8,128)(2,1)S(1)}, u32[]{:S(2)}, u32[]{:S(2)}) collective-permute-start(bf16[304,1024]{1,0:T(8,128)(2,1)S(1)} %get-tuple-element.44), channel_id=1, source_target_pairs={{0,2},{1,3},{2,0},{3,1},{4,6},{5,7},{6,4},{7,5},{8,10},{9,11},{10,... | collective-permute-start | bytes 1867784 | tf_op jit(solution)/shard_map/ppermute | solution.py:469
  13.8 0.0 collective-permute-start.5
  13.8 0.0 copy-done
  13.8 0.0 copy-done.3
  13.8 3.7 %shard_map.103 = (bf16[400,1024]{1,0:T(8,128)(2,1)S(1)}, bf16[400,1024]{1,0:T(8,128)(2,1)}, bf16[112,1024]{1,0:T(8,128)(2,1)S(1)}, bf16[112,1024]{1,0:T(8,128)(2,1)S(1)}) custom-call(s32[8,1024]{1,0:T(8,128)S(1)} %get-tuple-element.40.info, s32[1,1024]{1,0:T(1,128)S(1)} %bitcast.8, bf16[1024,1024]{1,0:T(8,128)(2,1)S(1)} %copy-done), custom_call_target="tpu_custom_call" | custom-call | tf_op jit(solution)/shard_map/pallas_call | solution.py:435
  17.5 6.0 %collective-permute-done.2 = bf16[40,1152]{1,0:T(8,128)(2,1)S(1)} collective-permute-done((bf16[40,1152]{1,0:T(8,128)(2,1)S(1)}, bf16[40,1152]{1,0:T(8,128)(2,1)S(1)}, u32[]{:S(2)}, u32[]{:S(2)}) %collective-permute-start.2) | collective-permute-done | bytes 92192 | tf_op jit(solution)/shard_map/ppermute | solution.py:469
  23.5 0.0 collective-permute-done.refs_0_
  23.5 0.0 collective-permute-done.1.refs_1_
  23.5 3.8 %collective-permute-start.3 = (bf16[80,1152]{1,0:T(8,128)(2,1)S(1)}, bf16[80,1152]{1,0:T(8,128)(2,1)S(1)}, u32[]{:S(2)}, u32[]{:S(2)}) collective-permute-start(bf16[80,1152]{1,0:T(8,128)(2,1)S(1)} %get-tuple-element.43), channel_id=1, source_target_pairs={{0,12},{1,13},{2,14},{3,15},{4,8},{5,9},{6,10},{7,11},{8,4},{9,5},... | collective-permute-start | bytes 552968 | tf_op jit(solution)/shard_map/ppermute | solution.py:469
  27.4 1.3 %collective-permute-start.8 = (bf16[384,1024]{1,0:T(8,128)(2,1)S(1)}, bf16[384,1024]{1,0:T(8,128)(2,1)S(1)}, u32[]{:S(2)}, u32[]{:S(2)}) collective-permute-start(bf16[384,1024]{1,0:T(8,128)(2,1)S(1)} %get-tuple-element.50.cross_any), channel_id=1, source_target_pairs={{4,0},{5,1},{6,2},{7,3},{8,12},{9,13},{10,14},{11,15},{20,16},{21,... | collective-permute-start | bytes 2359304 | tf_op jit(solution)/shard_map/ppermute | solution.py:469
  28.6 0.7 collective-permute-start.9
  29.4 2.0 %collective-permute-done.3 = bf16[80,1152]{1,0:T(8,128)(2,1)S(1)} collective-permute-done((bf16[80,1152]{1,0:T(8,128)(2,1)S(1)}, bf16[80,1152]{1,0:T(8,128)(2,1)S(1)}, u32[]{:S(2)}, u32[]{:S(2)}) %collective-permute-start.3) | collective-permute-done | bytes 184352 | tf_op jit(solution)/shard_map/ppermute | solution.py:469
  31.4 0.0 collective-permute-done.4.refs_1_
  31.4 8.1 %collective-permute-done.5.refs_2_ = bf16[304,1024]{1,0:T(8,128)(2,1)S(1)} collective-permute-done((bf16[304,1024]{1,0:T(8,128)(2,1)S(1)}, bf16[304,1024]{1,0:T(8,128)(2,1)S(1)}, u32[]{:S(2)}, u32[]{:S(2)}) %collective-permute-start.5) | collective-permute-done | bytes 622624 | tf_op jit(solution)/shard_map/ppermute | solution.py:469
  39.6 0.5 collective-permute-start.6
  40.1 3.2 %shard_map.106 = (bf16[1024,1024]{1,0:T(8,128)(2,1)S(1)}, bf16[2,384,1024]{2,1,0:T(8,128)(2,1)S(1)}) custom-call(bf16[1024,1024]{1,0:T(8,128)(2,1)} %cent_ref.5, bf16[384,1024]{1,0:T(8,128)(2,1)} %own_any.1, bf16[384,1024]{1,0:T(8,128)(2,1)S(1)} %get-tuple-element.51.near_any), custom_call_target="tpu_custom_call" | custom-call | tf_op jit(solution)/shard_map/pallas_call | solution.py:435
  43.3 1.9 %collective-permute-start.10 = (bf16[400,1024]{1,0:T(8,128)(2,1)}, bf16[400,1024]{1,0:T(8,128)(2,1)S(1)}, u32[]{:S(2)}, u32[]{:S(2)}) collective-permute-start(bf16[400,1024]{1,0:T(8,128)(2,1)} %get-tuple-element.60), channel_id=1, source_target_pairs={{0,1},{1,0},{2,3},{3,2},{4,5},{5,4},{6,7},{7,6},{8,9},{9,8},{10,11... | collective-permute-start | bytes 2457608 | tf_op jit(solution)/shard_map/ppermute | solution.py:469
  45.2 2.9 %collective-permute-done.8.refs_0_ = bf16[384,1024]{1,0:T(8,128)(2,1)S(1)} collective-permute-done((bf16[384,1024]{1,0:T(8,128)(2,1)S(1)}, bf16[384,1024]{1,0:T(8,128)(2,1)S(1)}, u32[]{:S(2)}, u32[]{:S(2)}) %collective-permute-start.8) | collective-permute-done | bytes 786464 | tf_op jit(solution)/shard_map/ppermute | solution.py:469
  48.2 0.0 collective-permute-done.9.refs_1_
  48.2 0.0 copy-start.2
  48.2 1.3 %collective-permute-start.13 = (bf16[384,1024]{1,0:T(8,128)(2,1)S(1)}, bf16[384,1024]{1,0:T(8,128)(2,1)}, u32[]{:S(2)}, u32[]{:S(2)}) collective-permute-start(bf16[384,1024]{1,0:T(8,128)(2,1)S(1)} %get-tuple-element.68.last_any), channel_id=1, source_target_pairs={{4,0},{5,1},{6,2},{7,3},{8,12},{9,13},{10,14},{11,15},{20,16},{21,... | collective-permute-start | bytes 2359304 | tf_op jit(solution)/shard_map/ppermute | solution.py:469
  49.5 1.5 %collective-permute-done.6 = bf16[160,1152]{1,0:T(8,128)(2,1)S(1)} collective-permute-done((bf16[160,1152]{1,0:T(8,128)(2,1)S(1)}, bf16[160,1152]{1,0:T(8,128)(2,1)S(1)}, u32[]{:S(2)}, u32[]{:S(2)}) %collective-permute-start.6) | collective-permute-done | bytes 368672 | tf_op jit(solution)/shard_map/ppermute | solution.py:469
  51.0 0.2 collective-permute-start.7
  51.1 0.3 collective-permute-start.11
  51.5 1.4 %collective-permute-start.12 = (bf16[112,1024]{1,0:T(8,128)(2,1)S(1)}, bf16[112,1024]{1,0:T(8,128)(2,1)S(1)}, u32[]{:S(2)}, u32[]{:S(2)}) collective-permute-start(bf16[112,1024]{1,0:T(8,128)(2,1)S(1)} %get-tuple-element.64), channel_id=1, source_target_pairs={{0,3},{1,2},{2,1},{3,0},{4,7},{5,6},{6,5},{7,4},{8,11},{9,10},{10,... | collective-permute-start | bytes 688136 | tf_op jit(solution)/shard_map/ppermute | solution.py:469
  52.9 0.4 collective-permute-done.7.other_any
  53.2 3.1 %shard_map.108 = (bf16[640,1024]{1,0:T(8,128)(2,1)S(1)}, s32[16,640]{1,0:T(8,128)S(1)}, f32[8,128]{1,0:T(8,128)S(1)}, f32[8,128]{1,0:T(8,128)S(1)}) custom-call(bf16[320,1152]{1,0:T(8,128)(2,1)S(1)} %constant_dynamic-update-slice_fusion.mine_any, bf16[320,1152]{1,0:T(8,128)(2,1)S(1)} %collective-permute-done.7.other_any, ...), custom_call_target="tpu_custom_call" | custom-call | tf_op jit(solution)/shard_map/pallas_call | solution.py:435
  56.3 0.0 copy-done.2
  56.3 0.2 collective-permute-start.16
  56.5 1.0 %collective-permute-done.16 = f32[8,128]{1,0:T(8,128)S(1)} collective-permute-done((f32[8,128]{1,0:T(8,128)S(1)}, f32[8,128]{1,0:T(8,128)S(1)}, u32[]{:S(2)}, u32[]{:S(2)}) %collective-permute-start.16) | collective-permute-done | bytes 4128 | tf_op jit(solution)/shard_map/ppermute | solution.py:469
  57.6 0.1 collective-permute-start.17
  57.7 0.0 collective-permute-done.10.any1
  57.7 0.0 copy-start.1
  57.7 6.0 %shard_map.109.after.early = f32[24,128]{1,0:T(8,128)S(1)} custom-call(bf16[640,1024]{1,0:T(8,128)(2,1)S(1)} %get-tuple-element.55.scaled, s32[16,640]{1,0:T(8,128)S(1)} %get-tuple-element.56.facts_in.facts, bf16[2,384,1024]{2,1,0:T(8,128)(2,1)} %copy-done.2, bf16[384,1024]{1,0:T(8,128)(2,1)S(1)} %get-tuple-element.50.cross_any, ...), custom_call_target="tpu_custom_call" | custom-call | tf_op jit(solution)/shard_map/pallas_call | solution.py:435
  63.7 0.0 copy-done.1
  63.8 3.7 %shard_map.110 = (bf16[1024,1024]{1,0:T(8,128)(2,1)}, s32[1,1024]{1,0:T(1,128)}) custom-call(f32[24,128]{1,0:T(8,128)S(1)} %shard_map.109.after.early, bf16[640,1024]{1,0:T(8,128)(2,1)S(1)} %get-tuple-element.55.scaled, s32[16,640]{1,0:T(8,128)S(1)} %get-tuple-element.56.facts_in.facts, bf16[1024,1024]{1,0:T(8,128)(2,1)S(1)} %copy-done.1, s32[1,1024]{1,0:T(1,128)S(1)} %bitcast.9), custom_call_target="tpu_custom_call" | custom-call | tf_op jit(solution)/shard_map/pallas_call | solution.py:435
  67.4 0.0 collective-permute-done.11.any2
  67.4 0.0 collective-permute-done.12.any3
  67.4 0.0 copy-start.4
  67.5 0.7 copy-done.4
  68.1 2.8 %shard_map.111 = (bf16[1,3,128,1024]{3,2,1,0:T(8,128)(2,1)S(1)}, bf16[1,3,128,128]{3,2,1,0:T(8,128)(2,1)S(1)}) custom-call(bf16[640,1024]{1,0:T(8,128)(2,1)S(1)} %get-tuple-element.55.scaled, s32[16,640]{1,0:T(8,128)S(1)} %get-tuple-element.56.facts_in.facts, bf16[400,1024]{1,0:T(8,128)(2,1)S(1)} %get-tuple-element.59.any0, ...), custom_call_target="tpu_custom_call" | custom-call | tf_op jit(solution)/shard_map/pallas_call | solution.py:435
  70.9 0.0 collective-permute-done.13.far_any
  71.0 2.2 %shard_map.112 = (f32[8,128]{1,0:T(8,128)S(1)}, f32[8,128]{1,0:T(8,128)S(1)}) custom-call(f32[24,128]{1,0:T(8,128)S(1)} %shard_map.109.after.early, bf16[1,3,128,128]{3,2,1,0:T(8,128)(2,1)S(1)} %get-tuple-element.66.floors, bf16[1,3,128,1024]{3,2,1,0:T(8,128)(2,1)S(1)} %get-tuple-element.67.kept_any, bf16[384,1024]{1,0:T(8,128)(2,1)S(1)} %get-tuple-element.68.last_any, ...), custom_call_target="tpu_custom_call" | custom-call | tf_op jit(solution)/shard_map/pallas_call | solution.py:435
  73.1 2.0 %collective-permute-start.14 = (f32[8,128]{1,0:T(8,128)S(1)}, f32[8,128]{1,0:T(8,128)S(1)}, u32[]{:S(2)}, u32[]{:S(2)}) collective-permute-start(f32[8,128]{1,0:T(8,128)S(1)} %get-tuple-element.70), channel_id=1, source_target_pairs={{0,2},{1,3},{2,0},{3,1},{4,6},{5,7},{6,4},{7,5},{8,10},{9,11},{10,... | collective-permute-start | bytes 12296 | tf_op jit(solution)/shard_map/ppermute | solution.py:469
  75.1 0.0 collective-permute-done.17
  75.1 1.7 %collective-permute-done.14.across = f32[8,128]{1,0:T(8,128)S(1)} collective-permute-done((f32[8,128]{1,0:T(8,128)S(1)}, f32[8,128]{1,0:T(8,128)S(1)}, u32[]{:S(2)}, u32[]{:S(2)}) %collective-permute-start.14) | collective-permute-done | bytes 4128 | tf_op jit(solution)/shard_map/ppermute | solution.py:469
  76.8 0.1 collective-permute-start.15
  76.9 5.2 %collective-permute-start.20 = (f32[1,128]{1,0:T(1,128)S(1)}, f32[1,128]{1,0:T(1,128)S(1)}, u32[]{:S(2)}, u32[]{:S(2)}) collective-permute-start(f32[1,128]{1,0:T(1,128)S(1)} %get-tuple-element.76), channel_id=1, source_target_pairs={{0,8},{1,9},{2,10},{3,11},{4,12},{5,13},{6,14},{7,15},{8,0},{9,1},... | collective-permute-start | bytes 1544 | tf_op jit(solution)/shard_map/ppermute | solution.py:469
  82.1 1.4 %collective-permute-start.19 = (f32[1,128]{1,0:T(1,128)S(1)}, f32[1,128]{1,0:T(1,128)S(1)}, u32[]{:S(2)}, u32[]{:S(2)}) collective-permute-start(f32[1,128]{1,0:T(1,128)S(1)} %get-tuple-element.77), channel_id=1, source_target_pairs={{0,12},{1,13},{2,14},{3,15},{4,8},{5,9},{6,10},{7,11},{8,4},{9,5},... | collective-permute-start | bytes 1544 | tf_op jit(solution)/shard_map/ppermute | solution.py:469
  83.5 0.0 collective-permute-start.18
  83.5 0.1 collective-permute-done.20.share3
  83.6 3.8 %collective-permute-done.19.share2 = f32[1,128]{1,0:T(1,128)S(1)} collective-permute-done((f32[1,128]{1,0:T(1,128)S(1)}, f32[1,128]{1,0:T(1,128)S(1)}, u32[]{:S(2)}, u32[]{:S(2)}) %collective-permute-start.19) | collective-permute-done | bytes 544 | tf_op jit(solution)/shard_map/ppermute | solution.py:469
  87.4 0.0 collective-permute-done.18.share1
  87.4 0.0 collective-permute-done.15.beside
  87.4 1.0 %shard_map.113 = (f32[1,40]{1,0:T(1,128)}, f32[1,1024]{1,0:T(1,128)}) custom-call(s32[8,1024]{1,0:T(8,128)S(1)} %get-tuple-element.40.info, f32[8,128]{1,0:T(8,128)S(1)} %get-tuple-element.69.inside, f32[8,128]{1,0:T(8,128)S(1)} %collective-permute-done.14.across, f32[8,128]{1,0:T(8,128)S(1)} %collective-permute-done.15.beside, ...), custom_call_target="tpu_custom_call" | custom-call | tf_op jit(solution)/shard_map/pallas_call | solution.py:435
  (14 shorter events, 0.2 us)
Async XLA Ops:
  0.6 13.1 %copy-start = (bf16[1024,1024]{1,0:T(8,128)(2,1)S(1)}, bf16[1024,1024]{1,0:T(8,128)(2,1)}, u32[]{:S(2)}) copy-start(bf16[1024,1024]{1,0:T(8,128)(2,1)} %cent_ref.5) | copy-start | bytes 6291460
  0.6 13.1 %copy-start.3 = (s32[1024]{0:T(1024)S(1)}, s32[1024]{0:T(1024)}, u32[]{:S(2)}) copy-start(s32[1024]{0:T(1024)} %param.10) | copy-start | bytes 12292
  0.7 22.8 %collective-permute-start = (bf16[384,1024]{1,0:T(8,128)(2,1)}, bf16[384,1024]{1,0:T(8,128)(2,1)S(1)}, u32[]{:S(2)}, u32[]{:S(2)}) collective-permute-start(bf16[384,1024]{1,0:T(8,128)(2,1)} %own_any.1), channel_id=1, source_target_pairs={{0,4},{1,5},{2,6},{3,7},{4,0},{5,1},{6,2},{7,3},{8,12},{9,13},{10,... | collective-permute-start | bytes 2359304 | tf_op jit(solution)/shard_map/ppermute | solution.py:469
  3.7 19.8 %collective-permute-start.1 = (bf16[384,1024]{1,0:T(8,128)(2,1)}, bf16[384,1024]{1,0:T(8,128)(2,1)S(1)}, u32[]{:S(2)}, u32[]{:S(2)}) collective-permute-start(bf16[384,1024]{1,0:T(8,128)(2,1)} %own_any.1), channel_id=1, source_target_pairs={{4,8},{5,9},{6,10},{7,11},{8,4},{9,5},{10,6},{11,7},{20,24},{21,25... | collective-permute-start | bytes 2359304 | tf_op jit(solution)/shard_map/ppermute | solution.py:469
  7.8 15.6 %collective-permute-start.2 = (bf16[40,1152]{1,0:T(8,128)(2,1)S(1)}, bf16[40,1152]{1,0:T(8,128)(2,1)S(1)}, u32[]{:S(2)}, u32[]{:S(2)}) collective-permute-start(bf16[40,1152]{1,0:T(8,128)(2,1)S(1)} %get-tuple-element.41), channel_id=1, source_target_pairs={{0,4},{1,5},{2,6},{3,7},{4,0},{5,1},{6,2},{7,3},{8,12},{9,13},{10,... | collective-permute-start | bytes 276488 | tf_op jit(solution)/shard_map/ppermute | solution.py:469
  12.3 19.2 %collective-permute-start.4 = (bf16[304,1024]{1,0:T(8,128)(2,1)S(1)}, bf16[304,1024]{1,0:T(8,128)(2,1)S(1)}, u32[]{:S(2)}, u32[]{:S(2)}) collective-permute-start(bf16[304,1024]{1,0:T(8,128)(2,1)S(1)} %get-tuple-element.44), channel_id=1, source_target_pairs={{0,2},{1,3},{2,0},{3,1},{4,6},{5,7},{6,4},{7,5},{8,10},{9,11},{10,... | collective-permute-start | bytes 1867784 | tf_op jit(solution)/shard_map/ppermute | solution.py:469
  13.8 25.8 %collective-permute-start.5 = (bf16[304,1024]{1,0:T(8,128)(2,1)S(1)}, bf16[304,1024]{1,0:T(8,128)(2,1)S(1)}, u32[]{:S(2)}, u32[]{:S(2)}) collective-permute-start(bf16[304,1024]{1,0:T(8,128)(2,1)S(1)} %get-tuple-element.45), channel_id=1, source_target_pairs={{0,3},{1,2},{2,1},{3,0},{4,7},{5,6},{6,5},{7,4},{8,11},{9,10},{10,... | collective-permute-start | bytes 1867784 | tf_op jit(solution)/shard_map/ppermute | solution.py:469
  23.5 7.9 %collective-permute-start.3 = (bf16[80,1152]{1,0:T(8,128)(2,1)S(1)}, bf16[80,1152]{1,0:T(8,128)(2,1)S(1)}, u32[]{:S(2)}, u32[]{:S(2)}) collective-permute-start(bf16[80,1152]{1,0:T(8,128)(2,1)S(1)} %get-tuple-element.43), channel_id=1, source_target_pairs={{0,12},{1,13},{2,14},{3,15},{4,8},{5,9},{6,10},{7,11},{8,4},{9,5},... | collective-permute-start | bytes 552968 | tf_op jit(solution)/shard_map/ppermute | solution.py:469
  27.4 20.8 %collective-permute-start.8 = (bf16[384,1024]{1,0:T(8,128)(2,1)S(1)}, bf16[384,1024]{1,0:T(8,128)(2,1)S(1)}, u32[]{:S(2)}, u32[]{:S(2)}) collective-permute-start(bf16[384,1024]{1,0:T(8,128)(2,1)S(1)} %get-tuple-element.50.cross_any), channel_id=1, source_target_pairs={{4,0},{5,1},{6,2},{7,3},{8,12},{9,13},{10,14},{11,15},{20,16},{21,... | collective-permute-start | bytes 2359304 | tf_op jit(solution)/shard_map/ppermute | solution.py:469
  28.6 19.5 %collective-permute-start.9 = (bf16[384,1024]{1,0:T(8,128)(2,1)S(1)}, bf16[384,1024]{1,0:T(8,128)(2,1)S(1)}, u32[]{:S(2)}, u32[]{:S(2)}) collective-permute-start(bf16[384,1024]{1,0:T(8,128)(2,1)S(1)} %get-tuple-element.51.near_any), channel_id=1, source_target_pairs={{4,8},{5,9},{6,10},{7,11},{8,4},{9,5},{10,6},{11,7},{20,24},{21,25... | collective-permute-start | bytes 2359304 | tf_op jit(solution)/shard_map/ppermute | solution.py:469
  39.6 11.4 %collective-permute-start.6 = (bf16[160,1152]{1,0:T(8,128)(2,1)S(1)}, bf16[160,1152]{1,0:T(8,128)(2,1)S(1)}, u32[]{:S(2)}, u32[]{:S(2)}) collective-permute-start(bf16[160,1152]{1,0:T(8,128)(2,1)S(1)} %get-tuple-element.49), channel_id=1, source_target_pairs={{0,2},{1,3},{2,0},{3,1},{4,6},{5,7},{6,4},{7,5},{8,10},{9,11},{10,... | collective-permute-start | bytes 1105928 | tf_op jit(solution)/shard_map/ppermute | solution.py:469
  43.3 14.4 %collective-permute-start.10 = (bf16[400,1024]{1,0:T(8,128)(2,1)}, bf16[400,1024]{1,0:T(8,128)(2,1)S(1)}, u32[]{:S(2)}, u32[]{:S(2)}) collective-permute-start(bf16[400,1024]{1,0:T(8,128)(2,1)} %get-tuple-element.60), channel_id=1, source_target_pairs={{0,1},{1,0},{2,3},{3,2},{4,5},{5,4},{6,7},{7,6},{8,9},{9,8},{10,11... | collective-permute-start | bytes 2457608 | tf_op jit(solution)/shard_map/ppermute | solution.py:469
  48.2 8.2 %copy-start.2 = (bf16[2,384,1024]{2,1,0:T(8,128)(2,1)}, bf16[2,384,1024]{2,1,0:T(8,128)(2,1)S(1)}, u32[]{:S(2)}) copy-start(bf16[2,384,1024]{2,1,0:T(8,128)(2,1)S(1)} %get-tuple-element.57.units_any) | copy-start | bytes 4718596
  48.2 22.8 %collective-permute-start.13 = (bf16[384,1024]{1,0:T(8,128)(2,1)S(1)}, bf16[384,1024]{1,0:T(8,128)(2,1)}, u32[]{:S(2)}, u32[]{:S(2)}) collective-permute-start(bf16[384,1024]{1,0:T(8,128)(2,1)S(1)} %get-tuple-element.68.last_any), channel_id=1, source_target_pairs={{4,0},{5,1},{6,2},{7,3},{8,12},{9,13},{10,14},{11,15},{20,16},{21,... | collective-permute-start | bytes 2359304 | tf_op jit(solution)/shard_map/ppermute | solution.py:469
  51.0 2.3 %collective-permute-start.7 = (bf16[320,1152]{1,0:T(8,128)(2,1)S(1)}, bf16[320,1152]{1,0:T(8,128)(2,1)S(1)}, u32[]{:S(2)}, u32[]{:S(2)}) collective-permute-start(bf16[320,1152]{1,0:T(8,128)(2,1)S(1)} %constant_dynamic-update-slice_fusion.mine_any), channel_id=1, source_target_pairs={{0,1},{1,0},{2,3},{3,2},{4,5},{5,4},{6,7},{7,6},{8,9},{9,8},{10,11... | collective-permute-start | bytes 2211848 | tf_op jit(solution)/shard_map/ppermute | solution.py:469
  51.1 16.3 %collective-permute-start.11 = (bf16[112,1024]{1,0:T(8,128)(2,1)S(1)}, bf16[112,1024]{1,0:T(8,128)(2,1)S(1)}, u32[]{:S(2)}, u32[]{:S(2)}) collective-permute-start(bf16[112,1024]{1,0:T(8,128)(2,1)S(1)} %get-tuple-element.63), channel_id=1, source_target_pairs={{0,2},{1,3},{2,0},{3,1},{4,6},{5,7},{6,4},{7,5},{8,10},{9,11},{10,... | collective-permute-start | bytes 688136 | tf_op jit(solution)/shard_map/ppermute | solution.py:469
  51.5 16.0 %collective-permute-start.12 = (bf16[112,1024]{1,0:T(8,128)(2,1)S(1)}, bf16[112,1024]{1,0:T(8,128)(2,1)S(1)}, u32[]{:S(2)}, u32[]{:S(2)}) collective-permute-start(bf16[112,1024]{1,0:T(8,128)(2,1)S(1)} %get-tuple-element.64), channel_id=1, source_target_pairs={{0,3},{1,2},{2,1},{3,0},{4,7},{5,6},{6,5},{7,4},{8,11},{9,10},{10,... | collective-permute-start | bytes 688136 | tf_op jit(solution)/shard_map/ppermute | solution.py:469
  56.3 1.2 %collective-permute-start.16 = (f32[8,128]{1,0:T(8,128)S(1)}, f32[8,128]{1,0:T(8,128)S(1)}, u32[]{:S(2)}, u32[]{:S(2)}) collective-permute-start(f32[8,128]{1,0:T(8,128)S(1)} %get-tuple-element.72), channel_id=1, source_target_pairs={{0,1},{1,0},{2,3},{3,2},{4,5},{5,4},{6,7},{7,6},{8,9},{9,8},{10,11... | collective-permute-start | bytes 12296 | tf_op jit(solution)/shard_map/ppermute | solution.py:469
  57.6 17.5 %collective-permute-start.17 = (f32[4,128]{1,0:T(4,128)S(1)}, f32[4,128]{1,0:T(4,128)S(1)}, u32[]{:S(2)}, u32[]{:S(2)}) collective-permute-start(f32[4,128]{1,0:T(4,128)S(1)} %slice.27), channel_id=1, source_target_pairs={{0,2},{1,3},{2,0},{3,1},{4,6},{5,7},{6,4},{7,5},{8,10},{9,11},{10,... | collective-permute-start | bytes 6152 | tf_op jit(solution)/shard_map/ppermute | solution.py:469
  57.7 6.1 %copy-start.1 = (bf16[1024,1024]{1,0:T(8,128)(2,1)S(1)}, bf16[1024,1024]{1,0:T(8,128)(2,1)}, u32[]{:S(2)}) copy-start(bf16[1024,1024]{1,0:T(8,128)(2,1)} %cent_ref.5) | copy-start | bytes 6291460
  67.4 0.7 copy-start.4
  73.1 3.7 %collective-permute-start.14 = (f32[8,128]{1,0:T(8,128)S(1)}, f32[8,128]{1,0:T(8,128)S(1)}, u32[]{:S(2)}, u32[]{:S(2)}) collective-permute-start(f32[8,128]{1,0:T(8,128)S(1)} %get-tuple-element.70), channel_id=1, source_target_pairs={{0,2},{1,3},{2,0},{3,1},{4,6},{5,7},{6,4},{7,5},{8,10},{9,11},{10,... | collective-permute-start | bytes 12296 | tf_op jit(solution)/shard_map/ppermute | solution.py:469
  76.8 10.6 %collective-permute-start.15 = (f32[8,128]{1,0:T(8,128)S(1)}, f32[8,128]{1,0:T(8,128)S(1)}, u32[]{:S(2)}, u32[]{:S(2)}) collective-permute-start(f32[8,128]{1,0:T(8,128)S(1)} %pad_maximum_fusion.2), channel_id=1, source_target_pairs={{0,1},{1,0},{2,3},{3,2},{4,5},{5,4},{6,7},{7,6},{8,9},{9,8},{10,11... | collective-permute-start | bytes 12296 | tf_op jit(solution)/shard_map/ppermute | solution.py:469
  76.9 6.7 %collective-permute-start.20 = (f32[1,128]{1,0:T(1,128)S(1)}, f32[1,128]{1,0:T(1,128)S(1)}, u32[]{:S(2)}, u32[]{:S(2)}) collective-permute-start(f32[1,128]{1,0:T(1,128)S(1)} %get-tuple-element.76), channel_id=1, source_target_pairs={{0,8},{1,9},{2,10},{3,11},{4,12},{5,13},{6,14},{7,15},{8,0},{9,1},... | collective-permute-start | bytes 1544 | tf_op jit(solution)/shard_map/ppermute | solution.py:469
  82.1 5.3 %collective-permute-start.19 = (f32[1,128]{1,0:T(1,128)S(1)}, f32[1,128]{1,0:T(1,128)S(1)}, u32[]{:S(2)}, u32[]{:S(2)}) collective-permute-start(f32[1,128]{1,0:T(1,128)S(1)} %get-tuple-element.77), channel_id=1, source_target_pairs={{0,12},{1,13},{2,14},{3,15},{4,8},{5,9},{6,10},{7,11},{8,4},{9,5},... | collective-permute-start | bytes 1544 | tf_op jit(solution)/shard_map/ppermute | solution.py:469
  83.5 3.9 %collective-permute-start.18 = (f32[1,128]{1,0:T(1,128)S(1)}, f32[1,128]{1,0:T(1,128)S(1)}, u32[]{:S(2)}, u32[]{:S(2)}) collective-permute-start(f32[1,128]{1,0:T(1,128)S(1)} %get-tuple-element.78), channel_id=1, source_target_pairs={{0,4},{1,5},{2,6},{3,7},{4,0},{5,1},{6,2},{7,3},{8,12},{9,13},{10,... | collective-permute-start | bytes 1544 | tf_op jit(solution)/shard_map/ppermute | solution.py:469
where the time goes:
time: 88.8 us; the launch traced here: 88.5 us
  starting transfers between devices  30.1 us (34%)
  Pallas kernels  29.1 us (33%)
  waiting for transfers between devices  27.5 us (31%)
    ppermute x21, starting transfers between devices, exchange(): return lax.ppermute(value, 'shard', [(i, i ^ apart) for i in sources])  30.1 us
    pallas_call x12, Pallas kernels, run(): pl.pallas_call(kernel, out_shape=outs, in_specs=specs, scratch_shapes=lis...  29.1 us
    ppermute x21, waiting for transfers between devices, exchange(): return lax.ppermute(value, 'shard', [(i, i ^ apart) for i in sources])  27.5 us
  transfers between devices with their start and end apart: 21, of which 10 were waited for; matrix products, arithmetic and copies ran while one was open for 0% of the time, Pallas kernels for 32%

commit v1 on v0

--- a/solution.py
+++ b/solution.py
@@ -260,7 +260,7 @@
     units[1 - first] = unit_wide(near[...].astype(jnp.float32))
 
 
-def share_kernel(mine_any, other_any, unit_old, scaled, facts, share_low, share_high, mine_ref, other_ref, sems):
+def share_kernel(mine_any, other_any, unit_old, scaled, facts, share0, share1, share2, share3, mine_ref, other_ref, sems):
     copies = fetch(((mine_any, mine_ref), (other_any, other_ref)), sems)
     me, z, y, core = position()
     half = mine_ref.shape[0]
@@ -289,8 +289,8 @@
     block = sum((spot >= piece * step).astype(jnp.int32) for step in range(1, 16))
     together = jnp.where(spot - block * piece == lax.broadcasted_iota(jnp.int32, (count, 128), 1), 1.0, 0.0)
     share = jnp.dot(apart, together, precision=lax.Precision.HIGHEST, preferred_element_type=jnp.float32)
-    share_low[...] = share[0:8, :]
-    share_high[...] = share[8:16, :]
+    for k, out in enumerate((share0, share1, share2, share3)):
+        out[...] = jnp.concatenate([share[4 * g + k : 4 * g + k + 1, :] for g in range(4)], axis=0)
 
 
 def update_kernel(after, scaled, facts, cent_ref, prior_ref, fresh_rows, fresh_counts):
@@ -378,7 +378,7 @@
 
 
 def late_kernel(
-    cap, per, scaled, facts_in, any0, any1, any2, any3, after, updated, packed, floors, rows0, rows1, rows2, rows3, sems
+    cap, per, scaled, facts_in, any0, any1, any2, any3, after, packed, floors, rows0, rows1, rows2, rows3, sems
 ):
     me, z, y, core = position()
     part = per * cap
@@ -390,7 +390,9 @@
     redo(cap, per, scaled, facts_in, me, refs, (3 * part, 3 * part, 0, 0), packed, floors)
 
 
-def third_kernel(cap, per, early, floors, kept_any, last_any, far_any, inside, across, kept, two, sems):
+def third_kernel(
+    cap, per, early, floors, share0, share1, share2, share3, kept_any, last_any, far_any, inside, across, kept, two, sems
+):
     me, z, y, core = position()
     end = (z == 0) | (z == 3)
     at_end = pltpu.make_async_copy(far_any, two, sems.at[1])
@@ -407,6 +409,9 @@
     together = jnp.concatenate(lines + [jnp.zeros((16 - 4 * per, 4 * cap), jnp.float32)], axis=0)
     lane = lax.broadcasted_iota(jnp.int32, together.shape, 1)
     line = lax.broadcasted_iota(jnp.int32, together.shape, 0)
+    share = share0[...] + share1[...] + share2[...] + share3[...]
+    for r, g in enumerate((0, 2, 1, 3)):
+        (inside, across)[r // 2][8 + r % 2 : 9 + r % 2, :] = share[g : g + 1, :]
     for r in range(4):
         out, start = (inside, across)[r // 2], 4 * (r % 2)
         spread = jnp.zeros_like(together)
@@ -417,8 +422,8 @@
             out[start + t : start + t + 1, :] = jnp.sum(spread[4 * t : 4 * t + 4], axis=0, keepdims=True)
 
 
-def last_kernel(cap, scale_one, scale_two, info, inside, across, beside, share0, share1, share2, share3, density, level_two):
-    total = share0[...] + share1[...] + share2[...] + share3[...]
+def last_kernel(cap, scale_one, scale_two, info, inside, across, beside, density, level_two):
+    total = inside[8:9, :] + across[8:9, :] + beside[8:9, :]
     density[...] = jnp.log(total[:, 0 : density.shape[1]] / scale_one)
     values = jnp.concatenate([inside[0:4, :], beside[0:4, :], across[0:4, :], beside[4:8, :]], axis=0)
     rows = info.shape[1]
@@ -519,19 +524,17 @@
     far_set = exchange(last_set, 4, mids)
     other = exchange(mine, 1)
     gathered = pltpu.VMEM((8 * emb_rows, width + 128), bf16)
-    scaled, facts, share, share_high = call(
+    scaled, facts, *share = call(
         share_kernel,
         (
             shape((16 * emb_rows, width), bf16),
             shape((16, 16 * emb_rows), i32),
-            shape((8, 4 * cap), f32),
-            shape((8, 4 * cap), f32),
+            *[shape((4, 4 * cap), f32)] * 4,
         ),
         [gathered, gathered, pltpu.SemaphoreType.DMA((2,))],
         in_specs=[ANY, ANY, VMEM],
     )(mine, other, unit_old)
-    share = share + exchange(share_high, 1)
-    share = share[0:4] + exchange(share[4:8], 2)
+    share = [share[0], exchange(share[1], 4), exchange(share[2], 12), share[3]]
     early = call(
         functools.partial(early_kernel, cap, per),
         shape((24, 4 * cap), f32),
@@ -546,29 +549,30 @@
         ],
         in_specs=[VMEM, VMEM] + [ANY] * 7,
     )(scaled, facts, units, cross_set, passed, rows0, rows1, early2, early3)
-    new_centroids, counts = call(
-        update_kernel, (shape((rows, width), bf16), shape((1, rows), i32)), in_specs=[ANY] + [VMEM] * 4
-    )(early, scaled, facts, centroids, prior_row)
+    share[3], early = in_order(share[3], early)
+    share[3] = exchange(share[3], 8)
     kept = shape((1, per, 4 * cap, width), bf16)
     kept_rows, floors = call(
         functools.partial(late_kernel, cap, per),
         (kept, shape((1, per, 4 * cap, 128), bf16)),
         [room(rows_of(1))] * 4 + [pltpu.SemaphoreType.DMA((4,))],
-        in_specs=[VMEM] * 2 + [ANY] * 6,
-    )(scaled, facts, rows0, rows1, late2, late3, early, counts)
-    tile = shape((8, 4 * cap), f32)
+        in_specs=[VMEM] * 2 + [ANY] * 5,
+    )(scaled, facts, rows0, rows1, late2, late3, early)
+    tile = shape((16, 4 * cap), f32)
     inside, across = call(
         functools.partial(third_kernel, cap, per),
         (tile,) * 2,
         [room(kept), block_set, pltpu.SemaphoreType.DMA((2,))],
-        in_specs=[VMEM, VMEM] + [ANY] * 3,
-    )(early, floors, kept_rows, last_set, far_set)
+        in_specs=[VMEM] * 6 + [ANY] * 3,
+    )(early, floors, *share, kept_rows, last_set, far_set)
+    new_centroids, counts = call(
+        update_kernel, (shape((rows, width), bf16), shape((1, rows), i32)), in_specs=[ANY] + [VMEM] * 4
+    )(inside, scaled, facts, centroids, prior_row)
     across = exchange(across, 2)
-    beside = exchange(jnp.concatenate([inside[4:8], across[4:8]], axis=0), 1)
-    share = [share[0:1]] + [exchange(share[i : i + 1], apart) for i, apart in ((1, 4), (2, 12), (3, 8))]
+    beside = exchange(jnp.concatenate([inside[4:8], across[4:8], inside[9:10] + across[9:10]], axis=0), 1)
     density, level_two = call(
         functools.partial(last_kernel, cap, probe_count * BLOCK, BLOCK2), (shape((1, emb_rows), f32), shape((1, rows), f32))
-    )(info, inside, across, beside, *share)
+    )(info, inside, across, beside)
     return (density.reshape(-1), new_centroids, counts.reshape(-1), level_two.reshape(-1))
 
 

time: 88.8 us -> 83.6 us (0.941)
  waiting for transfers between devices: 27.5 us -> 24.8 us
  starting transfers between devices: 30.1 us -> 29.1 us
    ppermute x21 -> x19, waiting for transfers between devices: 27.5 us -> 24.8 us  [exchange(): return lax.ppermute(value, 'shard', [(i, i ^ apart) for i in sources])]
    ppermute x21 -> x19, starting transfers between devices: 30.1 us -> 29.1 us  [exchange(): return lax.ppermute(value, 'shard', [(i, i ^ apart) for i in sources])]
    pallas_call x12 -> x13, Pallas kernels: 29.1 us -> 28.3 us  [run(): pl.pallas_call(kernel, out_shape=outs, in_specs=specs, scratch_shapes=lis...]
  transfers between devices with their start and end apart: 21 -> 19, of which waited for: 10 -> 8; matrix products, arithmetic and copies ran while one was open for 0% -> 0% of each run, Pallas kernels for 32% -> 30%
where the time goes in v1:
time: 83.6 us; the launch traced here: 83.2 us
  starting transfers between devices  29.1 us (35%)
  Pallas kernels  28.3 us (34%)
  waiting for transfers between devices  24.8 us (30%)
  between operations  0.87 us (1%)
    ppermute x19, starting transfers between devices, exchange(): return lax.ppermute(value, 'shard', [(i, i ^ apart) for i in sources])  29.1 us
    pallas_call x13, Pallas kernels, run(): pl.pallas_call(kernel, out_shape=outs, in_specs=specs, scratch_shapes=lis...  28.3 us
    ppermute x19, waiting for transfers between devices, exchange(): return lax.ppermute(value, 'shard', [(i, i ^ apart) for i in sources])  24.8 us
  transfers between devices with their start and end apart: 19, of which 8 were waited for; matrix products, arithmetic and copies ran while one was open for 0% of the time, Pallas kernels for 30%

profile of v1, /device:TPU:0, one launch (start us, length us, event | category | flops | bytes accessed | tf_op | source)
XLA Modules:
  0.0 83.2 jit_solution(12133722250339831024)
XLA Ops:
  0.6 0.0 copy-start
  0.6 0.0 copy-start.3
  0.7 3.1 %collective-permute-start = (bf16[384,1024]{1,0:T(8,128)(2,1)}, bf16[384,1024]{1,0:T(8,128)(2,1)S(1)}, u32[]{:S(2)}, u32[]{:S(2)}) collective-permute-start(bf16[384,1024]{1,0:T(8,128)(2,1)} %own_any.1), channel_id=1, source_target_pairs={{0,4},{1,5},{2,6},{3,7},{4,0},{5,1},{6,2},{7,3},{8,12},{9,13},{10,... | collective-permute-start | bytes 2359304 | tf_op jit(solution)/shard_map/ppermute | solution.py:474
  3.7 0.7 collective-permute-start.1
  4.5 3.4 %shard_map.102 = (bf16[40,1152]{1,0:T(8,128)(2,1)S(1)}, bf16[304,1024]{1,0:T(8,128)(2,1)S(1)}, bf16[304,1024]{1,0:T(8,128)(2,1)S(1)}, s32[8,1024]{1,0:T(8,128)S(1)}) custom-call(s32[1,1024]{1,0:T(1,128)} %bitcast.10, bf16[40,1024]{1,0:T(8,128)(2,1)} %emb_any.1, s32[8,40]{1,0:T(8,128)} %bitcast.11, s32[1,40]{1,0:T(1,128)} %bitcast.12, s32[1,1024]{1,0:T(1,128)} %bitcast.7, ...), custom_call_target="tpu_custom_call" | custom-call | tf_op jit(solution)/shard_map/pallas_call | solution.py:440
  7.8 4.4 %collective-permute-start.2 = (bf16[40,1152]{1,0:T(8,128)(2,1)S(1)}, bf16[40,1152]{1,0:T(8,128)(2,1)S(1)}, u32[]{:S(2)}, u32[]{:S(2)}) collective-permute-start(bf16[40,1152]{1,0:T(8,128)(2,1)S(1)} %get-tuple-element.45), channel_id=1, source_target_pairs={{0,4},{1,5},{2,6},{3,7},{4,0},{5,1},{6,2},{7,3},{8,12},{9,13},{10,... | collective-permute-start | bytes 276488 | tf_op jit(solution)/shard_map/ppermute | solution.py:474
  12.3 1.5 %collective-permute-start.4 = (bf16[304,1024]{1,0:T(8,128)(2,1)S(1)}, bf16[304,1024]{1,0:T(8,128)(2,1)S(1)}, u32[]{:S(2)}, u32[]{:S(2)}) collective-permute-start(bf16[304,1024]{1,0:T(8,128)(2,1)S(1)} %get-tuple-element.48), channel_id=1, source_target_pairs={{0,2},{1,3},{2,0},{3,1},{4,6},{5,7},{6,4},{7,5},{8,10},{9,11},{10,... | collective-permute-start | bytes 1867784 | tf_op jit(solution)/shard_map/ppermute | solution.py:474
  13.8 0.0 collective-permute-start.5
  13.8 0.0 copy-done
  13.8 0.0 copy-done.3
  13.8 2.9 %shard_map.103 = (bf16[400,1024]{1,0:T(8,128)(2,1)S(1)}, bf16[400,1024]{1,0:T(8,128)(2,1)S(1)}, bf16[112,1024]{1,0:T(8,128)(2,1)S(1)}, bf16[112,1024]{1,0:T(8,128)(2,1)S(1)}) custom-call(s32[8,1024]{1,0:T(8,128)S(1)} %get-tuple-element.44.info, s32[1,1024]{1,0:T(1,128)S(1)} %bitcast.8, bf16[1024,1024]{1,0:T(8,128)(2,1)S(1)} %copy-done), custom_call_target="tpu_custom_call" | custom-call | tf_op jit(solution)/shard_map/pallas_call | solution.py:440
  16.7 6.7 %collective-permute-done.2 = bf16[40,1152]{1,0:T(8,128)(2,1)S(1)} collective-permute-done((bf16[40,1152]{1,0:T(8,128)(2,1)S(1)}, bf16[40,1152]{1,0:T(8,128)(2,1)S(1)}, u32[]{:S(2)}, u32[]{:S(2)}) %collective-permute-start.2) | collective-permute-done | bytes 92192 | tf_op jit(solution)/shard_map/ppermute | solution.py:474
  23.5 0.0 collective-permute-done.refs_0_
  23.5 0.0 collective-permute-done.1.refs_1_
  23.5 3.8 %collective-permute-start.3 = (bf16[80,1152]{1,0:T(8,128)(2,1)S(1)}, bf16[80,1152]{1,0:T(8,128)(2,1)S(1)}, u32[]{:S(2)}, u32[]{:S(2)}) collective-permute-start(bf16[80,1152]{1,0:T(8,128)(2,1)S(1)} %get-tuple-element.47), channel_id=1, source_target_pairs={{0,12},{1,13},{2,14},{3,15},{4,8},{5,9},{6,10},{7,11},{8,4},{9,5},... | collective-permute-start | bytes 552968 | tf_op jit(solution)/shard_map/ppermute | solution.py:474
  27.4 1.3 %collective-permute-start.8 = (bf16[384,1024]{1,0:T(8,128)(2,1)S(1)}, bf16[384,1024]{1,0:T(8,128)(2,1)S(1)}, u32[]{:S(2)}, u32[]{:S(2)}) collective-permute-start(bf16[384,1024]{1,0:T(8,128)(2,1)S(1)} %get-tuple-element.54.cross_any), channel_id=1, source_target_pairs={{4,0},{5,1},{6,2},{7,3},{8,12},{9,13},{10,14},{11,15},{20,16},{21,... | collective-permute-start | bytes 2359304 | tf_op jit(solution)/shard_map/ppermute | solution.py:474
  28.6 0.7 collective-permute-start.9
  29.4 2.0 %collective-permute-done.3 = bf16[80,1152]{1,0:T(8,128)(2,1)S(1)} collective-permute-done((bf16[80,1152]{1,0:T(8,128)(2,1)S(1)}, bf16[80,1152]{1,0:T(8,128)(2,1)S(1)}, u32[]{:S(2)}, u32[]{:S(2)}) %collective-permute-start.3) | collective-permute-done | bytes 184352 | tf_op jit(solution)/shard_map/ppermute | solution.py:474
  31.4 0.0 collective-permute-done.4.refs_1_
  31.4 8.1 %collective-permute-done.5.refs_2_ = bf16[304,1024]{1,0:T(8,128)(2,1)S(1)} collective-permute-done((bf16[304,1024]{1,0:T(8,128)(2,1)S(1)}, bf16[304,1024]{1,0:T(8,128)(2,1)S(1)}, u32[]{:S(2)}, u32[]{:S(2)}) %collective-permute-start.5) | collective-permute-done | bytes 622624 | tf_op jit(solution)/shard_map/ppermute | solution.py:474
  39.6 0.5 collective-permute-start.6
  40.1 3.2 %shard_map.106 = (bf16[1024,1024]{1,0:T(8,128)(2,1)S(1)}, bf16[2,384,1024]{2,1,0:T(8,128)(2,1)S(1)}) custom-call(bf16[1024,1024]{1,0:T(8,128)(2,1)} %cent_ref.5, bf16[384,1024]{1,0:T(8,128)(2,1)} %own_any.1, bf16[384,1024]{1,0:T(8,128)(2,1)S(1)} %get-tuple-element.55.near_any), custom_call_target="tpu_custom_call" | custom-call | tf_op jit(solution)/shard_map/pallas_call | solution.py:440
  43.3 1.9 %collective-permute-start.10 = (bf16[400,1024]{1,0:T(8,128)(2,1)S(1)}, bf16[400,1024]{1,0:T(8,128)(2,1)S(1)}, u32[]{:S(2)}, u32[]{:S(2)}) collective-permute-start(bf16[400,1024]{1,0:T(8,128)(2,1)S(1)} %get-tuple-element.65), channel_id=1, source_target_pairs={{0,1},{1,0},{2,3},{3,2},{4,5},{5,4},{6,7},{7,6},{8,9},{9,8},{10,11... | collective-permute-start | bytes 2457608 | tf_op jit(solution)/shard_map/ppermute | solution.py:474
  45.2 2.9 %collective-permute-done.8.refs_0_ = bf16[384,1024]{1,0:T(8,128)(2,1)S(1)} collective-permute-done((bf16[384,1024]{1,0:T(8,128)(2,1)S(1)}, bf16[384,1024]{1,0:T(8,128)(2,1)S(1)}, u32[]{:S(2)}, u32[]{:S(2)}) %collective-permute-start.8) | collective-permute-done | bytes 786464 | tf_op jit(solution)/shard_map/ppermute | solution.py:474
  48.2 0.0 collective-permute-done.9.refs_1_
  48.2 0.0 copy-start.2
  48.2 1.3 %collective-permute-start.16 = (bf16[384,1024]{1,0:T(8,128)(2,1)S(1)}, bf16[384,1024]{1,0:T(8,128)(2,1)}, u32[]{:S(2)}, u32[]{:S(2)}) collective-permute-start(bf16[384,1024]{1,0:T(8,128)(2,1)S(1)} %get-tuple-element.77.last_any), channel_id=1, source_target_pairs={{4,0},{5,1},{6,2},{7,3},{8,12},{9,13},{10,14},{11,15},{20,16},{21,... | collective-permute-start | bytes 2359304 | tf_op jit(solution)/shard_map/ppermute | solution.py:474
  49.5 1.5 %collective-permute-done.6 = bf16[160,1152]{1,0:T(8,128)(2,1)S(1)} collective-permute-done((bf16[160,1152]{1,0:T(8,128)(2,1)S(1)}, bf16[160,1152]{1,0:T(8,128)(2,1)S(1)}, u32[]{:S(2)}, u32[]{:S(2)}) %collective-permute-start.6) | collective-permute-done | bytes 368672 | tf_op jit(solution)/shard_map/ppermute | solution.py:474
  51.0 0.2 collective-permute-start.7
  51.1 0.3 collective-permute-start.11
  51.5 1.4 %collective-permute-start.12 = (bf16[112,1024]{1,0:T(8,128)(2,1)S(1)}, bf16[112,1024]{1,0:T(8,128)(2,1)S(1)}, u32[]{:S(2)}, u32[]{:S(2)}) collective-permute-start(bf16[112,1024]{1,0:T(8,128)(2,1)S(1)} %get-tuple-element.70), channel_id=1, source_target_pairs={{0,3},{1,2},{2,1},{3,0},{4,7},{5,6},{6,5},{7,4},{8,11},{9,10},{10,... | collective-permute-start | bytes 688136 | tf_op jit(solution)/shard_map/ppermute | solution.py:474
  52.9 0.4 collective-permute-done.7.other_any
  53.2 3.1 %shard_map.108 = (bf16[640,1024]{1,0:T(8,128)(2,1)S(1)}, s32[16,640]{1,0:T(8,128)S(1)}, f32[4,128]{1,0:T(4,128)S(1)}, f32[4,128]{1,0:T(4,128)S(1)}, f32[4,128]{1,0:T(4,128)S(1)}, /*index=5*/f32[4,128]{1,0:T(4,128)S(1)}) custom-call(bf16[320,1152]{1,0:T(8,128)(2,1)S(1)} %constant_dynamic-update-slice_fusion.mine_any, ...), custom_call_target="tpu_custom_call" | custom-call | tf_op jit(solution)/shard_map/pallas_call | solution.py:440
  56.4 0.0 copy-done.2
  56.4 0.0 collective-permute-done.10.any1
  56.4 6.0 %shard_map.109.refs_1_ = f32[24,128]{1,0:T(8,128)S(1)} custom-call(bf16[640,1024]{1,0:T(8,128)(2,1)S(1)} %get-tuple-element.60.scaled, s32[16,640]{1,0:T(8,128)S(1)} %get-tuple-element.61.facts_in.facts, bf16[2,384,1024]{2,1,0:T(8,128)(2,1)} %copy-done.2, bf16[384,1024]{1,0:T(8,128)(2,1)S(1)} %get-tuple-element.54.cross_any, ...), custom_call_target="tpu_custom_call" | custom-call | tf_op jit(solution)/shard_map/pallas_call | solution.py:440
  62.4 4.8 %collective-permute-start.15 = (f32[4,128]{1,0:T(4,128)S(1)}, f32[4,128]{1,0:T(4,128)S(1)}, u32[]{:S(2)}, u32[]{:S(2)}) collective-permute-start(f32[4,128]{1,0:T(4,128)S(1)} %get-tuple-element.75), channel_id=1, source_target_pairs={{0,8},{1,9},{2,10},{3,11},{4,12},{5,13},{6,14},{7,15},{8,0},{9,1},... | collective-permute-start | bytes 6152 | tf_op jit(solution)/shard_map/ppermute | solution.py:474
  67.1 0.0 collective-permute-start.13
  67.1 0.0 collective-permute-done.11.any2
  67.1 1.5 %collective-permute-start.14 = (f32[4,128]{1,0:T(4,128)S(1)}, f32[4,128]{1,0:T(4,128)S(1)}, u32[]{:S(2)}, u32[]{:S(2)}) collective-permute-start(f32[4,128]{1,0:T(4,128)S(1)} %get-tuple-element.74), channel_id=1, source_target_pairs={{0,12},{1,13},{2,14},{3,15},{4,8},{5,9},{6,10},{7,11},{8,4},{9,5},... | collective-permute-start | bytes 6152 | tf_op jit(solution)/shard_map/ppermute | solution.py:474
  68.7 0.0 collective-permute-done.12.any3
  68.7 2.8 %shard_map.111 = (bf16[1,3,128,1024]{3,2,1,0:T(8,128)(2,1)S(1)}, bf16[1,3,128,128]{3,2,1,0:T(8,128)(2,1)S(1)}) custom-call(bf16[640,1024]{1,0:T(8,128)(2,1)S(1)} %get-tuple-element.60.scaled, s32[16,640]{1,0:T(8,128)S(1)} %get-tuple-element.61.facts_in.facts, bf16[400,1024]{1,0:T(8,128)(2,1)S(1)} %get-tuple-element.64.any0, ...), custom_call_target="tpu_custom_call" | custom-call | tf_op jit(solution)/shard_map/pallas_call | solution.py:440
  71.5 0.0 copy-start.1
  71.5 0.0 collective-permute-done.15.share3
  71.5 0.0 collective-permute-done.13.share1
  71.5 1.0 %collective-permute-done.14.share2 = f32[4,128]{1,0:T(4,128)S(1)} collective-permute-done((f32[4,128]{1,0:T(4,128)S(1)}, f32[4,128]{1,0:T(4,128)S(1)}, u32[]{:S(2)}, u32[]{:S(2)}) %collective-permute-start.14) | collective-permute-done | bytes 2080 | tf_op jit(solution)/shard_map/ppermute | solution.py:474
  72.5 0.0 collective-permute-done.16.far_any
  72.5 2.2 %shard_map.112 = (f32[16,128]{1,0:T(8,128)S(1)}, f32[16,128]{1,0:T(8,128)S(1)}) custom-call(f32[24,128]{1,0:T(8,128)S(1)} %get-tuple-element.68.after.early, bf16[1,3,128,128]{3,2,1,0:T(8,128)(2,1)S(1)} %get-tuple-element.71.floors, f32[4,128]{1,0:T(4,128)S(1)} %get-tuple-element.72.share0, f32[4,128]{1,0:T(4,128)S(1)} %collective-permute-done.13.share1, ...), custom_call_target="tpu_custom_call" | custom-call | tf_op jit(solution)/shard_map/pallas_call | solution.py:440
  74.7 1.6 %collective-permute-start.17 = (f32[16,128]{1,0:T(8,128)S(1)}, f32[16,128]{1,0:T(8,128)S(1)}, u32[]{:S(2)}, u32[]{:S(2)}) collective-permute-start(f32[16,128]{1,0:T(8,128)S(1)} %get-tuple-element.79), channel_id=1, source_target_pairs={{0,2},{1,3},{2,0},{3,1},{4,6},{5,7},{6,4},{7,5},{8,10},{9,11},{10,... | collective-permute-start | bytes 24584 | tf_op jit(solution)/shard_map/ppermute | solution.py:474
  76.3 2.1 %collective-permute-done.17.across = f32[16,128]{1,0:T(8,128)S(1)} collective-permute-done((f32[16,128]{1,0:T(8,128)S(1)}, f32[16,128]{1,0:T(8,128)S(1)}, u32[]{:S(2)}, u32[]{:S(2)}) %collective-permute-start.17) | collective-permute-done | bytes 8224 | tf_op jit(solution)/shard_map/ppermute | solution.py:474
  78.4 0.1 collective-permute-start.18
  78.5 0.0 copy-done.1
  78.5 3.7 %shard_map.114 = (bf16[1024,1024]{1,0:T(8,128)(2,1)}, s32[1,1024]{1,0:T(1,128)}) custom-call(f32[16,128]{1,0:T(8,128)S(1)} %get-tuple-element.78.inside.after, bf16[640,1024]{1,0:T(8,128)(2,1)S(1)} %get-tuple-element.60.scaled, s32[16,640]{1,0:T(8,128)S(1)} %get-tuple-element.61.facts_in.facts, bf16[1024,1024]{1,0:T(8,128)(2,1)S(1)} %copy-done.1, ...), custom_call_target="tpu_custom_call" | custom-call | tf_op jit(solution)/shard_map/pallas_call | solution.py:440
  82.2 0.0 collective-permute-done.18.beside
  82.2 1.0 %shard_map.113 = (f32[1,40]{1,0:T(1,128)}, f32[1,1024]{1,0:T(1,128)}) custom-call(s32[8,1024]{1,0:T(8,128)S(1)} %get-tuple-element.44.info, f32[16,128]{1,0:T(8,128)S(1)} %get-tuple-element.78.inside.after, f32[16,128]{1,0:T(8,128)S(1)} %collective-permute-done.17.across, f32[9,128]{1,0:T(8,128)S(1)} %collective-permute-done.18.beside), custom_call_target="tpu_custom_call" | custom-call | tf_op jit(solution)/shard_map/pallas_call | solution.py:440
  (12 shorter events, 0.1 us)
Async XLA Ops:
  0.6 13.1 %copy-start = (bf16[1024,1024]{1,0:T(8,128)(2,1)S(1)}, bf16[1024,1024]{1,0:T(8,128)(2,1)}, u32[]{:S(2)}) copy-start(bf16[1024,1024]{1,0:T(8,128)(2,1)} %cent_ref.5) | copy-start | bytes 6291460
  0.6 13.1 %copy-start.3 = (s32[1024]{0:T(1024)S(1)}, s32[1024]{0:T(1024)}, u32[]{:S(2)}) copy-start(s32[1024]{0:T(1024)} %param.10) | copy-start | bytes 12292
  0.7 22.8 %collective-permute-start = (bf16[384,1024]{1,0:T(8,128)(2,1)}, bf16[384,1024]{1,0:T(8,128)(2,1)S(1)}, u32[]{:S(2)}, u32[]{:S(2)}) collective-permute-start(bf16[384,1024]{1,0:T(8,128)(2,1)} %own_any.1), channel_id=1, source_target_pairs={{0,4},{1,5},{2,6},{3,7},{4,0},{5,1},{6,2},{7,3},{8,12},{9,13},{10,... | collective-permute-start | bytes 2359304 | tf_op jit(solution)/shard_map/ppermute | solution.py:474
  3.7 19.8 %collective-permute-start.1 = (bf16[384,1024]{1,0:T(8,128)(2,1)}, bf16[384,1024]{1,0:T(8,128)(2,1)S(1)}, u32[]{:S(2)}, u32[]{:S(2)}) collective-permute-start(bf16[384,1024]{1,0:T(8,128)(2,1)} %own_any.1), channel_id=1, source_target_pairs={{4,8},{5,9},{6,10},{7,11},{8,4},{9,5},{10,6},{11,7},{20,24},{21,25... | collective-permute-start | bytes 2359304 | tf_op jit(solution)/shard_map/ppermute | solution.py:474
  7.8 15.6 %collective-permute-start.2 = (bf16[40,1152]{1,0:T(8,128)(2,1)S(1)}, bf16[40,1152]{1,0:T(8,128)(2,1)S(1)}, u32[]{:S(2)}, u32[]{:S(2)}) collective-permute-start(bf16[40,1152]{1,0:T(8,128)(2,1)S(1)} %get-tuple-element.45), channel_id=1, source_target_pairs={{0,4},{1,5},{2,6},{3,7},{4,0},{5,1},{6,2},{7,3},{8,12},{9,13},{10,... | collective-permute-start | bytes 276488 | tf_op jit(solution)/shard_map/ppermute | solution.py:474
  12.3 19.2 %collective-permute-start.4 = (bf16[304,1024]{1,0:T(8,128)(2,1)S(1)}, bf16[304,1024]{1,0:T(8,128)(2,1)S(1)}, u32[]{:S(2)}, u32[]{:S(2)}) collective-permute-start(bf16[304,1024]{1,0:T(8,128)(2,1)S(1)} %get-tuple-element.48), channel_id=1, source_target_pairs={{0,2},{1,3},{2,0},{3,1},{4,6},{5,7},{6,4},{7,5},{8,10},{9,11},{10,... | collective-permute-start | bytes 1867784 | tf_op jit(solution)/shard_map/ppermute | solution.py:474
  13.8 25.8 %collective-permute-start.5 = (bf16[304,1024]{1,0:T(8,128)(2,1)S(1)}, bf16[304,1024]{1,0:T(8,128)(2,1)S(1)}, u32[]{:S(2)}, u32[]{:S(2)}) collective-permute-start(bf16[304,1024]{1,0:T(8,128)(2,1)S(1)} %get-tuple-element.49), channel_id=1, source_target_pairs={{0,3},{1,2},{2,1},{3,0},{4,7},{5,6},{6,5},{7,4},{8,11},{9,10},{10,... | collective-permute-start | bytes 1867784 | tf_op jit(solution)/shard_map/ppermute | solution.py:474
  23.5 7.9 %collective-permute-start.3 = (bf16[80,1152]{1,0:T(8,128)(2,1)S(1)}, bf16[80,1152]{1,0:T(8,128)(2,1)S(1)}, u32[]{:S(2)}, u32[]{:S(2)}) collective-permute-start(bf16[80,1152]{1,0:T(8,128)(2,1)S(1)} %get-tuple-element.47), channel_id=1, source_target_pairs={{0,12},{1,13},{2,14},{3,15},{4,8},{5,9},{6,10},{7,11},{8,4},{9,5},... | collective-permute-start | bytes 552968 | tf_op jit(solution)/shard_map/ppermute | solution.py:474
  27.4 20.8 %collective-permute-start.8 = (bf16[384,1024]{1,0:T(8,128)(2,1)S(1)}, bf16[384,1024]{1,0:T(8,128)(2,1)S(1)}, u32[]{:S(2)}, u32[]{:S(2)}) collective-permute-start(bf16[384,1024]{1,0:T(8,128)(2,1)S(1)} %get-tuple-element.54.cross_any), channel_id=1, source_target_pairs={{4,0},{5,1},{6,2},{7,3},{8,12},{9,13},{10,14},{11,15},{20,16},{21,... | collective-permute-start | bytes 2359304 | tf_op jit(solution)/shard_map/ppermute | solution.py:474
  28.6 19.5 %collective-permute-start.9 = (bf16[384,1024]{1,0:T(8,128)(2,1)S(1)}, bf16[384,1024]{1,0:T(8,128)(2,1)S(1)}, u32[]{:S(2)}, u32[]{:S(2)}) collective-permute-start(bf16[384,1024]{1,0:T(8,128)(2,1)S(1)} %get-tuple-element.55.near_any), channel_id=1, source_target_pairs={{4,8},{5,9},{6,10},{7,11},{8,4},{9,5},{10,6},{11,7},{20,24},{21,25... | collective-permute-start | bytes 2359304 | tf_op jit(solution)/shard_map/ppermute | solution.py:474
  39.6 11.4 %collective-permute-start.6 = (bf16[160,1152]{1,0:T(8,128)(2,1)S(1)}, bf16[160,1152]{1,0:T(8,128)(2,1)S(1)}, u32[]{:S(2)}, u32[]{:S(2)}) collective-permute-start(bf16[160,1152]{1,0:T(8,128)(2,1)S(1)} %get-tuple-element.53), channel_id=1, source_target_pairs={{0,2},{1,3},{2,0},{3,1},{4,6},{5,7},{6,4},{7,5},{8,10},{9,11},{10,... | collective-permute-start | bytes 1105928 | tf_op jit(solution)/shard_map/ppermute | solution.py:474
  43.3 13.1 %collective-permute-start.10 = (bf16[400,1024]{1,0:T(8,128)(2,1)S(1)}, bf16[400,1024]{1,0:T(8,128)(2,1)S(1)}, u32[]{:S(2)}, u32[]{:S(2)}) collective-permute-start(bf16[400,1024]{1,0:T(8,128)(2,1)S(1)} %get-tuple-element.65), channel_id=1, source_target_pairs={{0,1},{1,0},{2,3},{3,2},{4,5},{5,4},{6,7},{7,6},{8,9},{9,8},{10,11... | collective-permute-start | bytes 2457608 | tf_op jit(solution)/shard_map/ppermute | solution.py:474
  48.2 8.2 %copy-start.2 = (bf16[2,384,1024]{2,1,0:T(8,128)(2,1)}, bf16[2,384,1024]{2,1,0:T(8,128)(2,1)S(1)}, u32[]{:S(2)}) copy-start(bf16[2,384,1024]{2,1,0:T(8,128)(2,1)S(1)} %get-tuple-element.62.units_any) | copy-start | bytes 4718596
  48.2 24.3 %collective-permute-start.16 = (bf16[384,1024]{1,0:T(8,128)(2,1)S(1)}, bf16[384,1024]{1,0:T(8,128)(2,1)}, u32[]{:S(2)}, u32[]{:S(2)}) collective-permute-start(bf16[384,1024]{1,0:T(8,128)(2,1)S(1)} %get-tuple-element.77.last_any), channel_id=1, source_target_pairs={{4,0},{5,1},{6,2},{7,3},{8,12},{9,13},{10,14},{11,15},{20,16},{21,... | collective-permute-start | bytes 2359304 | tf_op jit(solution)/shard_map/ppermute | solution.py:474
  51.0 2.3 %collective-permute-start.7 = (bf16[320,1152]{1,0:T(8,128)(2,1)S(1)}, bf16[320,1152]{1,0:T(8,128)(2,1)S(1)}, u32[]{:S(2)}, u32[]{:S(2)}) collective-permute-start(bf16[320,1152]{1,0:T(8,128)(2,1)S(1)} %constant_dynamic-update-slice_fusion.mine_any), channel_id=1, source_target_pairs={{0,1},{1,0},{2,3},{3,2},{4,5},{5,4},{6,7},{7,6},{8,9},{9,8},{10,11... | collective-permute-start | bytes 2211848 | tf_op jit(solution)/shard_map/ppermute | solution.py:474
  51.1 16.0 %collective-permute-start.11 = (bf16[112,1024]{1,0:T(8,128)(2,1)S(1)}, bf16[112,1024]{1,0:T(8,128)(2,1)S(1)}, u32[]{:S(2)}, u32[]{:S(2)}) collective-permute-start(bf16[112,1024]{1,0:T(8,128)(2,1)S(1)} %get-tuple-element.69), channel_id=1, source_target_pairs={{0,2},{1,3},{2,0},{3,1},{4,6},{5,7},{6,4},{7,5},{8,10},{9,11},{10,... | collective-permute-start | bytes 688136 | tf_op jit(solution)/shard_map/ppermute | solution.py:474
  51.5 17.2 %collective-permute-start.12 = (bf16[112,1024]{1,0:T(8,128)(2,1)S(1)}, bf16[112,1024]{1,0:T(8,128)(2,1)S(1)}, u32[]{:S(2)}, u32[]{:S(2)}) collective-permute-start(bf16[112,1024]{1,0:T(8,128)(2,1)S(1)} %get-tuple-element.70), channel_id=1, source_target_pairs={{0,3},{1,2},{2,1},{3,0},{4,7},{5,6},{6,5},{7,4},{8,11},{9,10},{10,... | collective-permute-start | bytes 688136 | tf_op jit(solution)/shard_map/ppermute | solution.py:474
  62.4 9.2 %collective-permute-start.15 = (f32[4,128]{1,0:T(4,128)S(1)}, f32[4,128]{1,0:T(4,128)S(1)}, u32[]{:S(2)}, u32[]{:S(2)}) collective-permute-start(f32[4,128]{1,0:T(4,128)S(1)} %get-tuple-element.75), channel_id=1, source_target_pairs={{0,8},{1,9},{2,10},{3,11},{4,12},{5,13},{6,14},{7,15},{8,0},{9,1},... | collective-permute-start | bytes 6152 | tf_op jit(solution)/shard_map/ppermute | solution.py:474
  67.1 4.4 %collective-permute-start.13 = (f32[4,128]{1,0:T(4,128)S(1)}, f32[4,128]{1,0:T(4,128)S(1)}, u32[]{:S(2)}, u32[]{:S(2)}) collective-permute-start(f32[4,128]{1,0:T(4,128)S(1)} %get-tuple-element.73), channel_id=1, source_target_pairs={{0,4},{1,5},{2,6},{3,7},{4,0},{5,1},{6,2},{7,3},{8,12},{9,13},{10,... | collective-permute-start | bytes 6152 | tf_op jit(solution)/shard_map/ppermute | solution.py:474
  67.1 5.4 %collective-permute-start.14 = (f32[4,128]{1,0:T(4,128)S(1)}, f32[4,128]{1,0:T(4,128)S(1)}, u32[]{:S(2)}, u32[]{:S(2)}) collective-permute-start(f32[4,128]{1,0:T(4,128)S(1)} %get-tuple-element.74), channel_id=1, source_target_pairs={{0,12},{1,13},{2,14},{3,15},{4,8},{5,9},{6,10},{7,11},{8,4},{9,5},... | collective-permute-start | bytes 6152 | tf_op jit(solution)/shard_map/ppermute | solution.py:474
  71.5 7.0 %copy-start.1 = (bf16[1024,1024]{1,0:T(8,128)(2,1)S(1)}, bf16[1024,1024]{1,0:T(8,128)(2,1)}, u32[]{:S(2)}) copy-start(bf16[1024,1024]{1,0:T(8,128)(2,1)} %cent_ref.5) | copy-start | bytes 6291460
  74.7 3.7 %collective-permute-start.17 = (f32[16,128]{1,0:T(8,128)S(1)}, f32[16,128]{1,0:T(8,128)S(1)}, u32[]{:S(2)}, u32[]{:S(2)}) collective-permute-start(f32[16,128]{1,0:T(8,128)S(1)} %get-tuple-element.79), channel_id=1, source_target_pairs={{0,2},{1,3},{2,0},{3,1},{4,6},{5,7},{6,4},{7,5},{8,10},{9,11},{10,... | collective-permute-start | bytes 24584 | tf_op jit(solution)/shard_map/ppermute | solution.py:474
  78.4 3.8 %collective-permute-start.18 = (f32[9,128]{1,0:T(8,128)S(1)}, f32[9,128]{1,0:T(8,128)S(1)}, u32[]{:S(2)}, u32[]{:S(2)}) collective-permute-start(f32[9,128]{1,0:T(8,128)S(1)} %pad_maximum_fusion.2), channel_id=1, source_target_pairs={{0,1},{1,0},{2,3},{3,2},{4,5},{5,4},{6,7},{7,6},{8,9},{9,8},{10,11... | collective-permute-start | bytes 13832 | tf_op jit(solution)/shard_map/ppermute | solution.py:474

commit v2 on v1

--- a/solution.py
+++ b/solution.py
@@ -534,7 +534,6 @@
         [gathered, gathered, pltpu.SemaphoreType.DMA((2,))],
         in_specs=[ANY, ANY, VMEM],
     )(mine, other, unit_old)
-    share = [share[0], exchange(share[1], 4), exchange(share[2], 12), share[3]]
     early = call(
         functools.partial(early_kernel, cap, per),
         shape((24, 4 * cap), f32),
@@ -549,8 +548,6 @@
         ],
         in_specs=[VMEM, VMEM] + [ANY] * 7,
     )(scaled, facts, units, cross_set, passed, rows0, rows1, early2, early3)
-    share[3], early = in_order(share[3], early)
-    share[3] = exchange(share[3], 8)
     kept = shape((1, per, 4 * cap, width), bf16)
     kept_rows, floors = call(
         functools.partial(late_kernel, cap, per),
@@ -558,6 +555,8 @@
         [room(rows_of(1))] * 4 + [pltpu.SemaphoreType.DMA((4,))],
         in_specs=[VMEM] * 2 + [ANY] * 5,
     )(scaled, facts, rows0, rows1, late2, late3, early)
+    *share, kept_rows = in_order(*share, kept_rows)
+    share = [share[0]] + [exchange(value, apart) for value, apart in zip(share[1:], (4, 12, 8))]
     tile = shape((16, 4 * cap), f32)
     inside, across = call(
         functools.partial(third_kernel, cap, per),
@@ -569,7 +568,9 @@
         update_kernel, (shape((rows, width), bf16), shape((1, rows), i32)), in_specs=[ANY] + [VMEM] * 4
     )(inside, scaled, facts, centroids, prior_row)
     across = exchange(across, 2)
-    beside = exchange(jnp.concatenate([inside[4:8], across[4:8], inside[9:10] + across[9:10]], axis=0), 1)
+    beside = jnp.concatenate([inside[4:8], across[4:8], inside[9:10] + across[9:10]], axis=0)
+    beside, counts = in_order(beside, counts)
+    beside = exchange(beside, 1)
     density, level_two = call(
         functools.partial(last_kernel, cap, probe_count * BLOCK, BLOCK2), (shape((1, emb_rows), f32), shape((1, rows), f32))
     )(info, inside, across, beside)

time: 83.6 us -> 87.2 us (1.043)
  waiting for transfers between devices: 24.8 us -> 28.4 us
    ppermute x19, waiting for transfers between devices: 24.8 us -> 28.4 us  [exchange(): return lax.ppermute(value, 'shard', [(i, i ^ apart) for i in sources])]
    pallas_call x13 -> x14, Pallas kernels: 28.3 us -> 28.3 us  [run(): pl.pallas_call(kernel, out_shape=outs, in_specs=specs, scratch_shapes=lis...]
  transfers between devices with their start and end apart: 19 -> 19, of which waited for: 8 -> 10; matrix products, arithmetic and copies ran while one was open for 0% -> 0% of each run, Pallas kernels for 30% -> 29%
where the time goes in v2:
time: 87.2 us; the launch traced here: 86.8 us
  starting transfers between devices  29.1 us (33%)
  waiting for transfers between devices  28.4 us (33%)
  Pallas kernels  28.3 us (32%)
    ppermute x19, starting transfers between devices, exchange(): return lax.ppermute(value, 'shard', [(i, i ^ apart) for i in sources])  29.1 us
    ppermute x19, waiting for transfers between devices, exchange(): return lax.ppermute(value, 'shard', [(i, i ^ apart) for i in sources])  28.4 us
    pallas_call x14, Pallas kernels, run(): pl.pallas_call(kernel, out_shape=outs, in_specs=specs, scratch_shapes=lis...  28.3 us
  transfers between devices with their start and end apart: 19, of which 10 were waited for; matrix products, arithmetic and copies ran while one was open for 0% of the time, Pallas kernels for 29%

profile of v2, /device:TPU:0, one launch (start us, length us, event | category | flops | bytes accessed | tf_op | source)
XLA Modules:
  0.0 86.8 jit_solution(2457383188254641227)
XLA Ops:
  0.6 0.0 copy-start
  0.6 0.0 copy-start.3
  0.7 3.1 %collective-permute-start = (bf16[384,1024]{1,0:T(8,128)(2,1)}, bf16[384,1024]{1,0:T(8,128)(2,1)S(1)}, u32[]{:S(2)}, u32[]{:S(2)}) collective-permute-start(bf16[384,1024]{1,0:T(8,128)(2,1)} %own_any.1), channel_id=1, source_target_pairs={{0,4},{1,5},{2,6},{3,7},{4,0},{5,1},{6,2},{7,3},{8,12},{9,13},{10,... | collective-permute-start | bytes 2359304 | tf_op jit(solution)/shard_map/ppermute | solution.py:474
  3.7 0.7 collective-permute-start.1
  4.5 3.4 %shard_map.102 = (bf16[40,1152]{1,0:T(8,128)(2,1)S(1)}, bf16[304,1024]{1,0:T(8,128)(2,1)S(1)}, bf16[304,1024]{1,0:T(8,128)(2,1)S(1)}, s32[8,1024]{1,0:T(8,128)S(1)}) custom-call(s32[1,1024]{1,0:T(1,128)} %bitcast.10, bf16[40,1024]{1,0:T(8,128)(2,1)} %emb_any.1, s32[8,40]{1,0:T(8,128)} %bitcast.11, s32[1,40]{1,0:T(1,128)} %bitcast.13, s32[1,1024]{1,0:T(1,128)} %bitcast.7, ...), custom_call_target="tpu_custom_call" | custom-call | tf_op jit(solution)/shard_map/pallas_call | solution.py:440
  7.8 4.4 %collective-permute-start.2 = (bf16[40,1152]{1,0:T(8,128)(2,1)S(1)}, bf16[40,1152]{1,0:T(8,128)(2,1)S(1)}, u32[]{:S(2)}, u32[]{:S(2)}) collective-permute-start(bf16[40,1152]{1,0:T(8,128)(2,1)S(1)} %get-tuple-element.50), channel_id=1, source_target_pairs={{0,4},{1,5},{2,6},{3,7},{4,0},{5,1},{6,2},{7,3},{8,12},{9,13},{10,... | collective-permute-start | bytes 276488 | tf_op jit(solution)/shard_map/ppermute | solution.py:474
  12.3 1.5 %collective-permute-start.4 = (bf16[304,1024]{1,0:T(8,128)(2,1)S(1)}, bf16[304,1024]{1,0:T(8,128)(2,1)S(1)}, u32[]{:S(2)}, u32[]{:S(2)}) collective-permute-start(bf16[304,1024]{1,0:T(8,128)(2,1)S(1)} %get-tuple-element.53), channel_id=1, source_target_pairs={{0,2},{1,3},{2,0},{3,1},{4,6},{5,7},{6,4},{7,5},{8,10},{9,11},{10,... | collective-permute-start | bytes 1867784 | tf_op jit(solution)/shard_map/ppermute | solution.py:474
  13.8 0.0 collective-permute-start.5
  13.8 0.0 copy-done
  13.8 0.0 copy-done.3
  13.8 2.9 %shard_map.103 = (bf16[400,1024]{1,0:T(8,128)(2,1)S(1)}, bf16[400,1024]{1,0:T(8,128)(2,1)S(1)}, bf16[112,1024]{1,0:T(8,128)(2,1)S(1)}, bf16[112,1024]{1,0:T(8,128)(2,1)S(1)}) custom-call(s32[8,1024]{1,0:T(8,128)S(1)} %get-tuple-element.49.info, s32[1,1024]{1,0:T(1,128)S(1)} %bitcast.8, bf16[1024,1024]{1,0:T(8,128)(2,1)S(1)} %copy-done), custom_call_target="tpu_custom_call" | custom-call | tf_op jit(solution)/shard_map/pallas_call | solution.py:440
  16.7 6.7 %collective-permute-done.2 = bf16[40,1152]{1,0:T(8,128)(2,1)S(1)} collective-permute-done((bf16[40,1152]{1,0:T(8,128)(2,1)S(1)}, bf16[40,1152]{1,0:T(8,128)(2,1)S(1)}, u32[]{:S(2)}, u32[]{:S(2)}) %collective-permute-start.2) | collective-permute-done | bytes 92192 | tf_op jit(solution)/shard_map/ppermute | solution.py:474
  23.5 0.0 collective-permute-done.refs_0_
  23.5 0.0 collective-permute-done.1.refs_1_
  23.5 3.8 %collective-permute-start.3 = (bf16[80,1152]{1,0:T(8,128)(2,1)S(1)}, bf16[80,1152]{1,0:T(8,128)(2,1)S(1)}, u32[]{:S(2)}, u32[]{:S(2)}) collective-permute-start(bf16[80,1152]{1,0:T(8,128)(2,1)S(1)} %get-tuple-element.52), channel_id=1, source_target_pairs={{0,12},{1,13},{2,14},{3,15},{4,8},{5,9},{6,10},{7,11},{8,4},{9,5},... | collective-permute-start | bytes 552968 | tf_op jit(solution)/shard_map/ppermute | solution.py:474
  27.4 1.3 %collective-permute-start.8 = (bf16[384,1024]{1,0:T(8,128)(2,1)S(1)}, bf16[384,1024]{1,0:T(8,128)(2,1)S(1)}, u32[]{:S(2)}, u32[]{:S(2)}) collective-permute-start(bf16[384,1024]{1,0:T(8,128)(2,1)S(1)} %get-tuple-element.59.cross_any), channel_id=1, source_target_pairs={{4,0},{5,1},{6,2},{7,3},{8,12},{9,13},{10,14},{11,15},{20,16},{21,... | collective-permute-start | bytes 2359304 | tf_op jit(solution)/shard_map/ppermute | solution.py:474
  28.6 0.7 collective-permute-start.9
  29.4 2.0 %collective-permute-done.3 = bf16[80,1152]{1,0:T(8,128)(2,1)S(1)} collective-permute-done((bf16[80,1152]{1,0:T(8,128)(2,1)S(1)}, bf16[80,1152]{1,0:T(8,128)(2,1)S(1)}, u32[]{:S(2)}, u32[]{:S(2)}) %collective-permute-start.3) | collective-permute-done | bytes 184352 | tf_op jit(solution)/shard_map/ppermute | solution.py:474
  31.4 0.0 collective-permute-done.4.refs_1_
  31.4 8.1 %collective-permute-done.5.refs_2_ = bf16[304,1024]{1,0:T(8,128)(2,1)S(1)} collective-permute-done((bf16[304,1024]{1,0:T(8,128)(2,1)S(1)}, bf16[304,1024]{1,0:T(8,128)(2,1)S(1)}, u32[]{:S(2)}, u32[]{:S(2)}) %collective-permute-start.5) | collective-permute-done | bytes 622624 | tf_op jit(solution)/shard_map/ppermute | solution.py:474
  39.6 0.5 collective-permute-start.6
  40.1 3.2 %shard_map.106 = (bf16[1024,1024]{1,0:T(8,128)(2,1)S(1)}, bf16[2,384,1024]{2,1,0:T(8,128)(2,1)S(1)}) custom-call(bf16[1024,1024]{1,0:T(8,128)(2,1)} %cent_ref.5, bf16[384,1024]{1,0:T(8,128)(2,1)} %own_any.1, bf16[384,1024]{1,0:T(8,128)(2,1)S(1)} %get-tuple-element.60.near_any), custom_call_target="tpu_custom_call" | custom-call | tf_op jit(solution)/shard_map/pallas_call | solution.py:440
  43.3 1.9 %collective-permute-start.10 = (bf16[400,1024]{1,0:T(8,128)(2,1)S(1)}, bf16[400,1024]{1,0:T(8,128)(2,1)S(1)}, u32[]{:S(2)}, u32[]{:S(2)}) collective-permute-start(bf16[400,1024]{1,0:T(8,128)(2,1)S(1)} %get-tuple-element.69), channel_id=1, source_target_pairs={{0,1},{1,0},{2,3},{3,2},{4,5},{5,4},{6,7},{7,6},{8,9},{9,8},{10,11... | collective-permute-start | bytes 2457608 | tf_op jit(solution)/shard_map/ppermute | solution.py:474
  45.2 2.9 %collective-permute-done.8.refs_0_ = bf16[384,1024]{1,0:T(8,128)(2,1)S(1)} collective-permute-done((bf16[384,1024]{1,0:T(8,128)(2,1)S(1)}, bf16[384,1024]{1,0:T(8,128)(2,1)S(1)}, u32[]{:S(2)}, u32[]{:S(2)}) %collective-permute-start.8) | collective-permute-done | bytes 786464 | tf_op jit(solution)/shard_map/ppermute | solution.py:474
  48.2 0.0 collective-permute-done.9.refs_1_
  48.2 0.0 copy-start.2
  48.2 1.3 %collective-permute-start.16 = (bf16[384,1024]{1,0:T(8,128)(2,1)S(1)}, bf16[384,1024]{1,0:T(8,128)(2,1)}, u32[]{:S(2)}, u32[]{:S(2)}) collective-permute-start(bf16[384,1024]{1,0:T(8,128)(2,1)S(1)} %get-tuple-element.85.last_any), channel_id=1, source_target_pairs={{4,0},{5,1},{6,2},{7,3},{8,12},{9,13},{10,14},{11,15},{20,16},{21,... | collective-permute-start | bytes 2359304 | tf_op jit(solution)/shard_map/ppermute | solution.py:474
  49.5 1.5 %collective-permute-done.6 = bf16[160,1152]{1,0:T(8,128)(2,1)S(1)} collective-permute-done((bf16[160,1152]{1,0:T(8,128)(2,1)S(1)}, bf16[160,1152]{1,0:T(8,128)(2,1)S(1)}, u32[]{:S(2)}, u32[]{:S(2)}) %collective-permute-start.6) | collective-permute-done | bytes 368672 | tf_op jit(solution)/shard_map/ppermute | solution.py:474
  51.0 0.2 collective-permute-start.7
  51.1 0.3 collective-permute-start.11
  51.5 1.4 %collective-permute-start.12 = (bf16[112,1024]{1,0:T(8,128)(2,1)S(1)}, bf16[112,1024]{1,0:T(8,128)(2,1)S(1)}, u32[]{:S(2)}, u32[]{:S(2)}) collective-permute-start(bf16[112,1024]{1,0:T(8,128)(2,1)S(1)} %get-tuple-element.73), channel_id=1, source_target_pairs={{0,3},{1,2},{2,1},{3,0},{4,7},{5,6},{6,5},{7,4},{8,11},{9,10},{10,... | collective-permute-start | bytes 688136 | tf_op jit(solution)/shard_map/ppermute | solution.py:474
  52.9 0.4 collective-permute-done.7.other_any
  53.2 3.1 %shard_map.108 = (bf16[640,1024]{1,0:T(8,128)(2,1)S(1)}, s32[16,640]{1,0:T(8,128)S(1)}, f32[4,128]{1,0:T(4,128)S(1)}, f32[4,128]{1,0:T(4,128)S(1)}, f32[4,128]{1,0:T(4,128)S(1)}, /*index=5*/f32[4,128]{1,0:T(4,128)S(1)}) custom-call(bf16[320,1152]{1,0:T(8,128)(2,1)S(1)} %constant_dynamic-update-slice_fusion.mine_any, ...), custom_call_target="tpu_custom_call" | custom-call | tf_op jit(solution)/shard_map/pallas_call | solution.py:440
  56.4 0.0 copy-done.2
  56.4 0.0 collective-permute-done.10.any1
  56.4 6.0 %shard_map.109.after.early = f32[24,128]{1,0:T(8,128)S(1)} custom-call(bf16[640,1024]{1,0:T(8,128)(2,1)S(1)} %get-tuple-element.64.scaled, s32[16,640]{1,0:T(8,128)S(1)} %get-tuple-element.65.facts_in.facts, bf16[2,384,1024]{2,1,0:T(8,128)(2,1)} %copy-done.2, bf16[384,1024]{1,0:T(8,128)(2,1)S(1)} %get-tuple-element.59.cross_any, ...), custom_call_target="tpu_custom_call" | custom-call | tf_op jit(solution)/shard_map/pallas_call | solution.py:440
  62.3 0.0 collective-permute-done.11.any2
  62.4 1.0 %collective-permute-done.12.any3 = bf16[112,1024]{1,0:T(8,128)(2,1)S(1)} collective-permute-done((bf16[112,1024]{1,0:T(8,128)(2,1)S(1)}, bf16[112,1024]{1,0:T(8,128)(2,1)S(1)}, u32[]{:S(2)}, u32[]{:S(2)}) %collective-permute-start.12) | collective-permute-done | bytes 229408 | tf_op jit(solution)/shard_map/ppermute | solution.py:474
  63.4 2.8 %shard_map.110 = (bf16[1,3,128,1024]{3,2,1,0:T(8,128)(2,1)S(1)}, bf16[1,3,128,128]{3,2,1,0:T(8,128)(2,1)S(1)}) custom-call(bf16[640,1024]{1,0:T(8,128)(2,1)S(1)} %get-tuple-element.64.scaled, s32[16,640]{1,0:T(8,128)S(1)} %get-tuple-element.65.facts_in.facts, bf16[400,1024]{1,0:T(8,128)(2,1)S(1)} %get-tuple-element.68.any0, ...), custom_call_target="tpu_custom_call" | custom-call | tf_op jit(solution)/shard_map/pallas_call | solution.py:440
  66.2 0.0 copy-start.1
  66.2 4.0 %collective-permute-start.13 = (f32[4,128]{1,0:T(4,128)S(1)}, f32[4,128]{1,0:T(4,128)S(1)}, u32[]{:S(2)}, u32[]{:S(2)}) collective-permute-start(f32[4,128]{1,0:T(4,128)S(1)} %get-tuple-element.81), channel_id=1, source_target_pairs={{0,4},{1,5},{2,6},{3,7},{4,0},{5,1},{6,2},{7,3},{8,12},{9,13},{10,... | collective-permute-start | bytes 6152 | tf_op jit(solution)/shard_map/ppermute | solution.py:474
  70.3 2.3 %collective-permute-start.14 = (f32[4,128]{1,0:T(4,128)S(1)}, f32[4,128]{1,0:T(4,128)S(1)}, u32[]{:S(2)}, u32[]{:S(2)}) collective-permute-start(f32[4,128]{1,0:T(4,128)S(1)} %get-tuple-element.82), channel_id=1, source_target_pairs={{0,12},{1,13},{2,14},{3,15},{4,8},{5,9},{6,10},{7,11},{8,4},{9,5},... | collective-permute-start | bytes 6152 | tf_op jit(solution)/shard_map/ppermute | solution.py:474
  72.6 0.0 collective-permute-start.15
  72.6 0.0 collective-permute-done.13.share1
  72.6 3.1 %collective-permute-done.14.share2 = f32[4,128]{1,0:T(4,128)S(1)} collective-permute-done((f32[4,128]{1,0:T(4,128)S(1)}, f32[4,128]{1,0:T(4,128)S(1)}, u32[]{:S(2)}, u32[]{:S(2)}) %collective-permute-start.14) | collective-permute-done | bytes 2080 | tf_op jit(solution)/shard_map/ppermute | solution.py:474
  75.6 1.4 %collective-permute-done.15.share3 = f32[4,128]{1,0:T(4,128)S(1)} collective-permute-done((f32[4,128]{1,0:T(4,128)S(1)}, f32[4,128]{1,0:T(4,128)S(1)}, u32[]{:S(2)}, u32[]{:S(2)}) %collective-permute-start.15) | collective-permute-done | bytes 2080 | tf_op jit(solution)/shard_map/ppermute | solution.py:474
  77.0 0.0 collective-permute-done.16.far_any
  77.1 2.2 %shard_map.112 = (f32[16,128]{1,0:T(8,128)S(1)}, f32[16,128]{1,0:T(8,128)S(1)}) custom-call(f32[24,128]{1,0:T(8,128)S(1)} %shard_map.109.after.early, bf16[1,3,128,128]{3,2,1,0:T(8,128)(2,1)S(1)} %get-tuple-element.74.floors, f32[4,128]{1,0:T(4,128)S(1)} %get-tuple-element.80.share0, f32[4,128]{1,0:T(4,128)S(1)} %collective-permute-done.13.share1, ...), custom_call_target="tpu_custom_call" | custom-call | tf_op jit(solution)/shard_map/pallas_call | solution.py:440
  79.2 1.6 %collective-permute-start.17 = (f32[16,128]{1,0:T(8,128)S(1)}, f32[16,128]{1,0:T(8,128)S(1)}, u32[]{:S(2)}, u32[]{:S(2)}) collective-permute-start(f32[16,128]{1,0:T(8,128)S(1)} %get-tuple-element.87), channel_id=1, source_target_pairs={{0,2},{1,3},{2,0},{3,1},{4,6},{5,7},{6,4},{7,5},{8,10},{9,11},{10,... | collective-permute-start | bytes 24584 | tf_op jit(solution)/shard_map/ppermute | solution.py:474
  80.8 0.0 copy-done.1
  80.8 3.7 %shard_map.113 = (bf16[1024,1024]{1,0:T(8,128)(2,1)}, s32[1,1024]{1,0:T(1,128)}) custom-call(f32[16,128]{1,0:T(8,128)S(1)} %get-tuple-element.86.after.inside, bf16[640,1024]{1,0:T(8,128)(2,1)S(1)} %get-tuple-element.64.scaled, s32[16,640]{1,0:T(8,128)S(1)} %get-tuple-element.65.facts_in.facts, bf16[1024,1024]{1,0:T(8,128)(2,1)S(1)} %copy-done.1, ...), custom_call_target="tpu_custom_call" | custom-call | tf_op jit(solution)/shard_map/pallas_call | solution.py:440
  84.5 0.0 collective-permute-done.17.across
  84.5 0.1 collective-permute-start.18
  84.6 1.2 %collective-permute-done.18.beside = f32[9,128]{1,0:T(8,128)S(1)} collective-permute-done((f32[9,128]{1,0:T(8,128)S(1)}, f32[9,128]{1,0:T(8,128)S(1)}, u32[]{:S(2)}, u32[]{:S(2)}) %collective-permute-start.18) | collective-permute-done | bytes 4640 | tf_op jit(solution)/shard_map/ppermute | solution.py:474
  85.8 1.0 %shard_map.115 = (f32[1,40]{1,0:T(1,128)}, f32[1,1024]{1,0:T(1,128)}) custom-call(s32[8,1024]{1,0:T(8,128)S(1)} %get-tuple-element.49.info, f32[16,128]{1,0:T(8,128)S(1)} %get-tuple-element.86.after.inside, f32[16,128]{1,0:T(8,128)S(1)} %collective-permute-done.17.across, f32[9,128]{1,0:T(8,128)S(1)} %collective-permute-done.18.beside), custom_call_target="tpu_custom_call" | custom-call | tf_op jit(solution)/shard_map/pallas_call | solution.py:440
  (13 shorter events, 0.1 us)
Async XLA Ops:
  0.6 13.1 %copy-start = (bf16[1024,1024]{1,0:T(8,128)(2,1)S(1)}, bf16[1024,1024]{1,0:T(8,128)(2,1)}, u32[]{:S(2)}) copy-start(bf16[1024,1024]{1,0:T(8,128)(2,1)} %cent_ref.5) | copy-start | bytes 6291460
  0.6 13.1 %copy-start.3 = (s32[1024]{0:T(1024)S(1)}, s32[1024]{0:T(1024)}, u32[]{:S(2)}) copy-start(s32[1024]{0:T(1024)} %param.10) | copy-start | bytes 12292
  0.7 22.8 %collective-permute-start = (bf16[384,1024]{1,0:T(8,128)(2,1)}, bf16[384,1024]{1,0:T(8,128)(2,1)S(1)}, u32[]{:S(2)}, u32[]{:S(2)}) collective-permute-start(bf16[384,1024]{1,0:T(8,128)(2,1)} %own_any.1), channel_id=1, source_target_pairs={{0,4},{1,5},{2,6},{3,7},{4,0},{5,1},{6,2},{7,3},{8,12},{9,13},{10,... | collective-permute-start | bytes 2359304 | tf_op jit(solution)/shard_map/ppermute | solution.py:474
  3.7 19.8 %collective-permute-start.1 = (bf16[384,1024]{1,0:T(8,128)(2,1)}, bf16[384,1024]{1,0:T(8,128)(2,1)S(1)}, u32[]{:S(2)}, u32[]{:S(2)}) collective-permute-start(bf16[384,1024]{1,0:T(8,128)(2,1)} %own_any.1), channel_id=1, source_target_pairs={{4,8},{5,9},{6,10},{7,11},{8,4},{9,5},{10,6},{11,7},{20,24},{21,25... | collective-permute-start | bytes 2359304 | tf_op jit(solution)/shard_map/ppermute | solution.py:474
  7.8 15.6 %collective-permute-start.2 = (bf16[40,1152]{1,0:T(8,128)(2,1)S(1)}, bf16[40,1152]{1,0:T(8,128)(2,1)S(1)}, u32[]{:S(2)}, u32[]{:S(2)}) collective-permute-start(bf16[40,1152]{1,0:T(8,128)(2,1)S(1)} %get-tuple-element.50), channel_id=1, source_target_pairs={{0,4},{1,5},{2,6},{3,7},{4,0},{5,1},{6,2},{7,3},{8,12},{9,13},{10,... | collective-permute-start | bytes 276488 | tf_op jit(solution)/shard_map/ppermute | solution.py:474
  12.3 19.2 %collective-permute-start.4 = (bf16[304,1024]{1,0:T(8,128)(2,1)S(1)}, bf16[304,1024]{1,0:T(8,128)(2,1)S(1)}, u32[]{:S(2)}, u32[]{:S(2)}) collective-permute-start(bf16[304,1024]{1,0:T(8,128)(2,1)S(1)} %get-tuple-element.53), channel_id=1, source_target_pairs={{0,2},{1,3},{2,0},{3,1},{4,6},{5,7},{6,4},{7,5},{8,10},{9,11},{10,... | collective-permute-start | bytes 1867784 | tf_op jit(solution)/shard_map/ppermute | solution.py:474
  13.8 25.8 %collective-permute-start.5 = (bf16[304,1024]{1,0:T(8,128)(2,1)S(1)}, bf16[304,1024]{1,0:T(8,128)(2,1)S(1)}, u32[]{:S(2)}, u32[]{:S(2)}) collective-permute-start(bf16[304,1024]{1,0:T(8,128)(2,1)S(1)} %get-tuple-element.54), channel_id=1, source_target_pairs={{0,3},{1,2},{2,1},{3,0},{4,7},{5,6},{6,5},{7,4},{8,11},{9,10},{10,... | collective-permute-start | bytes 1867784 | tf_op jit(solution)/shard_map/ppermute | solution.py:474
  23.5 7.9 %collective-permute-start.3 = (bf16[80,1152]{1,0:T(8,128)(2,1)S(1)}, bf16[80,1152]{1,0:T(8,128)(2,1)S(1)}, u32[]{:S(2)}, u32[]{:S(2)}) collective-permute-start(bf16[80,1152]{1,0:T(8,128)(2,1)S(1)} %get-tuple-element.52), channel_id=1, source_target_pairs={{0,12},{1,13},{2,14},{3,15},{4,8},{5,9},{6,10},{7,11},{8,4},{9,5},... | collective-permute-start | bytes 552968 | tf_op jit(solution)/shard_map/ppermute | solution.py:474
  27.4 20.8 %collective-permute-start.8 = (bf16[384,1024]{1,0:T(8,128)(2,1)S(1)}, bf16[384,1024]{1,0:T(8,128)(2,1)S(1)}, u32[]{:S(2)}, u32[]{:S(2)}) collective-permute-start(bf16[384,1024]{1,0:T(8,128)(2,1)S(1)} %get-tuple-element.59.cross_any), channel_id=1, source_target_pairs={{4,0},{5,1},{6,2},{7,3},{8,12},{9,13},{10,14},{11,15},{20,16},{21,... | collective-permute-start | bytes 2359304 | tf_op jit(solution)/shard_map/ppermute | solution.py:474
  28.6 19.5 %collective-permute-start.9 = (bf16[384,1024]{1,0:T(8,128)(2,1)S(1)}, bf16[384,1024]{1,0:T(8,128)(2,1)S(1)}, u32[]{:S(2)}, u32[]{:S(2)}) collective-permute-start(bf16[384,1024]{1,0:T(8,128)(2,1)S(1)} %get-tuple-element.60.near_any), channel_id=1, source_target_pairs={{4,8},{5,9},{6,10},{7,11},{8,4},{9,5},{10,6},{11,7},{20,24},{21,25... | collective-permute-start | bytes 2359304 | tf_op jit(solution)/shard_map/ppermute | solution.py:474
  39.6 11.4 %collective-permute-start.6 = (bf16[160,1152]{1,0:T(8,128)(2,1)S(1)}, bf16[160,1152]{1,0:T(8,128)(2,1)S(1)}, u32[]{:S(2)}, u32[]{:S(2)}) collective-permute-start(bf16[160,1152]{1,0:T(8,128)(2,1)S(1)} %get-tuple-element.58), channel_id=1, source_target_pairs={{0,2},{1,3},{2,0},{3,1},{4,6},{5,7},{6,4},{7,5},{8,10},{9,11},{10,... | collective-permute-start | bytes 1105928 | tf_op jit(solution)/shard_map/ppermute | solution.py:474
  43.3 13.1 %collective-permute-start.10 = (bf16[400,1024]{1,0:T(8,128)(2,1)S(1)}, bf16[400,1024]{1,0:T(8,128)(2,1)S(1)}, u32[]{:S(2)}, u32[]{:S(2)}) collective-permute-start(bf16[400,1024]{1,0:T(8,128)(2,1)S(1)} %get-tuple-element.69), channel_id=1, source_target_pairs={{0,1},{1,0},{2,3},{3,2},{4,5},{5,4},{6,7},{7,6},{8,9},{9,8},{10,11... | collective-permute-start | bytes 2457608 | tf_op jit(solution)/shard_map/ppermute | solution.py:474
  48.2 8.2 %copy-start.2 = (bf16[2,384,1024]{2,1,0:T(8,128)(2,1)}, bf16[2,384,1024]{2,1,0:T(8,128)(2,1)S(1)}, u32[]{:S(2)}) copy-start(bf16[2,384,1024]{2,1,0:T(8,128)(2,1)S(1)} %get-tuple-element.66.units_any) | copy-start | bytes 4718596
  48.2 28.9 %collective-permute-start.16 = (bf16[384,1024]{1,0:T(8,128)(2,1)S(1)}, bf16[384,1024]{1,0:T(8,128)(2,1)}, u32[]{:S(2)}, u32[]{:S(2)}) collective-permute-start(bf16[384,1024]{1,0:T(8,128)(2,1)S(1)} %get-tuple-element.85.last_any), channel_id=1, source_target_pairs={{4,0},{5,1},{6,2},{7,3},{8,12},{9,13},{10,14},{11,15},{20,16},{21,... | collective-permute-start | bytes 2359304 | tf_op jit(solution)/shard_map/ppermute | solution.py:474
  51.0 2.3 %collective-permute-start.7 = (bf16[320,1152]{1,0:T(8,128)(2,1)S(1)}, bf16[320,1152]{1,0:T(8,128)(2,1)S(1)}, u32[]{:S(2)}, u32[]{:S(2)}) collective-permute-start(bf16[320,1152]{1,0:T(8,128)(2,1)S(1)} %constant_dynamic-update-slice_fusion.mine_any), channel_id=1, source_target_pairs={{0,1},{1,0},{2,3},{3,2},{4,5},{5,4},{6,7},{7,6},{8,9},{9,8},{10,11... | collective-permute-start | bytes 2211848 | tf_op jit(solution)/shard_map/ppermute | solution.py:474
  51.1 11.2 %collective-permute-start.11 = (bf16[112,1024]{1,0:T(8,128)(2,1)S(1)}, bf16[112,1024]{1,0:T(8,128)(2,1)S(1)}, u32[]{:S(2)}, u32[]{:S(2)}) collective-permute-start(bf16[112,1024]{1,0:T(8,128)(2,1)S(1)} %get-tuple-element.72), channel_id=1, source_target_pairs={{0,2},{1,3},{2,0},{3,1},{4,6},{5,7},{6,4},{7,5},{8,10},{9,11},{10,... | collective-permute-start | bytes 688136 | tf_op jit(solution)/shard_map/ppermute | solution.py:474
  51.5 11.9 %collective-permute-start.12 = (bf16[112,1024]{1,0:T(8,128)(2,1)S(1)}, bf16[112,1024]{1,0:T(8,128)(2,1)S(1)}, u32[]{:S(2)}, u32[]{:S(2)}) collective-permute-start(bf16[112,1024]{1,0:T(8,128)(2,1)S(1)} %get-tuple-element.73), channel_id=1, source_target_pairs={{0,3},{1,2},{2,1},{3,0},{4,7},{5,6},{6,5},{7,4},{8,11},{9,10},{10,... | collective-permute-start | bytes 688136 | tf_op jit(solution)/shard_map/ppermute | solution.py:474
  66.2 14.6 %copy-start.1 = (bf16[1024,1024]{1,0:T(8,128)(2,1)S(1)}, bf16[1024,1024]{1,0:T(8,128)(2,1)}, u32[]{:S(2)}) copy-start(bf16[1024,1024]{1,0:T(8,128)(2,1)} %cent_ref.5) | copy-start | bytes 6291460
  66.2 6.3 %collective-permute-start.13 = (f32[4,128]{1,0:T(4,128)S(1)}, f32[4,128]{1,0:T(4,128)S(1)}, u32[]{:S(2)}, u32[]{:S(2)}) collective-permute-start(f32[4,128]{1,0:T(4,128)S(1)} %get-tuple-element.81), channel_id=1, source_target_pairs={{0,4},{1,5},{2,6},{3,7},{4,0},{5,1},{6,2},{7,3},{8,12},{9,13},{10,... | collective-permute-start | bytes 6152 | tf_op jit(solution)/shard_map/ppermute | solution.py:474
  70.3 5.4 %collective-permute-start.14 = (f32[4,128]{1,0:T(4,128)S(1)}, f32[4,128]{1,0:T(4,128)S(1)}, u32[]{:S(2)}, u32[]{:S(2)}) collective-permute-start(f32[4,128]{1,0:T(4,128)S(1)} %get-tuple-element.82), channel_id=1, source_target_pairs={{0,12},{1,13},{2,14},{3,15},{4,8},{5,9},{6,10},{7,11},{8,4},{9,5},... | collective-permute-start | bytes 6152 | tf_op jit(solution)/shard_map/ppermute | solution.py:474
  72.6 4.5 %collective-permute-start.15 = (f32[4,128]{1,0:T(4,128)S(1)}, f32[4,128]{1,0:T(4,128)S(1)}, u32[]{:S(2)}, u32[]{:S(2)}) collective-permute-start(f32[4,128]{1,0:T(4,128)S(1)} %get-tuple-element.83), channel_id=1, source_target_pairs={{0,8},{1,9},{2,10},{3,11},{4,12},{5,13},{6,14},{7,15},{8,0},{9,1},... | collective-permute-start | bytes 6152 | tf_op jit(solution)/shard_map/ppermute | solution.py:474
  79.2 5.3 %collective-permute-start.17 = (f32[16,128]{1,0:T(8,128)S(1)}, f32[16,128]{1,0:T(8,128)S(1)}, u32[]{:S(2)}, u32[]{:S(2)}) collective-permute-start(f32[16,128]{1,0:T(8,128)S(1)} %get-tuple-element.87), channel_id=1, source_target_pairs={{0,2},{1,3},{2,0},{3,1},{4,6},{5,7},{6,4},{7,5},{8,10},{9,11},{10,... | collective-permute-start | bytes 24584 | tf_op jit(solution)/shard_map/ppermute | solution.py:474
  84.5 1.2 %collective-permute-start.18 = (f32[9,128]{1,0:T(8,128)S(1)}, f32[9,128]{1,0:T(8,128)S(1)}, u32[]{:S(2)}, u32[]{:S(2)}) collective-permute-start(f32[9,128]{1,0:T(8,128)S(1)} %get-tuple-element.89), channel_id=1, source_target_pairs={{0,1},{1,0},{2,3},{3,2},{4,5},{5,4},{6,7},{7,6},{8,9},{9,8},{10,11... | collective-permute-start | bytes 13832 | tf_op jit(solution)/shard_map/ppermute | solution.py:474

commit v3 on v0

--- a/solution.py
+++ b/solution.py
@@ -378,7 +378,7 @@
 
 
 def late_kernel(
-    cap, per, scaled, facts_in, any0, any1, any2, any3, after, updated, packed, floors, rows0, rows1, rows2, rows3, sems
+    cap, per, scaled, facts_in, any0, any1, any2, any3, after, packed, floors, rows0, rows1, rows2, rows3, sems
 ):
     me, z, y, core = position()
     part = per * cap
@@ -417,8 +417,8 @@
             out[start + t : start + t + 1, :] = jnp.sum(spread[4 * t : 4 * t + 4], axis=0, keepdims=True)
 
 
-def last_kernel(cap, scale_one, scale_two, info, inside, across, beside, share0, share1, share2, share3, density, level_two):
-    total = share0[...] + share1[...] + share2[...] + share3[...]
+def last_kernel(cap, scale_one, scale_two, info, inside, across, beside, share, density, level_two):
+    total = share[...]
     density[...] = jnp.log(total[:, 0 : density.shape[1]] / scale_one)
     values = jnp.concatenate([inside[0:4, :], beside[0:4, :], across[0:4, :], beside[4:8, :]], axis=0)
     rows = info.shape[1]
@@ -515,7 +515,7 @@
         [block_set, block_set, pltpu.SemaphoreType.DMA((2,))],
         in_specs=[VMEM, HBM, ANY],
     )(centroids, centroids2, near_set)
-    passed, last_set, unit_old, units = in_order(passed, last_set, unit_old, units)
+    passed, last_set, mine, unit_old, units = in_order(passed, last_set, mine, unit_old, units)
     far_set = exchange(last_set, 4, mids)
     other = exchange(mine, 1)
     gathered = pltpu.VMEM((8 * emb_rows, width + 128), bf16)
@@ -546,16 +546,16 @@
         ],
         in_specs=[VMEM, VMEM] + [ANY] * 7,
     )(scaled, facts, units, cross_set, passed, rows0, rows1, early2, early3)
-    new_centroids, counts = call(
-        update_kernel, (shape((rows, width), bf16), shape((1, rows), i32)), in_specs=[ANY] + [VMEM] * 4
-    )(early, scaled, facts, centroids, prior_row)
     kept = shape((1, per, 4 * cap, width), bf16)
     kept_rows, floors = call(
         functools.partial(late_kernel, cap, per),
         (kept, shape((1, per, 4 * cap, 128), bf16)),
         [room(rows_of(1))] * 4 + [pltpu.SemaphoreType.DMA((4,))],
-        in_specs=[VMEM] * 2 + [ANY] * 6,
-    )(scaled, facts, rows0, rows1, late2, late3, early, counts)
+        in_specs=[VMEM] * 2 + [ANY] * 5,
+    )(scaled, facts, rows0, rows1, late2, late3, early)
+    share, kept_rows = in_order(share, kept_rows)
+    share = share[0:2] + exchange(share[2:4], 12)
+    share = share[0:1] + exchange(share[1:2], 4)
     tile = shape((8, 4 * cap), f32)
     inside, across = call(
         functools.partial(third_kernel, cap, per),
@@ -563,12 +563,16 @@
         [room(kept), block_set, pltpu.SemaphoreType.DMA((2,))],
         in_specs=[VMEM, VMEM] + [ANY] * 3,
     )(early, floors, kept_rows, last_set, far_set)
+    new_centroids, counts = call(
+        update_kernel, (shape((rows, width), bf16), shape((1, rows), i32)), in_specs=[ANY] + [VMEM] * 4
+    )(inside, scaled, facts, centroids, prior_row)
     across = exchange(across, 2)
-    beside = exchange(jnp.concatenate([inside[4:8], across[4:8]], axis=0), 1)
-    share = [share[0:1]] + [exchange(share[i : i + 1], apart) for i, apart in ((1, 4), (2, 12), (3, 8))]
+    beside = jnp.concatenate([inside[4:8], across[4:8]], axis=0)
+    beside, counts = in_order(beside, counts)
+    beside = exchange(beside, 1)
     density, level_two = call(
         functools.partial(last_kernel, cap, probe_count * BLOCK, BLOCK2), (shape((1, emb_rows), f32), shape((1, rows), f32))
-    )(info, inside, across, beside, *share)
+    )(info, inside, across, beside, share)
     return (density.reshape(-1), new_centroids, counts.reshape(-1), level_two.reshape(-1))
 
 

time: 88.8 us -> 81.1 us (0.913)
  starting transfers between devices: 30.1 us -> 24.5 us
  Pallas kernels: 29.1 us -> 27.2 us
    ppermute x21 -> x20, starting transfers between devices: 30.1 us -> 24.5 us  [exchange(): return lax.ppermute(value, 'shard', [(i, i ^ apart) for i in sources])]
    pallas_call x12 -> x14, Pallas kernels: 29.1 us -> 27.2 us  [run(): pl.pallas_call(kernel, out_shape=outs, in_specs=specs, scratch_shapes=lis...]
    ppermute x21 -> x20, waiting for transfers between devices: 27.5 us -> 27.9 us  [exchange(): return lax.ppermute(value, 'shard', [(i, i ^ apart) for i in sources])]
  transfers between devices with their start and end apart: 21 -> 20, of which waited for: 10 -> 7; matrix products, arithmetic and copies ran while one was open for 0% -> 0% of each run, Pallas kernels for 32% -> 32%
where the time goes in v3:
time: 81.1 us; the launch traced here: 80.8 us
  waiting for transfers between devices  27.9 us (34%)
  Pallas kernels  27.2 us (34%)
  starting transfers between devices  24.5 us (30%)
  between operations  0.95 us (1%)
    ppermute x20, waiting for transfers between devices, exchange(): return lax.ppermute(value, 'shard', [(i, i ^ apart) for i in sources])  27.9 us
    pallas_call x14, Pallas kernels, run(): pl.pallas_call(kernel, out_shape=outs, in_specs=specs, scratch_shapes=lis...  27.2 us
    ppermute x20, starting transfers between devices, exchange(): return lax.ppermute(value, 'shard', [(i, i ^ apart) for i in sources])  24.5 us
  transfers between devices with their start and end apart: 20, of which 7 were waited for; matrix products, arithmetic and copies ran while one was open for 0% of the time, Pallas kernels for 32%

profile of v3, /device:TPU:0, one launch (start us, length us, event | category | flops | bytes accessed | tf_op | source)
XLA Modules:
  0.0 80.8 jit_solution(15389258973063706132)
XLA Ops:
  0.6 0.0 copy-start
  0.6 0.0 copy-start.3
  0.7 3.1 %collective-permute-start = (bf16[384,1024]{1,0:T(8,128)(2,1)}, bf16[384,1024]{1,0:T(8,128)(2,1)S(1)}, u32[]{:S(2)}, u32[]{:S(2)}) collective-permute-start(bf16[384,1024]{1,0:T(8,128)(2,1)} %own_any.1), channel_id=1, source_target_pairs={{0,4},{1,5},{2,6},{3,7},{4,0},{5,1},{6,2},{7,3},{8,12},{9,13},{10,... | collective-permute-start | bytes 2359304 | tf_op jit(solution)/shard_map/ppermute | solution.py:469
  3.7 0.7 collective-permute-start.1
  4.5 3.4 %shard_map.102 = (bf16[40,1152]{1,0:T(8,128)(2,1)S(1)}, bf16[304,1024]{1,0:T(8,128)(2,1)S(1)}, bf16[304,1024]{1,0:T(8,128)(2,1)S(1)}, s32[8,1024]{1,0:T(8,128)S(1)}) custom-call(s32[1,1024]{1,0:T(1,128)} %bitcast.10, bf16[40,1024]{1,0:T(8,128)(2,1)} %emb_any.1, s32[8,40]{1,0:T(8,128)} %bitcast.11, s32[1,40]{1,0:T(1,128)} %bitcast.13, s32[1,1024]{1,0:T(1,128)} %bitcast.7, ...), custom_call_target="tpu_custom_call" | custom-call | tf_op jit(solution)/shard_map/pallas_call | solution.py:435
  7.8 4.4 %collective-permute-start.2 = (bf16[40,1152]{1,0:T(8,128)(2,1)S(1)}, bf16[40,1152]{1,0:T(8,128)(2,1)S(1)}, u32[]{:S(2)}, u32[]{:S(2)}) collective-permute-start(bf16[40,1152]{1,0:T(8,128)(2,1)S(1)} %get-tuple-element.46), channel_id=1, source_target_pairs={{0,4},{1,5},{2,6},{3,7},{4,0},{5,1},{6,2},{7,3},{8,12},{9,13},{10,... | collective-permute-start | bytes 276488 | tf_op jit(solution)/shard_map/ppermute | solution.py:469
  12.3 1.5 %collective-permute-start.6 = (bf16[304,1024]{1,0:T(8,128)(2,1)S(1)}, bf16[304,1024]{1,0:T(8,128)(2,1)S(1)}, u32[]{:S(2)}, u32[]{:S(2)}) collective-permute-start(bf16[304,1024]{1,0:T(8,128)(2,1)S(1)} %get-tuple-element.51), channel_id=1, source_target_pairs={{0,2},{1,3},{2,0},{3,1},{4,6},{5,7},{6,4},{7,5},{8,10},{9,11},{10,... | collective-permute-start | bytes 1867784 | tf_op jit(solution)/shard_map/ppermute | solution.py:469
  13.8 0.0 collective-permute-start.7
  13.8 0.0 copy-done
  13.8 0.0 copy-done.3
  13.8 2.9 %shard_map.103 = (bf16[400,1024]{1,0:T(8,128)(2,1)S(1)}, bf16[400,1024]{1,0:T(8,128)(2,1)S(1)}, bf16[112,1024]{1,0:T(8,128)(2,1)S(1)}, bf16[112,1024]{1,0:T(8,128)(2,1)S(1)}) custom-call(s32[8,1024]{1,0:T(8,128)S(1)} %get-tuple-element.45.info, s32[1,1024]{1,0:T(1,128)S(1)} %bitcast.8, bf16[1024,1024]{1,0:T(8,128)(2,1)S(1)} %copy-done), custom_call_target="tpu_custom_call" | custom-call | tf_op jit(solution)/shard_map/pallas_call | solution.py:435
  16.7 6.8 %collective-permute-done.2 = bf16[40,1152]{1,0:T(8,128)(2,1)S(1)} collective-permute-done((bf16[40,1152]{1,0:T(8,128)(2,1)S(1)}, bf16[40,1152]{1,0:T(8,128)(2,1)S(1)}, u32[]{:S(2)}, u32[]{:S(2)}) %collective-permute-start.2) | collective-permute-done | bytes 92192 | tf_op jit(solution)/shard_map/ppermute | solution.py:469
  23.5 0.0 collective-permute-done.refs_0_
  23.5 0.0 collective-permute-done.1.refs_1_
  23.5 3.8 %collective-permute-start.5 = (bf16[80,1152]{1,0:T(8,128)(2,1)S(1)}, bf16[80,1152]{1,0:T(8,128)(2,1)S(1)}, u32[]{:S(2)}, u32[]{:S(2)}) collective-permute-start(bf16[80,1152]{1,0:T(8,128)(2,1)S(1)} %get-tuple-element.50), channel_id=1, source_target_pairs={{0,12},{1,13},{2,14},{3,15},{4,8},{5,9},{6,10},{7,11},{8,4},{9,5},... | collective-permute-start | bytes 552968 | tf_op jit(solution)/shard_map/ppermute | solution.py:469
  27.4 1.3 %collective-permute-start.3 = (bf16[384,1024]{1,0:T(8,128)(2,1)S(1)}, bf16[384,1024]{1,0:T(8,128)(2,1)S(1)}, u32[]{:S(2)}, u32[]{:S(2)}) collective-permute-start(bf16[384,1024]{1,0:T(8,128)(2,1)S(1)} %get-tuple-element.48.cross_any), channel_id=1, source_target_pairs={{4,0},{5,1},{6,2},{7,3},{8,12},{9,13},{10,14},{11,15},{20,16},{21,... | collective-permute-start | bytes 2359304 | tf_op jit(solution)/shard_map/ppermute | solution.py:469
  28.6 0.7 collective-permute-start.4
  29.4 2.0 %collective-permute-done.5 = bf16[80,1152]{1,0:T(8,128)(2,1)S(1)} collective-permute-done((bf16[80,1152]{1,0:T(8,128)(2,1)S(1)}, bf16[80,1152]{1,0:T(8,128)(2,1)S(1)}, u32[]{:S(2)}, u32[]{:S(2)}) %collective-permute-start.5) | collective-permute-done | bytes 184352 | tf_op jit(solution)/shard_map/ppermute | solution.py:469
  31.4 0.0 collective-permute-done.6.refs_1_
  31.4 8.1 %collective-permute-done.7.refs_2_ = bf16[304,1024]{1,0:T(8,128)(2,1)S(1)} collective-permute-done((bf16[304,1024]{1,0:T(8,128)(2,1)S(1)}, bf16[304,1024]{1,0:T(8,128)(2,1)S(1)}, u32[]{:S(2)}, u32[]{:S(2)}) %collective-permute-start.7) | collective-permute-done | bytes 622624 | tf_op jit(solution)/shard_map/ppermute | solution.py:469
  39.6 0.5 collective-permute-start.8
  40.1 3.2 %shard_map.106 = (bf16[1024,1024]{1,0:T(8,128)(2,1)S(1)}, bf16[2,384,1024]{2,1,0:T(8,128)(2,1)S(1)}) custom-call(bf16[1024,1024]{1,0:T(8,128)(2,1)} %cent_ref.5, bf16[384,1024]{1,0:T(8,128)(2,1)} %own_any.1, bf16[384,1024]{1,0:T(8,128)(2,1)S(1)} %get-tuple-element.49.near_any), custom_call_target="tpu_custom_call" | custom-call | tf_op jit(solution)/shard_map/pallas_call | solution.py:435
  43.3 1.9 %collective-permute-start.10 = (bf16[400,1024]{1,0:T(8,128)(2,1)S(1)}, bf16[400,1024]{1,0:T(8,128)(2,1)S(1)}, u32[]{:S(2)}, u32[]{:S(2)}) collective-permute-start(bf16[400,1024]{1,0:T(8,128)(2,1)S(1)} %get-tuple-element.66), channel_id=1, source_target_pairs={{0,1},{1,0},{2,3},{3,2},{4,5},{5,4},{6,7},{7,6},{8,9},{9,8},{10,11... | collective-permute-start | bytes 2457608 | tf_op jit(solution)/shard_map/ppermute | solution.py:469
  45.2 5.7 %collective-permute-done.8 = bf16[160,1152]{1,0:T(8,128)(2,1)S(1)} collective-permute-done((bf16[160,1152]{1,0:T(8,128)(2,1)S(1)}, bf16[160,1152]{1,0:T(8,128)(2,1)S(1)}, u32[]{:S(2)}, u32[]{:S(2)}) %collective-permute-start.8) | collective-permute-done | bytes 368672 | tf_op jit(solution)/shard_map/ppermute | solution.py:469
  50.9 0.1 pad_maximum_fusion.refs_2_
  51.0 0.0 collective-permute-done.3.refs_0_
  51.0 0.0 collective-permute-done.4.refs_1_
  51.0 0.0 copy-start.2
  51.0 0.2 collective-permute-start.9
  51.2 1.3 %collective-permute-start.15 = (bf16[384,1024]{1,0:T(8,128)(2,1)S(1)}, bf16[384,1024]{1,0:T(8,128)(2,1)S(1)}, u32[]{:S(2)}, u32[]{:S(2)}) collective-permute-start(bf16[384,1024]{1,0:T(8,128)(2,1)S(1)} %get-tuple-element.76.last_any), channel_id=1, source_target_pairs={{4,0},{5,1},{6,2},{7,3},{8,12},{9,13},{10,14},{11,15},{20,16},{21,... | collective-permute-start | bytes 2359304 | tf_op jit(solution)/shard_map/ppermute | solution.py:469
  52.5 0.4 collective-permute-start.11
  52.9 1.4 %collective-permute-start.12 = (bf16[112,1024]{1,0:T(8,128)(2,1)S(1)}, bf16[112,1024]{1,0:T(8,128)(2,1)S(1)}, u32[]{:S(2)}, u32[]{:S(2)}) collective-permute-start(bf16[112,1024]{1,0:T(8,128)(2,1)S(1)} %get-tuple-element.70), channel_id=1, source_target_pairs={{0,3},{1,2},{2,1},{3,0},{4,7},{5,6},{6,5},{7,4},{8,11},{9,10},{10,... | collective-permute-start | bytes 688136 | tf_op jit(solution)/shard_map/ppermute | solution.py:469
  54.3 0.0 collective-permute-done.9.other_any
  54.3 3.1 %shard_map.108 = (bf16[640,1024]{1,0:T(8,128)(2,1)S(1)}, s32[16,640]{1,0:T(8,128)S(1)}, f32[8,128]{1,0:T(8,128)S(1)}, f32[8,128]{1,0:T(8,128)S(1)}) custom-call(bf16[320,1152]{1,0:T(8,128)(2,1)S(1)} %get-tuple-element.59.mine_any, bf16[320,1152]{1,0:T(8,128)(2,1)S(1)} %collective-permute-done.9.other_any, bf16[1024,1024]{1,0:T(8,128)(2,1)S(1)} %get-tuple-element.60.unit_old), custom_call_target="tpu_custom_call" | custom-call | tf_op jit(solution)/shard_map/pallas_call | solution.py:435
  57.4 0.0 copy-done.2
  57.4 0.5 collective-permute-start.13
  57.9 0.8 %collective-permute-done.13 = f32[8,128]{1,0:T(8,128)S(1)} collective-permute-done((f32[8,128]{1,0:T(8,128)S(1)}, f32[8,128]{1,0:T(8,128)S(1)}, u32[]{:S(2)}, u32[]{:S(2)}) %collective-permute-start.13) | collective-permute-done | bytes 4128 | tf_op jit(solution)/shard_map/ppermute | solution.py:469
  58.8 0.3 collective-permute-start.14
  59.1 0.0 collective-permute-done.10.any1
  59.1 5.9 %shard_map.109.after.early = f32[24,128]{1,0:T(8,128)S(1)} custom-call(bf16[640,1024]{1,0:T(8,128)(2,1)S(1)} %get-tuple-element.61.scaled, s32[16,640]{1,0:T(8,128)S(1)} %get-tuple-element.62.facts_in.facts, bf16[2,384,1024]{2,1,0:T(8,128)(2,1)} %copy-done.2, bf16[384,1024]{1,0:T(8,128)(2,1)S(1)} %get-tuple-element.48.cross_any, ...), custom_call_target="tpu_custom_call" | custom-call | tf_op jit(solution)/shard_map/pallas_call | solution.py:435
  65.0 0.0 collective-permute-done.11.any2
  65.0 0.0 collective-permute-done.12.any3
  65.0 2.8 %shard_map.110 = (bf16[1,3,128,1024]{3,2,1,0:T(8,128)(2,1)S(1)}, bf16[1,3,128,128]{3,2,1,0:T(8,128)(2,1)S(1)}) custom-call(bf16[640,1024]{1,0:T(8,128)(2,1)S(1)} %get-tuple-element.61.scaled, s32[16,640]{1,0:T(8,128)S(1)} %get-tuple-element.62.facts_in.facts, bf16[400,1024]{1,0:T(8,128)(2,1)S(1)} %get-tuple-element.65.any0, ...), custom_call_target="tpu_custom_call" | custom-call | tf_op jit(solution)/shard_map/pallas_call | solution.py:435
  67.9 0.0 collective-permute-done.14
  67.9 0.0 copy-start.1
  67.9 1.8 %collective-permute-start.18 = (f32[2,128]{1,0:T(2,128)S(1)}, f32[2,128]{1,0:T(2,128)S(1)}, u32[]{:S(2)}, u32[]{:S(2)}) collective-permute-start(f32[2,128]{1,0:T(2,128)S(1)} %slice.29), channel_id=1, source_target_pairs={{0,12},{1,13},{2,14},{3,15},{4,8},{5,9},{6,10},{7,11},{8,4},{9,5},... | collective-permute-start | bytes 3080 | tf_op jit(solution)/shard_map/ppermute | solution.py:469
  69.7 3.3 %collective-permute-done.15.far_any = bf16[384,1024]{1,0:T(8,128)(2,1)S(1)} collective-permute-done((bf16[384,1024]{1,0:T(8,128)(2,1)S(1)}, bf16[384,1024]{1,0:T(8,128)(2,1)S(1)}, u32[]{:S(2)}, u32[]{:S(2)}) %collective-permute-start.15) | collective-permute-done | bytes 786464 | tf_op jit(solution)/shard_map/ppermute | solution.py:469
  72.9 1.1 %shard_map.112 = (f32[8,128]{1,0:T(8,128)S(1)}, f32[8,128]{1,0:T(8,128)S(1)}) custom-call(f32[24,128]{1,0:T(8,128)S(1)} %shard_map.109.after.early, bf16[1,3,128,128]{3,2,1,0:T(8,128)(2,1)S(1)} %get-tuple-element.71.floors, bf16[1,3,128,1024]{3,2,1,0:T(8,128)(2,1)S(1)} %get-tuple-element.75.kept_any, bf16[384,1024]{1,0:T(8,128)(2,1)S(1)} %get-tuple-element.76.last_any, ...), custom_call_target="tpu_custom_call" | custom-call | tf_op jit(solution)/shard_map/pallas_call | solution.py:435
  74.1 0.6 collective-permute-start.16
  74.7 0.0 collective-permute-done.18
  74.7 0.1 collective-permute-start.19
  74.8 0.0 copy-done.1
  74.8 3.7 %shard_map.113 = (bf16[1024,1024]{1,0:T(8,128)(2,1)}, s32[1,1024]{1,0:T(1,128)}) custom-call(f32[8,128]{1,0:T(8,128)S(1)} %get-tuple-element.77.after.inside, bf16[640,1024]{1,0:T(8,128)(2,1)S(1)} %get-tuple-element.61.scaled, s32[16,640]{1,0:T(8,128)S(1)} %get-tuple-element.62.facts_in.facts, bf16[1024,1024]{1,0:T(8,128)(2,1)S(1)} %copy-done.1, ...), custom_call_target="tpu_custom_call" | custom-call | tf_op jit(solution)/shard_map/pallas_call | solution.py:435
  78.5 0.0 collective-permute-done.16.across
  78.5 0.1 collective-permute-start.17
  78.6 0.0 collective-permute-done.19
  78.6 1.1 %collective-permute-done.17.beside = f32[8,128]{1,0:T(8,128)S(1)} collective-permute-done((f32[8,128]{1,0:T(8,128)S(1)}, f32[8,128]{1,0:T(8,128)S(1)}, u32[]{:S(2)}, u32[]{:S(2)}) %collective-permute-start.17) | collective-permute-done | bytes 4128 | tf_op jit(solution)/shard_map/ppermute | solution.py:469
  79.7 1.0 %shard_map.115 = (f32[1,40]{1,0:T(1,128)}, f32[1,1024]{1,0:T(1,128)}) custom-call(s32[8,1024]{1,0:T(8,128)S(1)} %get-tuple-element.45.info, f32[8,128]{1,0:T(8,128)S(1)} %get-tuple-element.77.after.inside, f32[8,128]{1,0:T(8,128)S(1)} %collective-permute-done.16.across, f32[8,128]{1,0:T(8,128)S(1)} %collective-permute-done.17.beside, ...), custom_call_target="tpu_custom_call" | custom-call | tf_op jit(solution)/shard_map/pallas_call | solution.py:435
  (17 shorter events, 0.1 us)
Async XLA Ops:
  0.6 13.1 %copy-start = (bf16[1024,1024]{1,0:T(8,128)(2,1)S(1)}, bf16[1024,1024]{1,0:T(8,128)(2,1)}, u32[]{:S(2)}) copy-start(bf16[1024,1024]{1,0:T(8,128)(2,1)} %cent_ref.5) | copy-start | bytes 6291460
  0.6 13.1 %copy-start.3 = (s32[1024]{0:T(1024)S(1)}, s32[1024]{0:T(1024)}, u32[]{:S(2)}) copy-start(s32[1024]{0:T(1024)} %param.10) | copy-start | bytes 12292
  0.7 22.8 %collective-permute-start = (bf16[384,1024]{1,0:T(8,128)(2,1)}, bf16[384,1024]{1,0:T(8,128)(2,1)S(1)}, u32[]{:S(2)}, u32[]{:S(2)}) collective-permute-start(bf16[384,1024]{1,0:T(8,128)(2,1)} %own_any.1), channel_id=1, source_target_pairs={{0,4},{1,5},{2,6},{3,7},{4,0},{5,1},{6,2},{7,3},{8,12},{9,13},{10,... | collective-permute-start | bytes 2359304 | tf_op jit(solution)/shard_map/ppermute | solution.py:469
  3.7 19.8 %collective-permute-start.1 = (bf16[384,1024]{1,0:T(8,128)(2,1)}, bf16[384,1024]{1,0:T(8,128)(2,1)S(1)}, u32[]{:S(2)}, u32[]{:S(2)}) collective-permute-start(bf16[384,1024]{1,0:T(8,128)(2,1)} %own_any.1), channel_id=1, source_target_pairs={{4,8},{5,9},{6,10},{7,11},{8,4},{9,5},{10,6},{11,7},{20,24},{21,25... | collective-permute-start | bytes 2359304 | tf_op jit(solution)/shard_map/ppermute | solution.py:469
  7.8 15.6 %collective-permute-start.2 = (bf16[40,1152]{1,0:T(8,128)(2,1)S(1)}, bf16[40,1152]{1,0:T(8,128)(2,1)S(1)}, u32[]{:S(2)}, u32[]{:S(2)}) collective-permute-start(bf16[40,1152]{1,0:T(8,128)(2,1)S(1)} %get-tuple-element.46), channel_id=1, source_target_pairs={{0,4},{1,5},{2,6},{3,7},{4,0},{5,1},{6,2},{7,3},{8,12},{9,13},{10,... | collective-permute-start | bytes 276488 | tf_op jit(solution)/shard_map/ppermute | solution.py:469
  12.3 19.2 %collective-permute-start.6 = (bf16[304,1024]{1,0:T(8,128)(2,1)S(1)}, bf16[304,1024]{1,0:T(8,128)(2,1)S(1)}, u32[]{:S(2)}, u32[]{:S(2)}) collective-permute-start(bf16[304,1024]{1,0:T(8,128)(2,1)S(1)} %get-tuple-element.51), channel_id=1, source_target_pairs={{0,2},{1,3},{2,0},{3,1},{4,6},{5,7},{6,4},{7,5},{8,10},{9,11},{10,... | collective-permute-start | bytes 1867784 | tf_op jit(solution)/shard_map/ppermute | solution.py:469
  13.8 25.8 %collective-permute-start.7 = (bf16[304,1024]{1,0:T(8,128)(2,1)S(1)}, bf16[304,1024]{1,0:T(8,128)(2,1)S(1)}, u32[]{:S(2)}, u32[]{:S(2)}) collective-permute-start(bf16[304,1024]{1,0:T(8,128)(2,1)S(1)} %get-tuple-element.52), channel_id=1, source_target_pairs={{0,3},{1,2},{2,1},{3,0},{4,7},{5,6},{6,5},{7,4},{8,11},{9,10},{10,... | collective-permute-start | bytes 1867784 | tf_op jit(solution)/shard_map/ppermute | solution.py:469
  23.5 7.9 %collective-permute-start.5 = (bf16[80,1152]{1,0:T(8,128)(2,1)S(1)}, bf16[80,1152]{1,0:T(8,128)(2,1)S(1)}, u32[]{:S(2)}, u32[]{:S(2)}) collective-permute-start(bf16[80,1152]{1,0:T(8,128)(2,1)S(1)} %get-tuple-element.50), channel_id=1, source_target_pairs={{0,12},{1,13},{2,14},{3,15},{4,8},{5,9},{6,10},{7,11},{8,4},{9,5},... | collective-permute-start | bytes 552968 | tf_op jit(solution)/shard_map/ppermute | solution.py:469
  27.4 23.6 %collective-permute-start.3 = (bf16[384,1024]{1,0:T(8,128)(2,1)S(1)}, bf16[384,1024]{1,0:T(8,128)(2,1)S(1)}, u32[]{:S(2)}, u32[]{:S(2)}) collective-permute-start(bf16[384,1024]{1,0:T(8,128)(2,1)S(1)} %get-tuple-element.48.cross_any), channel_id=1, source_target_pairs={{4,0},{5,1},{6,2},{7,3},{8,12},{9,13},{10,14},{11,15},{20,16},{21,... | collective-permute-start | bytes 2359304 | tf_op jit(solution)/shard_map/ppermute | solution.py:469
  28.6 22.4 %collective-permute-start.4 = (bf16[384,1024]{1,0:T(8,128)(2,1)S(1)}, bf16[384,1024]{1,0:T(8,128)(2,1)S(1)}, u32[]{:S(2)}, u32[]{:S(2)}) collective-permute-start(bf16[384,1024]{1,0:T(8,128)(2,1)S(1)} %get-tuple-element.49.near_any), channel_id=1, source_target_pairs={{4,8},{5,9},{6,10},{7,11},{8,4},{9,5},{10,6},{11,7},{20,24},{21,25... | collective-permute-start | bytes 2359304 | tf_op jit(solution)/shard_map/ppermute | solution.py:469
  39.6 11.4 %collective-permute-start.8 = (bf16[160,1152]{1,0:T(8,128)(2,1)S(1)}, bf16[160,1152]{1,0:T(8,128)(2,1)S(1)}, u32[]{:S(2)}, u32[]{:S(2)}) collective-permute-start(bf16[160,1152]{1,0:T(8,128)(2,1)S(1)} %get-tuple-element.56), channel_id=1, source_target_pairs={{0,2},{1,3},{2,0},{3,1},{4,6},{5,7},{6,4},{7,5},{8,10},{9,11},{10,... | collective-permute-start | bytes 1105928 | tf_op jit(solution)/shard_map/ppermute | solution.py:469
  43.3 15.7 %collective-permute-start.10 = (bf16[400,1024]{1,0:T(8,128)(2,1)S(1)}, bf16[400,1024]{1,0:T(8,128)(2,1)S(1)}, u32[]{:S(2)}, u32[]{:S(2)}) collective-permute-start(bf16[400,1024]{1,0:T(8,128)(2,1)S(1)} %get-tuple-element.66), channel_id=1, source_target_pairs={{0,1},{1,0},{2,3},{3,2},{4,5},{5,4},{6,7},{7,6},{8,9},{9,8},{10,11... | collective-permute-start | bytes 2457608 | tf_op jit(solution)/shard_map/ppermute | solution.py:469
  51.0 6.4 %copy-start.2 = (bf16[2,384,1024]{2,1,0:T(8,128)(2,1)}, bf16[2,384,1024]{2,1,0:T(8,128)(2,1)S(1)}, u32[]{:S(2)}) copy-start(bf16[2,384,1024]{2,1,0:T(8,128)(2,1)S(1)} %get-tuple-element.63.units_any) | copy-start | bytes 4718596
  51.0 3.3 %collective-permute-start.9 = (bf16[320,1152]{1,0:T(8,128)(2,1)S(1)}, bf16[320,1152]{1,0:T(8,128)(2,1)S(1)}, u32[]{:S(2)}, u32[]{:S(2)}) collective-permute-start(bf16[320,1152]{1,0:T(8,128)(2,1)S(1)} %get-tuple-element.59.mine_any), channel_id=1, source_target_pairs={{0,1},{1,0},{2,3},{3,2},{4,5},{5,4},{6,7},{7,6},{8,9},{9,8},{10,11... | collective-permute-start | bytes 2211848 | tf_op jit(solution)/shard_map/ppermute | solution.py:469
  51.2 21.7 %collective-permute-start.15 = (bf16[384,1024]{1,0:T(8,128)(2,1)S(1)}, bf16[384,1024]{1,0:T(8,128)(2,1)S(1)}, u32[]{:S(2)}, u32[]{:S(2)}) collective-permute-start(bf16[384,1024]{1,0:T(8,128)(2,1)S(1)} %get-tuple-element.76.last_any), channel_id=1, source_target_pairs={{4,0},{5,1},{6,2},{7,3},{8,12},{9,13},{10,14},{11,15},{20,16},{21,... | collective-permute-start | bytes 2359304 | tf_op jit(solution)/shard_map/ppermute | solution.py:469
  52.5 12.5 %collective-permute-start.11 = (bf16[112,1024]{1,0:T(8,128)(2,1)S(1)}, bf16[112,1024]{1,0:T(8,128)(2,1)S(1)}, u32[]{:S(2)}, u32[]{:S(2)}) collective-permute-start(bf16[112,1024]{1,0:T(8,128)(2,1)S(1)} %get-tuple-element.69), channel_id=1, source_target_pairs={{0,2},{1,3},{2,0},{3,1},{4,6},{5,7},{6,4},{7,5},{8,10},{9,11},{10,... | collective-permute-start | bytes 688136 | tf_op jit(solution)/shard_map/ppermute | solution.py:469
  52.9 12.1 %collective-permute-start.12 = (bf16[112,1024]{1,0:T(8,128)(2,1)S(1)}, bf16[112,1024]{1,0:T(8,128)(2,1)S(1)}, u32[]{:S(2)}, u32[]{:S(2)}) collective-permute-start(bf16[112,1024]{1,0:T(8,128)(2,1)S(1)} %get-tuple-element.70), channel_id=1, source_target_pairs={{0,3},{1,2},{2,1},{3,0},{4,7},{5,6},{6,5},{7,4},{8,11},{9,10},{10,... | collective-permute-start | bytes 688136 | tf_op jit(solution)/shard_map/ppermute | solution.py:469
  57.4 1.3 %collective-permute-start.13 = (f32[8,128]{1,0:T(8,128)S(1)}, f32[8,128]{1,0:T(8,128)S(1)}, u32[]{:S(2)}, u32[]{:S(2)}) collective-permute-start(f32[8,128]{1,0:T(8,128)S(1)} %get-tuple-element.73), channel_id=1, source_target_pairs={{0,1},{1,0},{2,3},{3,2},{4,5},{5,4},{6,7},{7,6},{8,9},{9,8},{10,11... | collective-permute-start | bytes 12296 | tf_op jit(solution)/shard_map/ppermute | solution.py:469
  58.8 9.1 %collective-permute-start.14 = (f32[4,128]{1,0:T(4,128)S(1)}, f32[4,128]{1,0:T(4,128)S(1)}, u32[]{:S(2)}, u32[]{:S(2)}) collective-permute-start(f32[4,128]{1,0:T(4,128)S(1)} %slice.25), channel_id=1, source_target_pairs={{0,2},{1,3},{2,0},{3,1},{4,6},{5,7},{6,4},{7,5},{8,10},{9,11},{10,... | collective-permute-start | bytes 6152 | tf_op jit(solution)/shard_map/ppermute | solution.py:469
  67.9 6.9 %copy-start.1 = (bf16[1024,1024]{1,0:T(8,128)(2,1)S(1)}, bf16[1024,1024]{1,0:T(8,128)(2,1)}, u32[]{:S(2)}) copy-start(bf16[1024,1024]{1,0:T(8,128)(2,1)} %cent_ref.5) | copy-start | bytes 6291460
  67.9 6.8 %collective-permute-start.18 = (f32[2,128]{1,0:T(2,128)S(1)}, f32[2,128]{1,0:T(2,128)S(1)}, u32[]{:S(2)}, u32[]{:S(2)}) collective-permute-start(f32[2,128]{1,0:T(2,128)S(1)} %slice.29), channel_id=1, source_target_pairs={{0,12},{1,13},{2,14},{3,15},{4,8},{5,9},{6,10},{7,11},{8,4},{9,5},... | collective-permute-start | bytes 3080 | tf_op jit(solution)/shard_map/ppermute | solution.py:469
  74.1 4.4 %collective-permute-start.16 = (f32[8,128]{1,0:T(8,128)S(1)}, f32[8,128]{1,0:T(8,128)S(1)}, u32[]{:S(2)}, u32[]{:S(2)}) collective-permute-start(f32[8,128]{1,0:T(8,128)S(1)} %get-tuple-element.78), channel_id=1, source_target_pairs={{0,2},{1,3},{2,0},{3,1},{4,6},{5,7},{6,4},{7,5},{8,10},{9,11},{10,... | collective-permute-start | bytes 12296 | tf_op jit(solution)/shard_map/ppermute | solution.py:469
  74.7 3.9 %collective-permute-start.19 = (f32[1,128]{1,0:T(1,128)S(1)}, f32[1,128]{1,0:T(1,128)S(1)}, u32[]{:S(2)}, u32[]{:S(2)}) collective-permute-start(f32[1,128]{1,0:T(1,128)S(1)} %slice.31), channel_id=1, source_target_pairs={{0,4},{1,5},{2,6},{3,7},{4,0},{5,1},{6,2},{7,3},{8,12},{9,13},{10,... | collective-permute-start | bytes 1544 | tf_op jit(solution)/shard_map/ppermute | solution.py:469
  78.5 1.2 %collective-permute-start.17 = (f32[8,128]{1,0:T(8,128)S(1)}, f32[8,128]{1,0:T(8,128)S(1)}, u32[]{:S(2)}, u32[]{:S(2)}) collective-permute-start(f32[8,128]{1,0:T(8,128)S(1)} %get-tuple-element.80), channel_id=1, source_target_pairs={{0,1},{1,0},{2,3},{3,2},{4,5},{5,4},{6,7},{7,6},{8,9},{9,8},{10,11... | collective-permute-start | bytes 12296 | tf_op jit(solution)/shard_map/ppermute | solution.py:469

commit v4 on v3

--- a/solution.py
+++ b/solution.py
@@ -568,7 +568,6 @@
     )(inside, scaled, facts, centroids, prior_row)
     across = exchange(across, 2)
     beside = jnp.concatenate([inside[4:8], across[4:8]], axis=0)
-    beside, counts = in_order(beside, counts)
     beside = exchange(beside, 1)
     density, level_two = call(
         functools.partial(last_kernel, cap, probe_count * BLOCK, BLOCK2), (shape((1, emb_rows), f32), shape((1, rows), f32))

time: 81.1 us -> 83.3 us (1.027)
  waiting for transfers between devices: 27.9 us -> 30.2 us
    ppermute x20, waiting for transfers between devices: 27.9 us -> 30.2 us  [exchange(): return lax.ppermute(value, 'shard', [(i, i ^ apart) for i in sources])]
    pallas_call x14 -> x13, Pallas kernels: 27.2 us -> 27.2 us  [run(): pl.pallas_call(kernel, out_shape=outs, in_specs=specs, scratch_shapes=lis...]
  transfers between devices with their start and end apart: 20 -> 20, of which waited for: 7 -> 8; matrix products, arithmetic and copies ran while one was open for 0% -> 0% of each run, Pallas kernels for 32% -> 32%
where the time goes in v4:
time: 83.3 us; the launch traced here: 83 us
  waiting for transfers between devices  30.2 us (36%)
  Pallas kernels  27.2 us (33%)
  starting transfers between devices  24.5 us (29%)
  between operations  0.92 us (1%)
    ppermute x20, waiting for transfers between devices, exchange(): return lax.ppermute(value, 'shard', [(i, i ^ apart) for i in sources])  30.2 us
    pallas_call x13, Pallas kernels, run(): pl.pallas_call(kernel, out_shape=outs, in_specs=specs, scratch_shapes=lis...  27.2 us
    ppermute x20, starting transfers between devices, exchange(): return lax.ppermute(value, 'shard', [(i, i ^ apart) for i in sources])  24.5 us
  transfers between devices with their start and end apart: 20, of which 8 were waited for; matrix products, arithmetic and copies ran while one was open for 0% of the time, Pallas kernels for 32%

profile of v4, /device:TPU:0, one launch (start us, length us, event | category | flops | bytes accessed | tf_op | source)
XLA Modules:
  0.0 83.0 jit_solution(996968557322468957)
XLA Ops:
  0.6 0.0 copy-start
  0.6 0.0 copy-start.3
  0.7 3.1 %collective-permute-start = (bf16[384,1024]{1,0:T(8,128)(2,1)}, bf16[384,1024]{1,0:T(8,128)(2,1)S(1)}, u32[]{:S(2)}, u32[]{:S(2)}) collective-permute-start(bf16[384,1024]{1,0:T(8,128)(2,1)} %own_any.1), channel_id=1, source_target_pairs={{0,4},{1,5},{2,6},{3,7},{4,0},{5,1},{6,2},{7,3},{8,12},{9,13},{10,... | collective-permute-start | bytes 2359304 | tf_op jit(solution)/shard_map/ppermute | solution.py:469
  3.7 0.7 collective-permute-start.1
  4.5 3.4 %shard_map.102 = (bf16[40,1152]{1,0:T(8,128)(2,1)S(1)}, bf16[304,1024]{1,0:T(8,128)(2,1)S(1)}, bf16[304,1024]{1,0:T(8,128)(2,1)S(1)}, s32[8,1024]{1,0:T(8,128)S(1)}) custom-call(s32[1,1024]{1,0:T(1,128)} %bitcast.10, bf16[40,1024]{1,0:T(8,128)(2,1)} %emb_any.1, s32[8,40]{1,0:T(8,128)} %bitcast.11, s32[1,40]{1,0:T(1,128)} %bitcast.12, s32[1,1024]{1,0:T(1,128)} %bitcast.7, ...), custom_call_target="tpu_custom_call" | custom-call | tf_op jit(solution)/shard_map/pallas_call | solution.py:435
  7.8 4.4 %collective-permute-start.2 = (bf16[40,1152]{1,0:T(8,128)(2,1)S(1)}, bf16[40,1152]{1,0:T(8,128)(2,1)S(1)}, u32[]{:S(2)}, u32[]{:S(2)}) collective-permute-start(bf16[40,1152]{1,0:T(8,128)(2,1)S(1)} %get-tuple-element.44), channel_id=1, source_target_pairs={{0,4},{1,5},{2,6},{3,7},{4,0},{5,1},{6,2},{7,3},{8,12},{9,13},{10,... | collective-permute-start | bytes 276488 | tf_op jit(solution)/shard_map/ppermute | solution.py:469
  12.3 1.5 %collective-permute-start.6 = (bf16[304,1024]{1,0:T(8,128)(2,1)S(1)}, bf16[304,1024]{1,0:T(8,128)(2,1)S(1)}, u32[]{:S(2)}, u32[]{:S(2)}) collective-permute-start(bf16[304,1024]{1,0:T(8,128)(2,1)S(1)} %get-tuple-element.49), channel_id=1, source_target_pairs={{0,2},{1,3},{2,0},{3,1},{4,6},{5,7},{6,4},{7,5},{8,10},{9,11},{10,... | collective-permute-start | bytes 1867784 | tf_op jit(solution)/shard_map/ppermute | solution.py:469
  13.8 0.0 collective-permute-start.7
  13.8 0.0 copy-done
  13.8 0.0 copy-done.3
  13.8 2.9 %shard_map.103 = (bf16[400,1024]{1,0:T(8,128)(2,1)S(1)}, bf16[400,1024]{1,0:T(8,128)(2,1)S(1)}, bf16[112,1024]{1,0:T(8,128)(2,1)S(1)}, bf16[112,1024]{1,0:T(8,128)(2,1)S(1)}) custom-call(s32[8,1024]{1,0:T(8,128)S(1)} %get-tuple-element.43.info, s32[1,1024]{1,0:T(1,128)S(1)} %bitcast.8, bf16[1024,1024]{1,0:T(8,128)(2,1)S(1)} %copy-done), custom_call_target="tpu_custom_call" | custom-call | tf_op jit(solution)/shard_map/pallas_call | solution.py:435
  16.7 6.8 %collective-permute-done.2 = bf16[40,1152]{1,0:T(8,128)(2,1)S(1)} collective-permute-done((bf16[40,1152]{1,0:T(8,128)(2,1)S(1)}, bf16[40,1152]{1,0:T(8,128)(2,1)S(1)}, u32[]{:S(2)}, u32[]{:S(2)}) %collective-permute-start.2) | collective-permute-done | bytes 92192 | tf_op jit(solution)/shard_map/ppermute | solution.py:469
  23.5 0.0 collective-permute-done.refs_0_
  23.5 0.0 collective-permute-done.1.refs_1_
  23.5 3.8 %collective-permute-start.5 = (bf16[80,1152]{1,0:T(8,128)(2,1)S(1)}, bf16[80,1152]{1,0:T(8,128)(2,1)S(1)}, u32[]{:S(2)}, u32[]{:S(2)}) collective-permute-start(bf16[80,1152]{1,0:T(8,128)(2,1)S(1)} %get-tuple-element.48), channel_id=1, source_target_pairs={{0,12},{1,13},{2,14},{3,15},{4,8},{5,9},{6,10},{7,11},{8,4},{9,5},... | collective-permute-start | bytes 552968 | tf_op jit(solution)/shard_map/ppermute | solution.py:469
  27.4 1.3 %collective-permute-start.3 = (bf16[384,1024]{1,0:T(8,128)(2,1)S(1)}, bf16[384,1024]{1,0:T(8,128)(2,1)S(1)}, u32[]{:S(2)}, u32[]{:S(2)}) collective-permute-start(bf16[384,1024]{1,0:T(8,128)(2,1)S(1)} %get-tuple-element.46.cross_any), channel_id=1, source_target_pairs={{4,0},{5,1},{6,2},{7,3},{8,12},{9,13},{10,14},{11,15},{20,16},{21,... | collective-permute-start | bytes 2359304 | tf_op jit(solution)/shard_map/ppermute | solution.py:469
  28.6 0.7 collective-permute-start.4
  29.4 2.0 %collective-permute-done.5 = bf16[80,1152]{1,0:T(8,128)(2,1)S(1)} collective-permute-done((bf16[80,1152]{1,0:T(8,128)(2,1)S(1)}, bf16[80,1152]{1,0:T(8,128)(2,1)S(1)}, u32[]{:S(2)}, u32[]{:S(2)}) %collective-permute-start.5) | collective-permute-done | bytes 184352 | tf_op jit(solution)/shard_map/ppermute | solution.py:469
  31.4 0.0 collective-permute-done.6.refs_1_
  31.4 8.1 %collective-permute-done.7.refs_2_ = bf16[304,1024]{1,0:T(8,128)(2,1)S(1)} collective-permute-done((bf16[304,1024]{1,0:T(8,128)(2,1)S(1)}, bf16[304,1024]{1,0:T(8,128)(2,1)S(1)}, u32[]{:S(2)}, u32[]{:S(2)}) %collective-permute-start.7) | collective-permute-done | bytes 622624 | tf_op jit(solution)/shard_map/ppermute | solution.py:469
  39.6 0.5 collective-permute-start.8
  40.1 3.2 %shard_map.106 = (bf16[1024,1024]{1,0:T(8,128)(2,1)S(1)}, bf16[2,384,1024]{2,1,0:T(8,128)(2,1)S(1)}) custom-call(bf16[1024,1024]{1,0:T(8,128)(2,1)} %cent_ref.5, bf16[384,1024]{1,0:T(8,128)(2,1)} %own_any.1, bf16[384,1024]{1,0:T(8,128)(2,1)S(1)} %get-tuple-element.47.near_any), custom_call_target="tpu_custom_call" | custom-call | tf_op jit(solution)/shard_map/pallas_call | solution.py:435
  43.3 1.9 %collective-permute-start.10 = (bf16[400,1024]{1,0:T(8,128)(2,1)S(1)}, bf16[400,1024]{1,0:T(8,128)(2,1)S(1)}, u32[]{:S(2)}, u32[]{:S(2)}) collective-permute-start(bf16[400,1024]{1,0:T(8,128)(2,1)S(1)} %get-tuple-element.64), channel_id=1, source_target_pairs={{0,1},{1,0},{2,3},{3,2},{4,5},{5,4},{6,7},{7,6},{8,9},{9,8},{10,11... | collective-permute-start | bytes 2457608 | tf_op jit(solution)/shard_map/ppermute | solution.py:469
  45.2 5.7 %collective-permute-done.8 = bf16[160,1152]{1,0:T(8,128)(2,1)S(1)} collective-permute-done((bf16[160,1152]{1,0:T(8,128)(2,1)S(1)}, bf16[160,1152]{1,0:T(8,128)(2,1)S(1)}, u32[]{:S(2)}, u32[]{:S(2)}) %collective-permute-start.8) | collective-permute-done | bytes 368672 | tf_op jit(solution)/shard_map/ppermute | solution.py:469
  50.9 0.1 pad_maximum_fusion.refs_2_
  51.0 0.0 collective-permute-done.3.refs_0_
  51.0 0.0 collective-permute-done.4.refs_1_
  51.0 0.0 copy-start.2
  51.0 0.2 collective-permute-start.9
  51.2 1.3 %collective-permute-start.15 = (bf16[384,1024]{1,0:T(8,128)(2,1)S(1)}, bf16[384,1024]{1,0:T(8,128)(2,1)S(1)}, u32[]{:S(2)}, u32[]{:S(2)}) collective-permute-start(bf16[384,1024]{1,0:T(8,128)(2,1)S(1)} %get-tuple-element.74.last_any), channel_id=1, source_target_pairs={{4,0},{5,1},{6,2},{7,3},{8,12},{9,13},{10,14},{11,15},{20,16},{21,... | collective-permute-start | bytes 2359304 | tf_op jit(solution)/shard_map/ppermute | solution.py:469
  52.5 0.4 collective-permute-start.11
  52.9 1.4 %collective-permute-start.12 = (bf16[112,1024]{1,0:T(8,128)(2,1)S(1)}, bf16[112,1024]{1,0:T(8,128)(2,1)S(1)}, u32[]{:S(2)}, u32[]{:S(2)}) collective-permute-start(bf16[112,1024]{1,0:T(8,128)(2,1)S(1)} %get-tuple-element.68), channel_id=1, source_target_pairs={{0,3},{1,2},{2,1},{3,0},{4,7},{5,6},{6,5},{7,4},{8,11},{9,10},{10,... | collective-permute-start | bytes 688136 | tf_op jit(solution)/shard_map/ppermute | solution.py:469
  54.3 0.0 collective-permute-done.9.other_any
  54.3 3.1 %shard_map.108 = (bf16[640,1024]{1,0:T(8,128)(2,1)S(1)}, s32[16,640]{1,0:T(8,128)S(1)}, f32[8,128]{1,0:T(8,128)S(1)}, f32[8,128]{1,0:T(8,128)S(1)}) custom-call(bf16[320,1152]{1,0:T(8,128)(2,1)S(1)} %get-tuple-element.57.mine_any, bf16[320,1152]{1,0:T(8,128)(2,1)S(1)} %collective-permute-done.9.other_any, bf16[1024,1024]{1,0:T(8,128)(2,1)S(1)} %get-tuple-element.58.unit_old), custom_call_target="tpu_custom_call" | custom-call | tf_op jit(solution)/shard_map/pallas_call | solution.py:435
  57.4 0.0 copy-done.2
  57.4 0.5 collective-permute-start.13
  57.9 0.8 collective-permute-done.13
  58.8 0.3 collective-permute-start.14
  59.1 0.0 collective-permute-done.10.any1
  59.1 5.9 %shard_map.109.after.early = f32[24,128]{1,0:T(8,128)S(1)} custom-call(bf16[640,1024]{1,0:T(8,128)(2,1)S(1)} %get-tuple-element.59.scaled, s32[16,640]{1,0:T(8,128)S(1)} %get-tuple-element.60.facts_in.facts, bf16[2,384,1024]{2,1,0:T(8,128)(2,1)} %copy-done.2, bf16[384,1024]{1,0:T(8,128)(2,1)S(1)} %get-tuple-element.46.cross_any, ...), custom_call_target="tpu_custom_call" | custom-call | tf_op jit(solution)/shard_map/pallas_call | solution.py:435
  65.0 0.0 collective-permute-done.11.any2
  65.0 0.0 collective-permute-done.12.any3
  65.0 2.8 %shard_map.110 = (bf16[1,3,128,1024]{3,2,1,0:T(8,128)(2,1)S(1)}, bf16[1,3,128,128]{3,2,1,0:T(8,128)(2,1)S(1)}) custom-call(bf16[640,1024]{1,0:T(8,128)(2,1)S(1)} %get-tuple-element.59.scaled, s32[16,640]{1,0:T(8,128)S(1)} %get-tuple-element.60.facts_in.facts, bf16[400,1024]{1,0:T(8,128)(2,1)S(1)} %get-tuple-element.63.any0, ...), custom_call_target="tpu_custom_call" | custom-call | tf_op jit(solution)/shard_map/pallas_call | solution.py:435
  67.9 0.0 collective-permute-done.14
  67.9 0.0 copy-start.1
  67.9 1.8 %collective-permute-start.18 = (f32[2,128]{1,0:T(2,128)S(1)}, f32[2,128]{1,0:T(2,128)S(1)}, u32[]{:S(2)}, u32[]{:S(2)}) collective-permute-start(f32[2,128]{1,0:T(2,128)S(1)} %slice.29), channel_id=1, source_target_pairs={{0,12},{1,13},{2,14},{3,15},{4,8},{5,9},{6,10},{7,11},{8,4},{9,5},... | collective-permute-start | bytes 3080 | tf_op jit(solution)/shard_map/ppermute | solution.py:469
  69.7 3.3 %collective-permute-done.15.far_any = bf16[384,1024]{1,0:T(8,128)(2,1)S(1)} collective-permute-done((bf16[384,1024]{1,0:T(8,128)(2,1)S(1)}, bf16[384,1024]{1,0:T(8,128)(2,1)S(1)}, u32[]{:S(2)}, u32[]{:S(2)}) %collective-permute-start.15) | collective-permute-done | bytes 786464 | tf_op jit(solution)/shard_map/ppermute | solution.py:469
  72.9 1.1 %shard_map.112 = (f32[8,128]{1,0:T(8,128)S(1)}, f32[8,128]{1,0:T(8,128)S(1)}) custom-call(f32[24,128]{1,0:T(8,128)S(1)} %shard_map.109.after.early, bf16[1,3,128,128]{3,2,1,0:T(8,128)(2,1)S(1)} %get-tuple-element.69.floors, bf16[1,3,128,1024]{3,2,1,0:T(8,128)(2,1)S(1)} %get-tuple-element.73.kept_any, bf16[384,1024]{1,0:T(8,128)(2,1)S(1)} %get-tuple-element.74.last_any, ...), custom_call_target="tpu_custom_call" | custom-call | tf_op jit(solution)/shard_map/pallas_call | solution.py:435
  74.1 0.6 collective-permute-start.16
  74.7 0.0 collective-permute-done.18
  74.7 0.1 collective-permute-start.19
  74.8 3.0 %collective-permute-done.16.across = f32[8,128]{1,0:T(8,128)S(1)} collective-permute-done((f32[8,128]{1,0:T(8,128)S(1)}, f32[8,128]{1,0:T(8,128)S(1)}, u32[]{:S(2)}, u32[]{:S(2)}) %collective-permute-start.16) | collective-permute-done | bytes 4128 | tf_op jit(solution)/shard_map/ppermute | solution.py:469
  77.8 0.1 collective-permute-start.17
  77.8 0.5 collective-permute-done.19
  78.3 0.0 copy-done.1
  78.3 3.7 %shard_map.114 = (bf16[1024,1024]{1,0:T(8,128)(2,1)}, s32[1,1024]{1,0:T(1,128)}) custom-call(f32[8,128]{1,0:T(8,128)S(1)} %get-tuple-element.75.inside.after, bf16[640,1024]{1,0:T(8,128)(2,1)S(1)} %get-tuple-element.59.scaled, s32[16,640]{1,0:T(8,128)S(1)} %get-tuple-element.60.facts_in.facts, bf16[1024,1024]{1,0:T(8,128)(2,1)S(1)} %copy-done.1, ...), custom_call_target="tpu_custom_call" | custom-call | tf_op jit(solution)/shard_map/pallas_call | solution.py:435
  82.0 0.0 collective-permute-done.17.beside
  82.0 1.0 %shard_map.113 = (f32[1,40]{1,0:T(1,128)}, f32[1,1024]{1,0:T(1,128)}) custom-call(s32[8,1024]{1,0:T(8,128)S(1)} %get-tuple-element.43.info, f32[8,128]{1,0:T(8,128)S(1)} %get-tuple-element.75.inside.after, f32[8,128]{1,0:T(8,128)S(1)} %collective-permute-done.16.across, f32[8,128]{1,0:T(8,128)S(1)} %collective-permute-done.17.beside, ...), custom_call_target="tpu_custom_call" | custom-call | tf_op jit(solution)/shard_map/pallas_call | solution.py:435
  (16 shorter events, 0.1 us)
Async XLA Ops:
  0.6 13.1 %copy-start = (bf16[1024,1024]{1,0:T(8,128)(2,1)S(1)}, bf16[1024,1024]{1,0:T(8,128)(2,1)}, u32[]{:S(2)}) copy-start(bf16[1024,1024]{1,0:T(8,128)(2,1)} %cent_ref.5) | copy-start | bytes 6291460
  0.6 13.1 %copy-start.3 = (s32[1024]{0:T(1024)S(1)}, s32[1024]{0:T(1024)}, u32[]{:S(2)}) copy-start(s32[1024]{0:T(1024)} %param.10) | copy-start | bytes 12292
  0.7 22.8 %collective-permute-start = (bf16[384,1024]{1,0:T(8,128)(2,1)}, bf16[384,1024]{1,0:T(8,128)(2,1)S(1)}, u32[]{:S(2)}, u32[]{:S(2)}) collective-permute-start(bf16[384,1024]{1,0:T(8,128)(2,1)} %own_any.1), channel_id=1, source_target_pairs={{0,4},{1,5},{2,6},{3,7},{4,0},{5,1},{6,2},{7,3},{8,12},{9,13},{10,... | collective-permute-start | bytes 2359304 | tf_op jit(solution)/shard_map/ppermute | solution.py:469
  3.7 19.8 %collective-permute-start.1 = (bf16[384,1024]{1,0:T(8,128)(2,1)}, bf16[384,1024]{1,0:T(8,128)(2,1)S(1)}, u32[]{:S(2)}, u32[]{:S(2)}) collective-permute-start(bf16[384,1024]{1,0:T(8,128)(2,1)} %own_any.1), channel_id=1, source_target_pairs={{4,8},{5,9},{6,10},{7,11},{8,4},{9,5},{10,6},{11,7},{20,24},{21,25... | collective-permute-start | bytes 2359304 | tf_op jit(solution)/shard_map/ppermute | solution.py:469
  7.8 15.6 %collective-permute-start.2 = (bf16[40,1152]{1,0:T(8,128)(2,1)S(1)}, bf16[40,1152]{1,0:T(8,128)(2,1)S(1)}, u32[]{:S(2)}, u32[]{:S(2)}) collective-permute-start(bf16[40,1152]{1,0:T(8,128)(2,1)S(1)} %get-tuple-element.44), channel_id=1, source_target_pairs={{0,4},{1,5},{2,6},{3,7},{4,0},{5,1},{6,2},{7,3},{8,12},{9,13},{10,... | collective-permute-start | bytes 276488 | tf_op jit(solution)/shard_map/ppermute | solution.py:469
  12.3 19.2 %collective-permute-start.6 = (bf16[304,1024]{1,0:T(8,128)(2,1)S(1)}, bf16[304,1024]{1,0:T(8,128)(2,1)S(1)}, u32[]{:S(2)}, u32[]{:S(2)}) collective-permute-start(bf16[304,1024]{1,0:T(8,128)(2,1)S(1)} %get-tuple-element.49), channel_id=1, source_target_pairs={{0,2},{1,3},{2,0},{3,1},{4,6},{5,7},{6,4},{7,5},{8,10},{9,11},{10,... | collective-permute-start | bytes 1867784 | tf_op jit(solution)/shard_map/ppermute | solution.py:469
  13.8 25.8 %collective-permute-start.7 = (bf16[304,1024]{1,0:T(8,128)(2,1)S(1)}, bf16[304,1024]{1,0:T(8,128)(2,1)S(1)}, u32[]{:S(2)}, u32[]{:S(2)}) collective-permute-start(bf16[304,1024]{1,0:T(8,128)(2,1)S(1)} %get-tuple-element.50), channel_id=1, source_target_pairs={{0,3},{1,2},{2,1},{3,0},{4,7},{5,6},{6,5},{7,4},{8,11},{9,10},{10,... | collective-permute-start | bytes 1867784 | tf_op jit(solution)/shard_map/ppermute | solution.py:469
  23.5 7.9 %collective-permute-start.5 = (bf16[80,1152]{1,0:T(8,128)(2,1)S(1)}, bf16[80,1152]{1,0:T(8,128)(2,1)S(1)}, u32[]{:S(2)}, u32[]{:S(2)}) collective-permute-start(bf16[80,1152]{1,0:T(8,128)(2,1)S(1)} %get-tuple-element.48), channel_id=1, source_target_pairs={{0,12},{1,13},{2,14},{3,15},{4,8},{5,9},{6,10},{7,11},{8,4},{9,5},... | collective-permute-start | bytes 552968 | tf_op jit(solution)/shard_map/ppermute | solution.py:469
  27.4 23.6 %collective-permute-start.3 = (bf16[384,1024]{1,0:T(8,128)(2,1)S(1)}, bf16[384,1024]{1,0:T(8,128)(2,1)S(1)}, u32[]{:S(2)}, u32[]{:S(2)}) collective-permute-start(bf16[384,1024]{1,0:T(8,128)(2,1)S(1)} %get-tuple-element.46.cross_any), channel_id=1, source_target_pairs={{4,0},{5,1},{6,2},{7,3},{8,12},{9,13},{10,14},{11,15},{20,16},{21,... | collective-permute-start | bytes 2359304 | tf_op jit(solution)/shard_map/ppermute | solution.py:469
  28.6 22.4 %collective-permute-start.4 = (bf16[384,1024]{1,0:T(8,128)(2,1)S(1)}, bf16[384,1024]{1,0:T(8,128)(2,1)S(1)}, u32[]{:S(2)}, u32[]{:S(2)}) collective-permute-start(bf16[384,1024]{1,0:T(8,128)(2,1)S(1)} %get-tuple-element.47.near_any), channel_id=1, source_target_pairs={{4,8},{5,9},{6,10},{7,11},{8,4},{9,5},{10,6},{11,7},{20,24},{21,25... | collective-permute-start | bytes 2359304 | tf_op jit(solution)/shard_map/ppermute | solution.py:469
  39.6 11.4 %collective-permute-start.8 = (bf16[160,1152]{1,0:T(8,128)(2,1)S(1)}, bf16[160,1152]{1,0:T(8,128)(2,1)S(1)}, u32[]{:S(2)}, u32[]{:S(2)}) collective-permute-start(bf16[160,1152]{1,0:T(8,128)(2,1)S(1)} %get-tuple-element.54), channel_id=1, source_target_pairs={{0,2},{1,3},{2,0},{3,1},{4,6},{5,7},{6,4},{7,5},{8,10},{9,11},{10,... | collective-permute-start | bytes 1105928 | tf_op jit(solution)/shard_map/ppermute | solution.py:469
  43.3 15.7 %collective-permute-start.10 = (bf16[400,1024]{1,0:T(8,128)(2,1)S(1)}, bf16[400,1024]{1,0:T(8,128)(2,1)S(1)}, u32[]{:S(2)}, u32[]{:S(2)}) collective-permute-start(bf16[400,1024]{1,0:T(8,128)(2,1)S(1)} %get-tuple-element.64), channel_id=1, source_target_pairs={{0,1},{1,0},{2,3},{3,2},{4,5},{5,4},{6,7},{7,6},{8,9},{9,8},{10,11... | collective-permute-start | bytes 2457608 | tf_op jit(solution)/shard_map/ppermute | solution.py:469
  51.0 6.4 %copy-start.2 = (bf16[2,384,1024]{2,1,0:T(8,128)(2,1)}, bf16[2,384,1024]{2,1,0:T(8,128)(2,1)S(1)}, u32[]{:S(2)}) copy-start(bf16[2,384,1024]{2,1,0:T(8,128)(2,1)S(1)} %get-tuple-element.61.units_any) | copy-start | bytes 4718596
  51.0 3.3 %collective-permute-start.9 = (bf16[320,1152]{1,0:T(8,128)(2,1)S(1)}, bf16[320,1152]{1,0:T(8,128)(2,1)S(1)}, u32[]{:S(2)}, u32[]{:S(2)}) collective-permute-start(bf16[320,1152]{1,0:T(8,128)(2,1)S(1)} %get-tuple-element.57.mine_any), channel_id=1, source_target_pairs={{0,1},{1,0},{2,3},{3,2},{4,5},{5,4},{6,7},{7,6},{8,9},{9,8},{10,11... | collective-permute-start | bytes 2211848 | tf_op jit(solution)/shard_map/ppermute | solution.py:469
  51.2 21.7 %collective-permute-start.15 = (bf16[384,1024]{1,0:T(8,128)(2,1)S(1)}, bf16[384,1024]{1,0:T(8,128)(2,1)S(1)}, u32[]{:S(2)}, u32[]{:S(2)}) collective-permute-start(bf16[384,1024]{1,0:T(8,128)(2,1)S(1)} %get-tuple-element.74.last_any), channel_id=1, source_target_pairs={{4,0},{5,1},{6,2},{7,3},{8,12},{9,13},{10,14},{11,15},{20,16},{21,... | collective-permute-start | bytes 2359304 | tf_op jit(solution)/shard_map/ppermute | solution.py:469
  52.5 12.5 %collective-permute-start.11 = (bf16[112,1024]{1,0:T(8,128)(2,1)S(1)}, bf16[112,1024]{1,0:T(8,128)(2,1)S(1)}, u32[]{:S(2)}, u32[]{:S(2)}) collective-permute-start(bf16[112,1024]{1,0:T(8,128)(2,1)S(1)} %get-tuple-element.67), channel_id=1, source_target_pairs={{0,2},{1,3},{2,0},{3,1},{4,6},{5,7},{6,4},{7,5},{8,10},{9,11},{10,... | collective-permute-start | bytes 688136 | tf_op jit(solution)/shard_map/ppermute | solution.py:469
  52.9 12.1 %collective-permute-start.12 = (bf16[112,1024]{1,0:T(8,128)(2,1)S(1)}, bf16[112,1024]{1,0:T(8,128)(2,1)S(1)}, u32[]{:S(2)}, u32[]{:S(2)}) collective-permute-start(bf16[112,1024]{1,0:T(8,128)(2,1)S(1)} %get-tuple-element.68), channel_id=1, source_target_pairs={{0,3},{1,2},{2,1},{3,0},{4,7},{5,6},{6,5},{7,4},{8,11},{9,10},{10,... | collective-permute-start | bytes 688136 | tf_op jit(solution)/shard_map/ppermute | solution.py:469
  57.4 1.3 %collective-permute-start.13 = (f32[8,128]{1,0:T(8,128)S(1)}, f32[8,128]{1,0:T(8,128)S(1)}, u32[]{:S(2)}, u32[]{:S(2)}) collective-permute-start(f32[8,128]{1,0:T(8,128)S(1)} %get-tuple-element.71), channel_id=1, source_target_pairs={{0,1},{1,0},{2,3},{3,2},{4,5},{5,4},{6,7},{7,6},{8,9},{9,8},{10,11... | collective-permute-start | bytes 12296 | tf_op jit(solution)/shard_map/ppermute | solution.py:469
  58.8 9.1 %collective-permute-start.14 = (f32[4,128]{1,0:T(4,128)S(1)}, f32[4,128]{1,0:T(4,128)S(1)}, u32[]{:S(2)}, u32[]{:S(2)}) collective-permute-start(f32[4,128]{1,0:T(4,128)S(1)} %slice.25), channel_id=1, source_target_pairs={{0,2},{1,3},{2,0},{3,1},{4,6},{5,7},{6,4},{7,5},{8,10},{9,11},{10,... | collective-permute-start | bytes 6152 | tf_op jit(solution)/shard_map/ppermute | solution.py:469
  67.9 10.4 %copy-start.1 = (bf16[1024,1024]{1,0:T(8,128)(2,1)S(1)}, bf16[1024,1024]{1,0:T(8,128)(2,1)}, u32[]{:S(2)}) copy-start(bf16[1024,1024]{1,0:T(8,128)(2,1)} %cent_ref.5) | copy-start | bytes 6291460
  67.9 6.8 %collective-permute-start.18 = (f32[2,128]{1,0:T(2,128)S(1)}, f32[2,128]{1,0:T(2,128)S(1)}, u32[]{:S(2)}, u32[]{:S(2)}) collective-permute-start(f32[2,128]{1,0:T(2,128)S(1)} %slice.29), channel_id=1, source_target_pairs={{0,12},{1,13},{2,14},{3,15},{4,8},{5,9},{6,10},{7,11},{8,4},{9,5},... | collective-permute-start | bytes 3080 | tf_op jit(solution)/shard_map/ppermute | solution.py:469
  74.1 3.7 %collective-permute-start.16 = (f32[8,128]{1,0:T(8,128)S(1)}, f32[8,128]{1,0:T(8,128)S(1)}, u32[]{:S(2)}, u32[]{:S(2)}) collective-permute-start(f32[8,128]{1,0:T(8,128)S(1)} %get-tuple-element.76), channel_id=1, source_target_pairs={{0,2},{1,3},{2,0},{3,1},{4,6},{5,7},{6,4},{7,5},{8,10},{9,11},{10,... | collective-permute-start | bytes 12296 | tf_op jit(solution)/shard_map/ppermute | solution.py:469
  74.7 3.6 %collective-permute-start.19 = (f32[1,128]{1,0:T(1,128)S(1)}, f32[1,128]{1,0:T(1,128)S(1)}, u32[]{:S(2)}, u32[]{:S(2)}) collective-permute-start(f32[1,128]{1,0:T(1,128)S(1)} %slice.31), channel_id=1, source_target_pairs={{0,4},{1,5},{2,6},{3,7},{4,0},{5,1},{6,2},{7,3},{8,12},{9,13},{10,... | collective-permute-start | bytes 1544 | tf_op jit(solution)/shard_map/ppermute | solution.py:469
  77.8 4.2 %collective-permute-start.17 = (f32[8,128]{1,0:T(8,128)S(1)}, f32[8,128]{1,0:T(8,128)S(1)}, u32[]{:S(2)}, u32[]{:S(2)}) collective-permute-start(f32[8,128]{1,0:T(8,128)S(1)} %pad_maximum_fusion.3), channel_id=1, source_target_pairs={{0,1},{1,0},{2,3},{3,2},{4,5},{5,4},{6,7},{7,6},{8,9},{9,8},{10,11... | collective-permute-start | bytes 12296 | tf_op jit(solution)/shard_map/ppermute | solution.py:469
